TPU v7x, 32 devices: a whole 2x2x4 slice. The times are simulated.
32 devices in a mesh: lat: 4 (over x, core), lon: 8 (over z, y).
Axes of the slice: x: 2, y: 2, z: 4, core: 2. Of those that a mesh axis runs over, the one named last changes fastest.
Arguments:
- latent_field: float32 [32, 8, 64, 1024], P(None, None, 'lat', 'lon'), may hold values from -6 to 6
- east_courant: float32 [8, 64, 1024], P(None, 'lat', 'lon'), may hold values from -0.45 to 0.45
- north_courant: float32 [8, 64, 1024], P(None, 'lat', 'lon'), may hold values from -0.45 to 0.45
- mixing: float32 [7, 64, 1024], P(None, 'lat', 'lon'), may hold values from 0.2 to 5
- sunlit: int32 [4, 64], P('lat', 'lon'), may hold values from 0 to 1, as said below
- decode_w: bfloat16 [224, 32], replicated, may hold values from -1 to 1
- react_a: bfloat16 [256, 224], replicated, may hold values from -0.375 to 0.375
- react_b: bfloat16 [256, 224], replicated, may hold values from -0.375 to 0.375
- stoich: bfloat16 [224, 256], replicated, may hold values from -0.375 to 0.375
- encode_w: bfloat16 [32, 224], replicated, may hold values from -0.375 to 0.375
- rate_const: float32 [256], replicated, may hold values from 0.05 to 0.5
Outputs:
- advanced: float32 [32, 8, 64, 1024], P(None, None, 'lat', 'lon')
Inputs may be any that keep to these rules, and one draw needn't show every extreme that they name: In each row of blocks the sunlit blocks form one run, periodic in longitude, of 16 to 48 blocks.
All inputs are finite; a program needn't handle non-finite values.
Results may differ from a plain program's by a relative error of at most 0.0035.
Values may be sent and summed in bfloat16 or wider, within the bound.
No kernel may reach another device: no remote copies, remote signals or barrier semaphores. Data moves between devices by JAX's collectives and lax.ppermute only.
A program may use at most 128 MiB of HBM per device.

v0:
```python
import functools
import itertools

import jax
import jax.numpy as jnp
from jax import lax
from jax.experimental import pallas as pl
from jax.experimental.pallas import tpu as pltpu
from jax.sharding import PartitionSpec as P

BLOCK = 16
SUBSTEPS = 2
STEPS = 2
GROUP = 16
ROWS_AT_ONCE = 8
ROWS_IN_FLIGHT = 2
LEVELS_AT_ONCE = 4
LAG = 1

F32 = jnp.float32
BF16 = jnp.bfloat16
VMEM_BYTES = 48 * 1024 * 1024
FIRST_VMEM_BYTES = 56 * 1024 * 1024


def lane_ids(shape):
    return lax.broadcasted_iota(jnp.int32, shape, len(shape) - 1)


def fold_weights(decode_t, react_a_t, react_b_t, stoich, encode, rate, linear_out, encode_out):
    n_reactions = react_a_t.shape[1]
    contract = (((0,), (1,)), ((), ()))
    for part, react in enumerate((react_a_t, react_b_t)):
        product = lax.dot_general(
            react[...], decode_t[...], contract, preferred_element_type=F32
        )
        for group in range(n_reactions // GROUP):
            at = (2 * group + part) * GROUP
            linear_out[at : at + GROUP, :] = product[
                group * GROUP : (group + 1) * GROUP
            ].astype(BF16)
    folded = jnp.dot(encode[...], stoich[...], preferred_element_type=F32)
    encode_out[...] = (folded * rate[...]).astype(BF16)


def at_ends():
    index = lax.axis_index("lat")
    return index == 0, index == lax.axis_size("lat") - 1


def is_even(axis):
    return lax.axis_index(axis) % 2 == 0


def by_parity(axis, up, down, into_first, into_second):
    even = is_even(axis)
    into_first[...] = jnp.where(even, up, down)
    into_second[...] = jnp.where(even, down, up)


def pack_sides(value, coef, at, west, east):
    lanes = lane_ids(value.shape)
    size = value.shape[-1]
    turned = pltpu.roll(value * coef, at, 1)
    west = jnp.where(lanes == at, turned, west)
    east = jnp.where(lanes == (at + size - 1) % size, turned, east)
    return west, east


def first_kernel(latent, east_c, north_c, lon_a, lon_b, lat_a, lat_b, *scratch):
    tiles, east_v, north_v, sems = scratch
    n_levels, n_species, n_rows, n_cols = tiles.shape
    lanes = lane_ids((1, n_cols))
    is_first, is_last = at_ends()
    copies = [
        pltpu.make_async_copy(east_c, east_v, sems.at[n_levels]),
        pltpu.make_async_copy(north_c, north_v, sems.at[n_levels + 1]),
    ]
    levels = [
        pltpu.make_async_copy(latent.at[:, level], tiles.at[level], sems.at[level])
        for level in range(n_levels)
    ]
    for copy in copies + levels:
        copy.start()
    for copy in copies:
        copy.wait()
    sides = (jnp.zeros((n_species, n_cols), F32),) * 2
    for level in range(n_levels):
        levels[level].wait()
        tile = jnp.transpose(tiles[level], (1, 0, 2))
        for r in range(n_rows):
            at = level * n_rows + r
            value = tile[r]
            speed = east_v[level, r : r + 1, :]
            coef = jnp.where(lanes == 0, jnp.minimum(speed, 0.0), jnp.maximum(speed, 0.0))
            sides = pack_sides(value, coef, at, *sides)
        ends = []
        for r, closed, clip in ((0, is_first, jnp.minimum), (n_rows - 1, is_last, jnp.maximum)):
            speed = clip(north_v[level, r : r + 1, :], 0.0)
            ends.append((tile[r] * jnp.where(closed, 0.0, speed)).astype(BF16))
        by_parity("lat", ends[1], ends[0], lat_a.at[level], lat_b.at[level])
    by_parity("lon", sides[1], sides[0], lon_a, lon_b)


def step_kernel(
    n_levels,
    n_rows,
    first,
    last,
    sun,
    field,
    east_c,
    north_c,
    mixing,
    lon_a_in,
    lon_b_in,
    lat_a_in,
    lat_b_in,
    *refs,
):
    if first:
        weights, refs = refs[:6], refs[6:]
        linear, encode = refs[5:7]
    else:
        (linear, encode), refs = refs[:2], refs[2:]
    half_rows = n_rows // 2
    south_in, north_in, west_in, east_in, coefs, diffused = refs[-6:]
    if last:
        staged, sems = refs[-8:-6]
    by_parity("lon", lon_a_in[...], lon_b_in[...], east_in, west_in)
    by_parity("lat", lat_a_in[...], lat_b_in[...], north_in, south_in)
    n_species, n_cols = west_in.shape
    n_reactions = encode.shape[1]
    cells = n_levels * n_rows
    lanes = lane_ids((1, n_cols))
    row_ids = lax.broadcasted_iota(jnp.int32, (n_rows, n_cols), 0)
    is_first, is_last = at_ends()
    if first:
        latent, field = field, refs[-7]
        fold_weights(*weights, linear, encode)
        for level in range(n_levels):
            field[level] = jnp.transpose(latent[:, level], (1, 0, 2))
    CENTRE, EAST, WEST, NORTH, SOUTH, SCALE, LOWER, UPPER = range(8)

    upper = None
    for level in range(n_levels):
        ce, cn = east_c[level], north_c[level]
        east, west = jnp.maximum(ce, 0.0), jnp.minimum(ce, 0.0)
        north = jnp.where((row_ids == n_rows - 1) & is_last, 0.0, jnp.maximum(cn, 0.0))
        south = jnp.where((row_ids == 0) & is_first, 0.0, jnp.minimum(cn, 0.0))
        coefs[CENTRE, level] = 1.0 - east + west - north + south
        coefs[EAST, level] = east
        coefs[WEST, level] = west
        coefs[NORTH, level] = north
        coefs[SOUTH, level] = south
        pivot = 1.0
        if level > 0:
            below = mixing[level - 1]
            pivot = pivot + below - below * upper
        if level < n_levels - 1:
            pivot = pivot + mixing[level]
        scale = 1.0 / pivot
        coefs[SCALE, level] = scale
        if level > 0:
            coefs[LOWER, level] = below * scale
        if level < n_levels - 1:
            upper = mixing[level] * scale
            coefs[UPPER, level] = upper

    lit = jnp.zeros((1, n_cols), jnp.int32)
    for block in range(n_cols // BLOCK):
        lit = jnp.where(lanes // BLOCK == block, sun[0, block], lit)
    lit = lit > 0

    def coef(kind, level, r):
        return coefs[kind, level, pl.ds(r, 1), :]

    def transport(slot):
        r = jnp.minimum(slot, n_rows - 1)
        before, after = jnp.maximum(r - 1, 0), jnp.minimum(r + 1, n_rows - 1)
        right = None
        for level in range(n_levels):
            at = level * n_rows + r
            value = field[level, r]
            from_west = jnp.where(
                lanes == 0,
                pltpu.roll(west_in[...], (n_cols + 1 - at) % n_cols, 1),
                pltpu.roll(value * coef(EAST, level, r), 1, 1),
            )
            from_east = jnp.where(
                lanes == n_cols - 1,
                pltpu.roll(east_in[...], n_cols - 1 - at, 1),
                pltpu.roll(value * coef(WEST, level, r), n_cols - 1, 1),
            )
            from_south = jnp.where(
                r == 0,
                south_in[level].astype(F32),
                field[level, before] * coef(NORTH, level, before),
            )
            from_north = jnp.where(
                r == n_rows - 1,
                north_in[level].astype(F32),
                field[level, after] * coef(SOUTH, level, after),
            )
            moved = value * coef(CENTRE, level, r) + (from_west - from_east) + (from_south - from_north)
            scaled = moved * coef(SCALE, level, r)
            right = scaled if level == 0 else scaled + coef(LOWER, level, r) * right
            diffused[level, slot] = right
            yield
        for level in range(n_levels - 2, -1, -1):
            right = diffused[level, slot] + coef(UPPER, level, r) * right
            diffused[level, slot] = right
            yield

    def product_of(rounded):
        both = jnp.dot(linear[...], rounded, preferred_element_type=F32)
        parts = [
            both[at : at + GROUP] * both[at + GROUP : at + 2 * GROUP]
            for at in range(0, 2 * n_reactions, 2 * GROUP)
        ]
        return jnp.concatenate(parts, axis=0).astype(BF16)

    for r in range(ROWS_IN_FLIGHT):
        for _ in transport(r):
            pass
    lit_tile = jnp.concatenate([lit] * LEVELS_AT_ONCE, axis=1)

    def tile_at(level, r):
        return jnp.concatenate(
            [diffused[level + extra, r] for extra in range(LEVELS_AT_ONCE)], axis=1
        )

    def rows(turn, sides):
        units, ahead = [], {}
        for first_row in range(0, ROWS_AT_ONCE, ROWS_IN_FLIGHT):
            in_flight = [turn * ROWS_AT_ONCE + first_row + extra for extra in range(ROWS_IN_FLIGHT)]
            places = [
                (level, r) for r in in_flight for level in range(0, n_levels, LEVELS_AT_ONCE)
            ]
            steps = itertools.chain(*[transport(r + ROWS_IN_FLIGHT) for r in in_flight])
            share = -(-(2 * n_levels - 1) * ROWS_IN_FLIGHT // (SUBSTEPS * len(places)))
            for substep in range(SUBSTEPS):
                for place in places:
                    ahead[len(units)] = (steps, share)
                    units.append((substep, place))
        rounded, rates = {}, {}
        for at in range(len(units) + LAG):
            if at < len(units):
                substep, (level, r) = units[at]
                if substep == 0:
                    rounded[at] = tile_at(level, r).astype(BF16)
                rates[at] = product_of(rounded.pop(at))
                steps, share = ahead[at]
                for _ in itertools.islice(steps, share):
                    pass
            if at >= LAG:
                done = at - LAG
                substep, (level, r) = units[done]
                change = jnp.dot(encode[...], rates.pop(done), preferred_element_type=F32)
                tile = tile_at(level, r)
                value = tile + jnp.where(lit_tile, change, 0.0)
                if substep < SUBSTEPS - 1:
                    later = done + ROWS_IN_FLIGHT * (n_levels // LEVELS_AT_ONCE)
                    rounded[later] = (tile.astype(BF16).astype(F32) + change).astype(BF16)
                for extra in range(LEVELS_AT_ONCE):
                    part = value[:, extra * n_cols : (extra + 1) * n_cols]
                    at_level = level + extra
                    if last or substep < SUBSTEPS - 1:
                        diffused[at_level, r] = part
                    else:
                        refs[0][at_level, r] = part
                        speed = east_c[at_level, pl.ds(r, 1), :]
                        side = jnp.where(
                            lanes == 0, jnp.minimum(speed, 0.0), jnp.maximum(speed, 0.0)
                        )
                        sides = pack_sides(part, side, at_level * n_rows + r, *sides)
        return sides

    if last:

        def sends(half):
            within = pl.ds(pl.multiple_of(half * half_rows, half_rows), half_rows)
            return [
                pltpu.make_async_copy(
                    staged.at[half, level], refs[0].at[:, level, within], sems.at[half, level]
                )
                for level in range(n_levels)
            ]

        def half_done(half, carry):
            for turn in range(half_rows // ROWS_AT_ONCE):
                rows(half * (half_rows // ROWS_AT_ONCE) + turn, None)
            for level, copy in enumerate(sends(half)):
                within = pl.ds(half * half_rows, half_rows)
                staged[half, level] = jnp.transpose(diffused[level, within], (1, 0, 2))
                copy.start()
            return carry

        lax.fori_loop(0, 2, half_done, 0)
        for half in range(2):
            for copy in sends(half):
                copy.wait()
        return
    out, lon_a, lon_b, lat_a, lat_b = refs[:5]
    zeros = jnp.zeros((n_species, n_cols), F32)
    west, east = lax.fori_loop(0, n_rows // ROWS_AT_ONCE, rows, (zeros, zeros))
    by_parity("lon", east, west, lon_a, lon_b)
    for level in range(n_levels):
        south = (out[level, 0] * coefs[SOUTH, level, :1]).astype(BF16)
        north = (out[level, n_rows - 1] * coefs[NORTH, level, n_rows - 1 :]).astype(BF16)
        by_parity("lat", north, south, lat_a.at[level], lat_b.at[level])


def vmem(count):
    return [pl.BlockSpec(memory_space=pltpu.VMEM)] * count


def exchanged(lon_a, lon_b, lat_a, lat_b):
    def swapped(array, axis, first):
        size = lax.axis_size(axis)
        pairs = [(i % size, (i + 1) % size) for i in range(first, size + first, 2)]
        return lax.ppermute(array, axis, pairs + [(j, i) for i, j in pairs])

    lon_b, lon_a = swapped(lon_b, "lon", 1), swapped(lon_a, "lon", 0)
    lat_b, lat_a = swapped(lat_b, "lat", 1), swapped(lat_a, "lat", 0)
    return lon_a, lon_b, lat_a, lat_b


def on_device(
    latent_field,
    east_courant,
    north_courant,
    mixing,
    sunlit,
    decode_w,
    react_a,
    react_b,
    stoich,
    encode_w,
    rate_const,
):
    n_species, n_levels, n_rows, n_cols = latent_field.shape
    layered = jax.ShapeDtypeStruct((n_levels, n_rows, n_species, n_cols), F32)
    side = jax.ShapeDtypeStruct((n_species, n_cols), F32)
    edge = jax.ShapeDtypeStruct((n_levels, n_species, n_cols), BF16)
    params = pltpu.CompilerParams(vmem_limit_bytes=VMEM_BYTES)
    smem = pl.BlockSpec(memory_space=pltpu.SMEM)
    hbm = pl.BlockSpec(memory_space=pltpu.HBM)
    n_reactions = react_a.shape[0]
    edges = pl.pallas_call(
        first_kernel,
        out_shape=(side, side, edge, edge),
        in_specs=[hbm] * 3,
        out_specs=tuple(vmem(4)),
        scratch_shapes=[
            pltpu.VMEM((n_levels, n_species, n_rows, n_cols), F32),
            pltpu.VMEM((n_levels, n_rows, n_cols), F32),
            pltpu.VMEM((n_levels, n_rows, n_cols), F32),
            pltpu.SemaphoreType.DMA((n_levels + 2,)),
        ],
        compiler_params=pltpu.CompilerParams(vmem_limit_bytes=FIRST_VMEM_BYTES),
        name="first_sends",
        cost_estimate=pl.CostEstimate(flops=4_000_000_000, bytes_accessed=2_000_000, transcendentals=0),
    )(latent_field, east_courant, north_courant)
    weights = (decode_w.T, react_a.T, react_b.T, stoich, encode_w, rate_const[None])
    folded = (
        jax.ShapeDtypeStruct((2 * n_reactions, n_species), BF16),
        jax.ShapeDtypeStruct((n_species, n_reactions), BF16),
    )
    field = latent_field
    for step in range(STEPS):
        first, last = step == 0, step == STEPS - 1
        halos = exchanged(*edges)
        scratch = [pltpu.VMEM(layered.shape, F32)] if first else []
        if last:
            scratch += [
                pltpu.VMEM((2, n_levels, n_species, n_rows // 2, n_cols), F32),
                pltpu.SemaphoreType.DMA((2, n_levels)),
            ]
        scratch += [pltpu.VMEM(array.shape, array.dtype) for array in (edge, edge, side, side)]
        scratch += [
            pltpu.VMEM((8, n_levels, n_rows, n_cols), F32),
            pltpu.VMEM((n_levels, n_rows + ROWS_IN_FLIGHT, n_species, n_cols), F32),
        ]
        outs = pl.pallas_call(
            functools.partial(step_kernel, n_levels, n_rows, first, last),
            out_shape=(jax.ShapeDtypeStruct(latent_field.shape, F32),)
            if last
            else (layered, side, side, edge, edge, *folded),
            in_specs=[smem] + vmem(8 + len(weights)),
            out_specs=(hbm,) if last else tuple(vmem(7)),
            scratch_shapes=scratch,
            compiler_params=params,
            name="splitting_step",
            cost_estimate=pl.CostEstimate(flops=20_000_000_000, bytes_accessed=1, transcendentals=0),
        )(sunlit, field, east_courant, north_courant, mixing, *halos, *weights)
        field, edges, weights = outs[0], outs[1:5], outs[5:]
    return field


def solution(mesh):
    placed = (
        P(None, None, "lat", "lon"),
        P(None, "lat", "lon"),
        P(None, "lat", "lon"),
        P(None, "lat", "lon"),
        P("lat", "lon"),
        P(),
        P(),
        P(),
        P(),
        P(),
        P(),
    )
    return jax.shard_map(
        on_device,
        mesh=mesh,
        in_specs=placed,
        out_specs=P(None, None, "lat", "lon"),
        check_vma=False,
    )
```

profile of v0, /device:TPU:0, one launch (start us, length us, event | category | flops | bytes accessed | tf_op | source)
XLA Modules:
  0.0 45.2 jit_solution(9465004041520027542)
XLA Ops:
  0.0 0.0 copy-start.5
  0.0 0.0 copy-start.4
  0.0 0.0 copy-start
  0.0 0.0 copy-start.10
  0.0 0.0 copy-start.6
  0.0 0.0 copy-start.9
  0.0 0.0 copy-start.8
  0.0 0.0 copy-start.3
  0.0 0.0 copy-start.2
  0.1 0.0 copy-start.1
  0.1 0.0 copy-start.7
  0.1 3.1 %first_sends.1 = (f32[32,128]{1,0:T(8,128)}, f32[32,128]{1,0:T(8,128)}, bf16[8,32,128]{2,1,0:T(8,128)(2,1)}, bf16[8,32,128]{2,1,0:T(8,128)(2,1)}) custom-call(f32[32,8,16,128]{3,2,1,0:T(8,128)} %field.1, f32[8,16,128]{2,1,0:T(8,128)} %east_c.5, f32[8,16,128]{2,1,0:T(8,128)} %north_c.5), custom_call_target="tpu_custom_call" | custom-call | flops 4000000000 | bytes 2000000 | tf_op jit(solution)/shard_map/first_sends/pallas_call | solution.py:350
  3.2 0.5 %collective-permute-start.2 = (bf16[8,32,128]{2,1,0:T(8,128)(2,1)}, bf16[8,32,128]{2,1,0:T(8,128)(2,1)S(1)}, u32[]{:S(2)}, u32[]{:S(2)}) collective-permute-start(bf16[8,32,128]{2,1,0:T(8,128)(2,1)} %get-tuple-element.18), channel_id=1, source_target_pairs={{0,8},{16,24},{8,0},{24,16},{1,9},{17,25},{9,1},{25,17},{2,10},{18... | collective-permute-start | bytes 196616 | tf_op jit(solution)/shard_map/ppermute | solution.py:322
  3.7 2.6 %collective-permute-start.3 = (bf16[8,32,128]{2,1,0:T(8,128)(2,1)}, bf16[8,32,128]{2,1,0:T(8,128)(2,1)S(1)}, u32[]{:S(2)}, u32[]{:S(2)}) collective-permute-start(bf16[8,32,128]{2,1,0:T(8,128)(2,1)} %get-tuple-element.19), channel_id=1, source_target_pairs={{8,16},{24,0},{16,8},{0,24},{9,17},{25,1},{17,9},{1,25},{10,18},{2... | collective-permute-start | bytes 196616 | tf_op jit(solution)/shard_map/ppermute | solution.py:322
  6.3 1.5 %collective-permute-start = (f32[32,128]{1,0:T(8,128)}, f32[32,128]{1,0:T(8,128)S(1)}, u32[]{:S(2)}, u32[]{:S(2)}) collective-permute-start(f32[32,128]{1,0:T(8,128)} %get-tuple-element.16), channel_id=1, source_target_pairs={{0,1},{2,3},{4,5},{6,7},{1,0},{3,2},{5,4},{7,6},{8,9},{10,11},{12,... | collective-permute-start | bytes 49160 | tf_op jit(solution)/shard_map/ppermute | solution.py:322
  7.8 3.5 %collective-permute-start.1 = (f32[32,128]{1,0:T(8,128)}, f32[32,128]{1,0:T(8,128)S(1)}, u32[]{:S(2)}, u32[]{:S(2)}) collective-permute-start(f32[32,128]{1,0:T(8,128)} %get-tuple-element.17), channel_id=1, source_target_pairs={{1,2},{3,4},{5,6},{7,0},{2,1},{4,3},{6,5},{0,7},{9,10},{11,12},{13... | collective-permute-start | bytes 49160 | tf_op jit(solution)/shard_map/ppermute | solution.py:322
  11.4 0.0 collective-permute-done.lon_a_in
  11.4 3.1 %collective-permute-done.1.lon_b_in = f32[32,128]{1,0:T(8,128)S(1)} collective-permute-done((f32[32,128]{1,0:T(8,128)}, f32[32,128]{1,0:T(8,128)S(1)}, u32[]{:S(2)}, u32[]{:S(2)}) %collective-permute-start.1) | collective-permute-done | bytes 16416 | tf_op jit(solution)/shard_map/ppermute | solution.py:322
  14.5 0.0 collective-permute-done.2.lat_a_in
  14.5 0.0 collective-permute-done.3.lat_b_in
  14.5 0.0 copy-done.5
  14.5 0.0 copy-done.4
  14.5 0.0 copy-done
  14.5 0.0 copy-done.10
  14.5 0.0 copy-done.6
  14.5 0.0 copy-done.9
  14.5 0.0 copy-done.8
  14.5 0.0 copy-done.3
  14.6 0.0 copy-done.2
  14.6 0.0 copy-done.1
  14.6 0.0 copy-done.7
  14.6 11.4 %splitting_step.2 = (f32[8,16,32,128]{3,2,1,0:T(8,128)S(1)}, f32[32,128]{1,0:T(8,128)S(1)}, f32[32,128]{1,0:T(8,128)S(1)}, bf16[8,32,128]{2,1,0:T(8,128)(2,1)S(1...) custom-call(s32[1,8]{1,0:T(1,128)S(1)} %copy-done.10, ...), custom_call_target="tpu_custom_call" | custom-call | flops 20000000000 | bytes 1 | tf_op jit(solution)/shard_map/splitting_step/pallas_call | solution.py:385
  26.0 0.1 collective-permute-start.6
  26.1 0.6 %collective-permute-start.7 = (bf16[8,32,128]{2,1,0:T(8,128)(2,1)S(1)}, bf16[8,32,128]{2,1,0:T(8,128)(2,1)S(1)}, u32[]{:S(2)}, u32[]{:S(2)}) collective-permute-start(bf16[8,32,128]{2,1,0:T(8,128)(2,1)S(1)} %get-tuple-element.24), channel_id=1, source_target_pairs={{8,16},{24,0},{16,8},{0,24},{9,17},{25,1},{17,9},{1,25},{10,18},{2... | collective-permute-start | bytes 196616 | tf_op jit(solution)/shard_map/ppermute | solution.py:322
  26.8 0.0 collective-permute-start.4
  26.8 3.5 %collective-permute-start.5 = (f32[32,128]{1,0:T(8,128)S(1)}, f32[32,128]{1,0:T(8,128)S(1)}, u32[]{:S(2)}, u32[]{:S(2)}) collective-permute-start(f32[32,128]{1,0:T(8,128)S(1)} %get-tuple-element.22), channel_id=1, source_target_pairs={{1,2},{3,4},{5,6},{7,0},{2,1},{4,3},{6,5},{0,7},{9,10},{11,12},{13... | collective-permute-start | bytes 49160 | tf_op jit(solution)/shard_map/ppermute | solution.py:322
  30.3 0.2 collective-permute-done.4.lon_a_in
  30.5 2.7 %collective-permute-done.5.lon_b_in = f32[32,128]{1,0:T(8,128)S(1)} collective-permute-done((f32[32,128]{1,0:T(8,128)S(1)}, f32[32,128]{1,0:T(8,128)S(1)}, u32[]{:S(2)}, u32[]{:S(2)}) %collective-permute-start.5) | collective-permute-done | bytes 16416 | tf_op jit(solution)/shard_map/ppermute | solution.py:322
  33.2 0.0 collective-permute-done.6.lat_a_in
  33.2 0.0 collective-permute-done.7.lat_b_in
  33.2 12.0 %splitting_step.3 = f32[32,8,16,128]{3,2,1,0:T(8,128)} custom-call(s32[1,8]{1,0:T(1,128)S(1)} %copy-done.10, f32[8,16,32,128]{3,2,1,0:T(8,128)S(1)} %get-tuple-element.20.field, f32[8,16,128]{2,1,0:T(8,128)S(1)} %copy-done.4, f32[8,16,128]{2,1,0:T(8,128)S(1)} %copy-done.5, f32[7,16,128]{2,1,0:T(8,128)S(1)} %copy-done.6, ...), custom_call_target="tpu_custom_call" | custom-call | flops 20000000000 | bytes 1 | tf_op jit(solution)/shard_map/splitting_step/pallas_call | solution.py:385
Async XLA Ops:
  0.0 14.5 %copy-start.5 = (f32[8,16,128]{2,1,0:T(8,128)S(1)}, f32[8,16,128]{2,1,0:T(8,128)}, u32[]{:S(2)}) copy-start(f32[8,16,128]{2,1,0:T(8,128)} %north_c.5) | copy-start | bytes 196612
  0.0 14.5 %copy-start.4 = (f32[8,16,128]{2,1,0:T(8,128)S(1)}, f32[8,16,128]{2,1,0:T(8,128)}, u32[]{:S(2)}) copy-start(f32[8,16,128]{2,1,0:T(8,128)} %east_c.5) | copy-start | bytes 196612
  0.0 14.5 %copy-start = (f32[32,8,16,128]{3,2,1,0:T(8,128)S(1)}, f32[32,8,16,128]{3,2,1,0:T(8,128)}, u32[]{:S(2)}) copy-start(f32[32,8,16,128]{3,2,1,0:T(8,128)} %field.1) | copy-start | bytes 6291460
  0.0 14.5 %copy-start.10 = (s32[1,8]{1,0:T(1,128)S(1)}, s32[1,8]{1,0:T(1,128)}, u32[]{:S(2)}) copy-start(s32[1,8]{1,0:T(1,128)} %sun.3) | copy-start | bytes 100
  0.0 14.5 %copy-start.6 = (f32[7,16,128]{2,1,0:T(8,128)S(1)}, f32[7,16,128]{2,1,0:T(8,128)}, u32[]{:S(2)}) copy-start(f32[7,16,128]{2,1,0:T(8,128)} %mixing.3) | copy-start | bytes 172036
  0.0 14.5 %copy-start.9 = (f32[256]{0:T(256)S(1)}, f32[256]{0:T(256)}, u32[]{:S(2)}) copy-start(f32[256]{0:T(256)} %param.21) | copy-start | bytes 3076
  0.0 14.5 %copy-start.8 = (bf16[32,224]{1,0:T(8,128)(2,1)S(1)}, bf16[32,224]{1,0:T(8,128)(2,1)}, u32[]{:S(2)}) copy-start(bf16[32,224]{1,0:T(8,128)(2,1)} %refs_4_.1) | copy-start | bytes 43012
  0.0 14.5 %copy-start.3 = (bf16[224,256]{1,0:T(8,128)(2,1)S(1)}, bf16[224,256]{1,0:T(8,128)(2,1)}, u32[]{:S(2)}) copy-start(bf16[224,256]{1,0:T(8,128)(2,1)} %refs_3_.1) | copy-start | bytes 344068
  0.0 14.5 %copy-start.2 = (bf16[256,224]{0,1:T(8,128)(2,1)S(1)}, bf16[256,224]{0,1:T(8,128)(2,1)}, u32[]{:S(2)}) copy-start(bf16[256,224]{0,1:T(8,128)(2,1)} %param.18) | copy-start | bytes 344068
  0.1 14.5 %copy-start.1 = (bf16[256,224]{0,1:T(8,128)(2,1)S(1)}, bf16[256,224]{0,1:T(8,128)(2,1)}, u32[]{:S(2)}) copy-start(bf16[256,224]{0,1:T(8,128)(2,1)} %param.17) | copy-start | bytes 344068
  0.1 14.5 %copy-start.7 = (bf16[224,32]{0,1:T(8,128)(2,1)S(1)}, bf16[224,32]{0,1:T(8,128)(2,1)}, u32[]{:S(2)}) copy-start(bf16[224,32]{0,1:T(8,128)(2,1)} %param.16) | copy-start | bytes 43012
  3.2 11.3 %collective-permute-start.2 = (bf16[8,32,128]{2,1,0:T(8,128)(2,1)}, bf16[8,32,128]{2,1,0:T(8,128)(2,1)S(1)}, u32[]{:S(2)}, u32[]{:S(2)}) collective-permute-start(bf16[8,32,128]{2,1,0:T(8,128)(2,1)} %get-tuple-element.18), channel_id=1, source_target_pairs={{0,8},{16,24},{8,0},{24,16},{1,9},{17,25},{9,1},{25,17},{2,10},{18... | collective-permute-start | bytes 196616 | tf_op jit(solution)/shard_map/ppermute | solution.py:322
  3.7 10.8 %collective-permute-start.3 = (bf16[8,32,128]{2,1,0:T(8,128)(2,1)}, bf16[8,32,128]{2,1,0:T(8,128)(2,1)S(1)}, u32[]{:S(2)}, u32[]{:S(2)}) collective-permute-start(bf16[8,32,128]{2,1,0:T(8,128)(2,1)} %get-tuple-element.19), channel_id=1, source_target_pairs={{8,16},{24,0},{16,8},{0,24},{9,17},{25,1},{17,9},{1,25},{10,18},{2... | collective-permute-start | bytes 196616 | tf_op jit(solution)/shard_map/ppermute | solution.py:322
  6.3 5.1 %collective-permute-start = (f32[32,128]{1,0:T(8,128)}, f32[32,128]{1,0:T(8,128)S(1)}, u32[]{:S(2)}, u32[]{:S(2)}) collective-permute-start(f32[32,128]{1,0:T(8,128)} %get-tuple-element.16), channel_id=1, source_target_pairs={{0,1},{2,3},{4,5},{6,7},{1,0},{3,2},{5,4},{7,6},{8,9},{10,11},{12,... | collective-permute-start | bytes 49160 | tf_op jit(solution)/shard_map/ppermute | solution.py:322
  7.8 6.6 %collective-permute-start.1 = (f32[32,128]{1,0:T(8,128)}, f32[32,128]{1,0:T(8,128)S(1)}, u32[]{:S(2)}, u32[]{:S(2)}) collective-permute-start(f32[32,128]{1,0:T(8,128)} %get-tuple-element.17), channel_id=1, source_target_pairs={{1,2},{3,4},{5,6},{7,0},{2,1},{4,3},{6,5},{0,7},{9,10},{11,12},{13... | collective-permute-start | bytes 49160 | tf_op jit(solution)/shard_map/ppermute | solution.py:322
  26.0 7.2 %collective-permute-start.6 = (bf16[8,32,128]{2,1,0:T(8,128)(2,1)S(1)}, bf16[8,32,128]{2,1,0:T(8,128)(2,1)S(1)}, u32[]{:S(2)}, u32[]{:S(2)}) collective-permute-start(bf16[8,32,128]{2,1,0:T(8,128)(2,1)S(1)} %get-tuple-element.23), channel_id=1, source_target_pairs={{0,8},{16,24},{8,0},{24,16},{1,9},{17,25},{9,1},{25,17},{2,10},{18... | collective-permute-start | bytes 196616 | tf_op jit(solution)/shard_map/ppermute | solution.py:322
  26.1 7.1 %collective-permute-start.7 = (bf16[8,32,128]{2,1,0:T(8,128)(2,1)S(1)}, bf16[8,32,128]{2,1,0:T(8,128)(2,1)S(1)}, u32[]{:S(2)}, u32[]{:S(2)}) collective-permute-start(bf16[8,32,128]{2,1,0:T(8,128)(2,1)S(1)} %get-tuple-element.24), channel_id=1, source_target_pairs={{8,16},{24,0},{16,8},{0,24},{9,17},{25,1},{17,9},{1,25},{10,18},{2... | collective-permute-start | bytes 196616 | tf_op jit(solution)/shard_map/ppermute | solution.py:322
  26.8 3.7 %collective-permute-start.4 = (f32[32,128]{1,0:T(8,128)S(1)}, f32[32,128]{1,0:T(8,128)S(1)}, u32[]{:S(2)}, u32[]{:S(2)}) collective-permute-start(f32[32,128]{1,0:T(8,128)S(1)} %get-tuple-element.21), channel_id=1, source_target_pairs={{0,1},{2,3},{4,5},{6,7},{1,0},{3,2},{5,4},{7,6},{8,9},{10,11},{12,... | collective-permute-start | bytes 49160 | tf_op jit(solution)/shard_map/ppermute | solution.py:322
  26.8 6.4 %collective-permute-start.5 = (f32[32,128]{1,0:T(8,128)S(1)}, f32[32,128]{1,0:T(8,128)S(1)}, u32[]{:S(2)}, u32[]{:S(2)}) collective-permute-start(f32[32,128]{1,0:T(8,128)S(1)} %get-tuple-element.22), channel_id=1, source_target_pairs={{1,2},{3,4},{5,6},{7,0},{2,1},{4,3},{6,5},{0,7},{9,10},{11,12},{13... | collective-permute-start | bytes 49160 | tf_op jit(solution)/shard_map/ppermute | solution.py:322
where the time goes:
time: 45.3 us; the launch traced here: 45.2 us
  Pallas kernels  26.5 us (58%)
  starting transfers between devices  12.5 us (28%)
  waiting for transfers between devices  6 us (13%)
    pallas_call x2, Pallas kernels, on_device(): pl.pallas_call(functools.partial(step_kernel, n_levels, n_rows, first, la...  23.4 us
    ppermute x8, starting transfers between devices, swapped(): return lax.ppermute(array, axis, pairs + [(j, i) for i, j in pairs])  12.5 us
    ppermute x8, waiting for transfers between devices, swapped(): return lax.ppermute(array, axis, pairs + [(j, i) for i, j in pairs])  6 us
    pallas_call x1, Pallas kernels, on_device(): pl.pallas_call(first_kernel, out_shape=(side, side, edge, edge), in_specs...  3.07 us
  transfers between devices with their start and end apart: 8, of which 3 were waited for; matrix products, arithmetic and copies ran while one was open for 0% of the time, Pallas kernels for 0%

commit v1 on v0

--- a/solution.py
+++ b/solution.py
@@ -58,23 +58,20 @@
     into_second[...] = jnp.where(even, down, up)
 
 
-def pack_sides(value, coef, at, west, east):
-    lanes = lane_ids(value.shape)
-    size = value.shape[-1]
-    turned = pltpu.roll(value * coef, at, 1)
-    west = jnp.where(lanes == at, turned, west)
-    east = jnp.where(lanes == (at + size - 1) % size, turned, east)
-    return west, east
-
-
-def first_kernel(latent, east_c, north_c, lon_a, lon_b, lat_a, lat_b, *scratch):
-    tiles, east_v, north_v, sems = scratch
+COLUMN_ROWS = 40
+EAST_ROW, NORTH_ROW, MIXING_ROW, LIT_ROW = 32, 33, 34, 35
+
+
+def first_kernel(sun, latent, east_c, north_c, mixing, lon_a, lon_b, lat_a, lat_b, *scratch):
+    tiles, east_v, north_v, mixing_v, sems = scratch
     n_levels, n_species, n_rows, n_cols = tiles.shape
     lanes = lane_ids((1, n_cols))
     is_first, is_last = at_ends()
     copies = [
-        pltpu.make_async_copy(east_c, east_v, sems.at[n_levels]),
-        pltpu.make_async_copy(north_c, north_v, sems.at[n_levels + 1]),
+        pltpu.make_async_copy(source, held, sems.at[n_levels + at])
+        for at, (source, held) in enumerate(
+            ((east_c, east_v), (north_c, north_v), (mixing, mixing_v))
+        )
     ]
     levels = [
         pltpu.make_async_copy(latent.at[:, level], tiles.at[level], sems.at[level])
@@ -84,22 +81,83 @@
         copy.start()
     for copy in copies:
         copy.wait()
-    sides = (jnp.zeros((n_species, n_cols), F32),) * 2
+    turns = (0, 1, -2, -1)
+    columns = [jnp.zeros((COLUMN_ROWS, n_cols), F32) for _ in turns]
     for level in range(n_levels):
         levels[level].wait()
-        tile = jnp.transpose(tiles[level], (1, 0, 2))
+        extra = [east_v[level], north_v[level]]
+        if level < n_levels - 1:
+            extra.append(mixing_v[level])
+        extra += [jnp.zeros((n_rows, n_cols), F32)] * (COLUMN_ROWS - n_species - len(extra))
+        tile = jnp.transpose(
+            jnp.concatenate([tiles[level]] + [plane[None] for plane in extra], axis=0), (1, 0, 2)
+        )
         for r in range(n_rows):
             at = level * n_rows + r
-            value = tile[r]
-            speed = east_v[level, r : r + 1, :]
-            coef = jnp.where(lanes == 0, jnp.minimum(speed, 0.0), jnp.maximum(speed, 0.0))
-            sides = pack_sides(value, coef, at, *sides)
+            turned = pltpu.roll(tile[r], at, 1)
+            columns = [
+                jnp.where(lanes == (at + turn) % n_cols, turned, column)
+                for turn, column in zip(turns, columns)
+            ]
         ends = []
         for r, closed, clip in ((0, is_first, jnp.minimum), (n_rows - 1, is_last, jnp.maximum)):
             speed = clip(north_v[level, r : r + 1, :], 0.0)
-            ends.append((tile[r] * jnp.where(closed, 0.0, speed)).astype(BF16))
+            ends.append((tile[r, :n_species] * jnp.where(closed, 0.0, speed)).astype(BF16))
         by_parity("lat", ends[1], ends[0], lat_a.at[level], lat_b.at[level])
-    by_parity("lon", sides[1], sides[0], lon_a, lon_b)
+    columns = [
+        column if turn == 0 else pltpu.roll(column, -turn % n_cols, 1)
+        for turn, column in zip(turns, columns)
+    ]
+    kinds = lax.broadcasted_iota(jnp.int32, (COLUMN_ROWS, n_cols), 0)
+    lit_west = sun[0, 0].astype(F32)
+    lit_east = sun[0, n_cols // BLOCK - 1].astype(F32)
+    west = [jnp.where(kinds == LIT_ROW, lit_west, columns[at]) for at in (0, 1)]
+    east = [jnp.where(kinds == LIT_ROW, lit_east, columns[at]) for at in (3, 2)]
+    by_parity("lon", jnp.concatenate(east, axis=0), jnp.concatenate(west, axis=0), lon_a, lon_b)
+
+
+def split_columns(message):
+    return message[:COLUMN_ROWS], message[COLUMN_ROWS:]
+
+
+def inflow(column, n_species, clip):
+    return column[:n_species] * clip(column[EAST_ROW : EAST_ROW + 1], 0.0)
+
+
+def lat_inflow(column, n_species, clip):
+    return column[:n_species] * clip(column[NORTH_ROW : NORTH_ROW + 1], 0.0)
+
+
+def diffused_column(column, west, east, south, north, n_species, n_levels, n_rows, ends):
+    n_cols = column.shape[1]
+    lanes = lane_ids((1, n_cols))
+    levels, rows = lanes // n_rows, lanes % n_rows
+    is_first, is_last = ends
+    speed = column[EAST_ROW : EAST_ROW + 1]
+    lat_speed = column[NORTH_ROW : NORTH_ROW + 1]
+    up = jnp.where((rows == n_rows - 1) & is_last, 0.0, jnp.maximum(lat_speed, 0.0))
+    down = jnp.where((rows == 0) & is_first, 0.0, jnp.minimum(lat_speed, 0.0))
+    value = column[:n_species]
+    from_south = jnp.where(rows == 0, south, pltpu.roll(value * up, 1, 1))
+    from_north = jnp.where(rows == n_rows - 1, north, pltpu.roll(value * down, n_cols - 1, 1))
+    centre = 1.0 - jnp.abs(speed) - up + down
+    moved = value * centre + (west - east) + (from_south - from_north)
+    above = column[MIXING_ROW : MIXING_ROW + 1]
+    below = jnp.where(levels == 0, 0.0, pltpu.roll(above, n_rows, 1))
+    upper = jnp.zeros((1, n_cols), F32)
+    scale = upper
+    for level in range(n_levels):
+        pivot = 1.0 + below + above - below * pltpu.roll(upper, n_rows, 1)
+        scale = jnp.where(levels == level, 1.0 / pivot, scale)
+        upper = above * scale
+    solved = jnp.zeros_like(moved)
+    for level in range(n_levels):
+        swept = (moved + below * pltpu.roll(solved, n_rows, 1)) * scale
+        solved = jnp.where(levels == level, swept, solved)
+    for level in range(n_levels - 2, -1, -1):
+        swept = solved + upper * pltpu.roll(solved, n_cols - n_rows, 1)
+        solved = jnp.where(levels == level, swept, solved)
+    return solved
 
 
 def step_kernel(
@@ -120,14 +178,13 @@
 ):
     if first:
         weights, refs = refs[:6], refs[6:]
-        linear, encode = refs[5:7]
+        linear, encode = refs[3:5]
     else:
-        (linear, encode), refs = refs[:2], refs[2:]
+        (lon_a_own, lon_b_own, linear, encode), refs = refs[:4], refs[4:]
     half_rows = n_rows // 2
     south_in, north_in, west_in, east_in, coefs, diffused = refs[-6:]
     if last:
         staged, sems = refs[-8:-6]
-    by_parity("lon", lon_a_in[...], lon_b_in[...], east_in, west_in)
     by_parity("lat", lat_a_in[...], lat_b_in[...], north_in, south_in)
     n_species, n_cols = west_in.shape
     n_reactions = encode.shape[1]
@@ -167,6 +224,10 @@
             upper = mixing[level] * scale
             coefs[UPPER, level] = upper
 
+    even = is_even("lon")
+    west_near, west_far = split_columns(jnp.where(even, lon_b_in[...], lon_a_in[...]))
+    east_near, east_far = split_columns(jnp.where(even, lon_a_in[...], lon_b_in[...]))
+
     lit = jnp.zeros((1, n_cols), jnp.int32)
     for block in range(n_cols // BLOCK):
         lit = jnp.where(lanes // BLOCK == block, sun[0, block], lit)
@@ -184,7 +245,7 @@
             value = field[level, r]
             from_west = jnp.where(
                 lanes == 0,
-                pltpu.roll(west_in[...], (n_cols + 1 - at) % n_cols, 1),
+                pltpu.roll(west_in[...], (n_cols - at) % n_cols, 1),
                 pltpu.roll(value * coef(EAST, level, r), 1, 1),
             )
             from_east = jnp.where(
@@ -220,6 +281,53 @@
         ]
         return jnp.concatenate(parts, axis=0).astype(BF16)
 
+    if first:
+        west_in[...] = inflow(west_near, n_species, jnp.maximum)
+        east_in[...] = inflow(east_near, n_species, jnp.minimum)
+    else:
+        own_west, _ = split_columns(jnp.where(even, lon_b_own[...], lon_a_own[...]))
+        own_east, _ = split_columns(jnp.where(even, lon_a_own[...], lon_b_own[...]))
+        ends = is_first, is_last
+
+        def corner(edge, at, turn):
+            return pltpu.roll(edge[n_levels + at].astype(F32), turn, 1)
+
+        def column_after(at, near, west, east):
+            return diffused_column(
+                near,
+                inflow(west, n_species, jnp.maximum),
+                inflow(east, n_species, jnp.minimum),
+                corner(south_in, at, n_cols - (n_rows - 1)),
+                corner(north_in, at, n_rows - 1),
+                n_species,
+                n_levels,
+                n_rows,
+                ends,
+            )
+
+        pair = jnp.concatenate(
+            [
+                column_after(0, west_near, west_far, own_west),
+                column_after(1, east_near, own_east, east_far),
+            ],
+            axis=1,
+        )
+        rounded = pair.astype(BF16)
+        current, summed = rounded.astype(F32), None
+        for substep in range(SUBSTEPS):
+            change = jnp.dot(encode[...], product_of(rounded), preferred_element_type=F32)
+            summed = change if summed is None else summed + change
+            current = current + change
+            rounded = current.astype(BF16)
+        pair_lit = jnp.concatenate(
+            [near[LIT_ROW : LIT_ROW + 1] for near in (west_near, east_near)], axis=1
+        )
+        pair = pair + jnp.where(pair_lit > 0.0, summed, 0.0)
+        west_speed = west_near[EAST_ROW : EAST_ROW + 1]
+        east_speed = east_near[EAST_ROW : EAST_ROW + 1]
+        west_in[...] = pair[:, :n_cols] * jnp.maximum(west_speed, 0.0)
+        east_in[...] = pair[:, n_cols:] * jnp.minimum(east_speed, 0.0)
+
     for r in range(ROWS_IN_FLIGHT):
         for _ in transport(r):
             pass
@@ -230,7 +338,7 @@
             [diffused[level + extra, r] for extra in range(LEVELS_AT_ONCE)], axis=1
         )
 
-    def rows(turn, sides):
+    def rows(turn, carry):
         units, ahead = [], {}
         for first_row in range(0, ROWS_AT_ONCE, ROWS_IN_FLIGHT):
             in_flight = [turn * ROWS_AT_ONCE + first_row + extra for extra in range(ROWS_IN_FLIGHT)]
@@ -269,12 +377,7 @@
                         diffused[at_level, r] = part
                     else:
                         refs[0][at_level, r] = part
-                        speed = east_c[at_level, pl.ds(r, 1), :]
-                        side = jnp.where(
-                            lanes == 0, jnp.minimum(speed, 0.0), jnp.maximum(speed, 0.0)
-                        )
-                        sides = pack_sides(part, side, at_level * n_rows + r, *sides)
-        return sides
+        return carry
 
     if last:
 
@@ -301,29 +404,26 @@
             for copy in sends(half):
                 copy.wait()
         return
-    out, lon_a, lon_b, lat_a, lat_b = refs[:5]
-    zeros = jnp.zeros((n_species, n_cols), F32)
-    west, east = lax.fori_loop(0, n_rows // ROWS_AT_ONCE, rows, (zeros, zeros))
-    by_parity("lon", east, west, lon_a, lon_b)
+    out, lat_a, lat_b = refs[:3]
+    lax.fori_loop(0, n_rows // ROWS_AT_ONCE, rows, 0)
     for level in range(n_levels):
         south = (out[level, 0] * coefs[SOUTH, level, :1]).astype(BF16)
         north = (out[level, n_rows - 1] * coefs[NORTH, level, n_rows - 1 :]).astype(BF16)
         by_parity("lat", north, south, lat_a.at[level], lat_b.at[level])
+    for at, near in enumerate((west_near, east_near)):
+        south = jnp.where(is_first, 0.0, lat_inflow(near, n_species, jnp.minimum)).astype(BF16)
+        north = jnp.where(is_last, 0.0, lat_inflow(near, n_species, jnp.maximum)).astype(BF16)
+        by_parity("lat", north, south, lat_a.at[n_levels + at], lat_b.at[n_levels + at])
 
 
 def vmem(count):
     return [pl.BlockSpec(memory_space=pltpu.VMEM)] * count
 
 
-def exchanged(lon_a, lon_b, lat_a, lat_b):
-    def swapped(array, axis, first):
-        size = lax.axis_size(axis)
-        pairs = [(i % size, (i + 1) % size) for i in range(first, size + first, 2)]
-        return lax.ppermute(array, axis, pairs + [(j, i) for i, j in pairs])
-
-    lon_b, lon_a = swapped(lon_b, "lon", 1), swapped(lon_a, "lon", 0)
-    lat_b, lat_a = swapped(lat_b, "lat", 1), swapped(lat_a, "lat", 0)
-    return lon_a, lon_b, lat_a, lat_b
+def swapped(array, axis, first):
+    size = lax.axis_size(axis)
+    pairs = [(i % size, (i + 1) % size) for i in range(first, size + first, 2)]
+    return lax.ppermute(array, axis, pairs + [(j, i) for i, j in pairs])
 
 
 def on_device(
@@ -341,61 +441,67 @@
 ):
     n_species, n_levels, n_rows, n_cols = latent_field.shape
     layered = jax.ShapeDtypeStruct((n_levels, n_rows, n_species, n_cols), F32)
+    column = jax.ShapeDtypeStruct((2 * COLUMN_ROWS, n_cols), F32)
     side = jax.ShapeDtypeStruct((n_species, n_cols), F32)
     edge = jax.ShapeDtypeStruct((n_levels, n_species, n_cols), BF16)
+    cornered = jax.ShapeDtypeStruct((n_levels + 2, n_species, n_cols), BF16)
     params = pltpu.CompilerParams(vmem_limit_bytes=VMEM_BYTES)
     smem = pl.BlockSpec(memory_space=pltpu.SMEM)
     hbm = pl.BlockSpec(memory_space=pltpu.HBM)
     n_reactions = react_a.shape[0]
-    edges = pl.pallas_call(
+    lon_a, lon_b, lat_a, lat_b = pl.pallas_call(
         first_kernel,
-        out_shape=(side, side, edge, edge),
-        in_specs=[hbm] * 3,
+        out_shape=(column, column, edge, edge),
+        in_specs=[smem] + [hbm] * 4,
         out_specs=tuple(vmem(4)),
         scratch_shapes=[
             pltpu.VMEM((n_levels, n_species, n_rows, n_cols), F32),
-            pltpu.VMEM((n_levels, n_rows, n_cols), F32),
-            pltpu.VMEM((n_levels, n_rows, n_cols), F32),
-            pltpu.SemaphoreType.DMA((n_levels + 2,)),
+            pltpu.VMEM(east_courant.shape, F32),
+            pltpu.VMEM(north_courant.shape, F32),
+            pltpu.VMEM(mixing.shape, F32),
+            pltpu.SemaphoreType.DMA((n_levels + 3,)),
         ],
         compiler_params=pltpu.CompilerParams(vmem_limit_bytes=FIRST_VMEM_BYTES),
         name="first_sends",
         cost_estimate=pl.CostEstimate(flops=4_000_000_000, bytes_accessed=2_000_000, transcendentals=0),
-    )(latent_field, east_courant, north_courant)
+    )(sunlit, latent_field, east_courant, north_courant, mixing)
     weights = (decode_w.T, react_a.T, react_b.T, stoich, encode_w, rate_const[None])
     folded = (
         jax.ShapeDtypeStruct((2 * n_reactions, n_species), BF16),
         jax.ShapeDtypeStruct((n_species, n_reactions), BF16),
     )
+    lon_halos = swapped(lon_a, "lon", 0), swapped(lon_b, "lon", 1)
     field = latent_field
     for step in range(STEPS):
         first, last = step == 0, step == STEPS - 1
-        halos = exchanged(*edges)
+        lat_halos = swapped(lat_a, "lat", 0), swapped(lat_b, "lat", 1)
         scratch = [pltpu.VMEM(layered.shape, F32)] if first else []
         if last:
             scratch += [
                 pltpu.VMEM((2, n_levels, n_species, n_rows // 2, n_cols), F32),
                 pltpu.SemaphoreType.DMA((2, n_levels)),
             ]
-        scratch += [pltpu.VMEM(array.shape, array.dtype) for array in (edge, edge, side, side)]
+        scratch += [pltpu.VMEM(array.shape, array.dtype) for array in (*lat_halos, side, side)]
         scratch += [
             pltpu.VMEM((8, n_levels, n_rows, n_cols), F32),
             pltpu.VMEM((n_levels, n_rows + ROWS_IN_FLIGHT, n_species, n_cols), F32),
         ]
+        operands = weights if first else (lon_a, lon_b, *weights)
         outs = pl.pallas_call(
             functools.partial(step_kernel, n_levels, n_rows, first, last),
             out_shape=(jax.ShapeDtypeStruct(latent_field.shape, F32),)
             if last
-            else (layered, side, side, edge, edge, *folded),
-            in_specs=[smem] + vmem(8 + len(weights)),
-            out_specs=(hbm,) if last else tuple(vmem(7)),
+            else (layered, cornered, cornered, *folded),
+            in_specs=[smem] + vmem(8 + len(operands)),
+            out_specs=(hbm,) if last else tuple(vmem(5)),
             scratch_shapes=scratch,
             compiler_params=params,
             name="splitting_step",
             cost_estimate=pl.CostEstimate(flops=20_000_000_000, bytes_accessed=1, transcendentals=0),
-        )(sunlit, field, east_courant, north_courant, mixing, *halos, *weights)
-        field, edges, weights = outs[0], outs[1:5], outs[5:]
-    return field
+        )(sunlit, field, east_courant, north_courant, mixing, *lon_halos, *lat_halos, *operands)
+        if not last:
+            field, lat_a, lat_b, *weights = outs
+    return outs[0]
 
 
 def solution(mesh):

time: 45.3 us -> 46 us (1.015)
  starting transfers between devices: 12.5 us -> 8.93 us
  Pallas kernels: 26.5 us -> 29.6 us
  waiting for transfers between devices: 6 us -> 6.96 us
    ppermute x8 -> x6, starting transfers between devices: 12.5 us -> 8.93 us  [swapped(): return lax.ppermute(array, axis, pairs + [(j, i) for i, j in pairs])]
    pallas_call x2, Pallas kernels: 23.4 us -> 25.6 us  [on_device(): pl.pallas_call(functools.partial(step_kernel, n_levels, n_rows, first, la...]
    ppermute x8 -> x6, waiting for transfers between devices: 6 us -> 6.96 us  [swapped(): return lax.ppermute(array, axis, pairs + [(j, i) for i, j in pairs])]
    pallas_call x1, Pallas kernels: 3.07 us -> 4 us  [on_device(): pl.pallas_call(first_kernel, out_shape=(column, column, edge, edge), in_s...]
  transfers between devices with their start and end apart: 8 -> 6, of which waited for: 3 -> 3; matrix products, arithmetic and copies ran while one was open for 0% -> 0% of each run, Pallas kernels for 0% -> 0%
where the time goes in v1:
time: 46 us; the launch traced here: 45.9 us
  Pallas kernels  29.6 us (64%)
  starting transfers between devices  8.93 us (19%)
  waiting for transfers between devices  6.96 us (15%)
    pallas_call x2, Pallas kernels, on_device(): pl.pallas_call(functools.partial(step_kernel, n_levels, n_rows, first, la...  25.6 us
    ppermute x6, starting transfers between devices, swapped(): return lax.ppermute(array, axis, pairs + [(j, i) for i, j in pairs])  8.93 us
    ppermute x6, waiting for transfers between devices, swapped(): return lax.ppermute(array, axis, pairs + [(j, i) for i, j in pairs])  6.96 us
    pallas_call x1, Pallas kernels, on_device(): pl.pallas_call(first_kernel, out_shape=(column, column, edge, edge), in_s...  4 us
  transfers between devices with their start and end apart: 6, of which 3 were waited for; matrix products, arithmetic and copies ran while one was open for 0% of the time, Pallas kernels for 0%

profile of v1, /device:TPU:0, one launch (start us, length us, event | category | flops | bytes accessed | tf_op | source)
XLA Modules:
  0.0 45.9 jit_solution(10739263638340047136)
XLA Ops:
  0.0 0.0 copy-start.12
  0.0 0.0 copy-start.6
  0.0 0.0 copy-start.5
  0.0 0.0 copy-start.4
  0.0 0.0 copy-start
  0.0 0.0 copy-start.11
  0.0 0.0 copy-start.10
  0.0 0.0 copy-start.3
  0.0 0.0 copy-start.2
  0.1 0.0 copy-start.1
  0.1 0.0 copy-start.9
  0.1 4.0 %first_sends.1 = (f32[80,128]{1,0:T(8,128)}, f32[80,128]{1,0:T(8,128)}, bf16[8,32,128]{2,1,0:T(8,128)(2,1)}, bf16[8,32,128]{2,1,0:T(8,128)(2,1)}) custom-call(s32[1,8]{1,0:T(1,128)} %sun.5, f32[32,8,16,128]{3,2,1,0:T(8,128)} %field.1, f32[8,16,128]{2,1,0:T(8,128)} %east_c.5, f32[8,16,128]{2,1,0:T(8,128)} %north_c.5, f32[7,16,128]{2,1,0:T(8,128)} %mixing.5), custom_call_target="tpu_custom_call" | custom-call | flops 4000000000 | bytes 2000000 | tf_op jit(solution)/shard_map/first_sends/pallas_call | solution.py:452
  4.1 0.5 %collective-permute-start.2 = (bf16[8,32,128]{2,1,0:T(8,128)(2,1)}, bf16[8,32,128]{2,1,0:T(8,128)(2,1)S(1)}, u32[]{:S(2)}, u32[]{:S(2)}) collective-permute-start(bf16[8,32,128]{2,1,0:T(8,128)(2,1)} %get-tuple-element.16), channel_id=1, source_target_pairs={{0,8},{16,24},{8,0},{24,16},{1,9},{17,25},{9,1},{25,17},{2,10},{18... | collective-permute-start | bytes 196616 | tf_op jit(solution)/shard_map/ppermute | solution.py:426
  4.6 2.6 %collective-permute-start.3 = (bf16[8,32,128]{2,1,0:T(8,128)(2,1)}, bf16[8,32,128]{2,1,0:T(8,128)(2,1)S(1)}, u32[]{:S(2)}, u32[]{:S(2)}) collective-permute-start(bf16[8,32,128]{2,1,0:T(8,128)(2,1)} %get-tuple-element.17), channel_id=1, source_target_pairs={{8,16},{24,0},{16,8},{0,24},{9,17},{25,1},{17,9},{1,25},{10,18},{2... | collective-permute-start | bytes 196616 | tf_op jit(solution)/shard_map/ppermute | solution.py:426
  7.2 1.5 %collective-permute-start = (f32[80,128]{1,0:T(8,128)}, f32[80,128]{1,0:T(8,128)S(1)}, u32[]{:S(2)}, u32[]{:S(2)}) collective-permute-start(f32[80,128]{1,0:T(8,128)} %get-tuple-element.14.refs_0_), channel_id=1, source_target_pairs={{0,1},{2,3},{4,5},{6,7},{1,0},{3,2},{5,4},{7,6},{8,9},{10,11},{12,... | collective-permute-start | bytes 122888 | tf_op jit(solution)/shard_map/ppermute | solution.py:426
  8.8 3.5 %collective-permute-start.1 = (f32[80,128]{1,0:T(8,128)}, f32[80,128]{1,0:T(8,128)S(1)}, u32[]{:S(2)}, u32[]{:S(2)}) collective-permute-start(f32[80,128]{1,0:T(8,128)} %get-tuple-element.15.refs_1_), channel_id=1, source_target_pairs={{1,2},{3,4},{5,6},{7,0},{2,1},{4,3},{6,5},{0,7},{9,10},{11,12},{13... | collective-permute-start | bytes 122888 | tf_op jit(solution)/shard_map/ppermute | solution.py:426
  12.3 0.0 collective-permute-done.lon_a_in
  12.3 3.4 %collective-permute-done.1.lon_b_in = f32[80,128]{1,0:T(8,128)S(1)} collective-permute-done((f32[80,128]{1,0:T(8,128)}, f32[80,128]{1,0:T(8,128)S(1)}, u32[]{:S(2)}, u32[]{:S(2)}) %collective-permute-start.1) | collective-permute-done | bytes 40992 | tf_op jit(solution)/shard_map/ppermute | solution.py:426
  15.7 0.0 collective-permute-done.2.lat_a_in
  15.7 0.0 collective-permute-done.3.lat_b_in
  15.7 0.0 copy-done.12
  15.7 0.0 copy-done.6
  15.7 0.0 copy-done.5
  15.7 0.0 copy-done.4
  15.7 0.0 copy-done
  15.7 0.0 copy-done.11
  15.7 0.0 copy-done.10
  15.7 0.0 copy-done.3
  15.7 0.0 copy-done.2
  15.8 0.0 copy-done.1
  15.8 0.0 copy-done.9
  15.8 0.0 copy-start.7
  15.8 0.0 copy-start.8
  15.8 11.3 %splitting_step.2 = (f32[8,16,32,128]{3,2,1,0:T(8,128)S(1)}, bf16[10,32,128]{2,1,0:T(8,128)(2,1)S(1)}, bf16[10,32,128]{2,1,0:T(8,128)(2,1)S(1)}, bf16[512,32]{1,0:T(8,128)(2,1)S(1)}, bf16[32,256]{1,0:T(8,128)(2,1)S(1)}) custom-call(s32[1,8]{1,0:T(1,128)S(1)} %copy-done.12, f32[32,8,16,128]{3,2,1,0:T(8,128)S(1)} %copy-done, f32[8,16,128]{2,1,0:T(8,128)S(1)} %copy-done.4, ...), custom_call_target="tpu_custom_call" | custom-call | flops 20000000000 | bytes 1 | tf_op jit(solution)/shard_map/splitting_step/pallas_call | solution.py:490
  27.1 0.1 collective-permute-start.4
  27.2 0.6 %collective-permute-start.5 = (bf16[10,32,128]{2,1,0:T(8,128)(2,1)S(1)}, bf16[10,32,128]{2,1,0:T(8,128)(2,1)S(1)}, u32[]{:S(2)}, u32[]{:S(2)}) collective-permute-start(bf16[10,32,128]{2,1,0:T(8,128)(2,1)S(1)} %get-tuple-element.20), channel_id=1, source_target_pairs={{8,16},{24,0},{16,8},{0,24},{9,17},{25,1},{17,9},{1,25},{10,18},{2... | collective-permute-start | bytes 245768 | tf_op jit(solution)/shard_map/ppermute | solution.py:426
  27.9 0.6 %collective-permute-done.4.lat_a_in = bf16[10,32,128]{2,1,0:T(8,128)(2,1)S(1)} collective-permute-done((bf16[10,32,128]{2,1,0:T(8,128)(2,1)S(1)}, bf16[10,32,128]{2,1,0:T(8,128)(2,1)S(1)}, u32[]{:S(2)}, u32[]{:S(2)}) %collective-permute-start.4) | collective-permute-done | bytes 81952 | tf_op jit(solution)/shard_map/ppermute | solution.py:426
  28.5 3.0 %collective-permute-done.5.lat_b_in = bf16[10,32,128]{2,1,0:T(8,128)(2,1)S(1)} collective-permute-done((bf16[10,32,128]{2,1,0:T(8,128)(2,1)S(1)}, bf16[10,32,128]{2,1,0:T(8,128)(2,1)S(1)}, u32[]{:S(2)}, u32[]{:S(2)}) %collective-permute-start.5) | collective-permute-done | bytes 81952 | tf_op jit(solution)/shard_map/ppermute | solution.py:426
  31.4 0.0 copy-done.7
  31.4 0.0 copy-done.8
  31.5 14.3 %splitting_step.3 = f32[32,8,16,128]{3,2,1,0:T(8,128)} custom-call(s32[1,8]{1,0:T(1,128)S(1)} %copy-done.12, f32[8,16,32,128]{3,2,1,0:T(8,128)S(1)} %get-tuple-element.18.field, f32[8,16,128]{2,1,0:T(8,128)S(1)} %copy-done.4, f32[8,16,128]{2,1,0:T(8,128)S(1)} %copy-done.5, f32[7,16,128]{2,1,0:T(8,128)S(1)} %copy-done.6, ...), custom_call_target="tpu_custom_call" | custom-call | flops 20000000000 | bytes 1 | tf_op jit(solution)/shard_map/splitting_step/pallas_call | solution.py:490
Async XLA Ops:
  0.0 15.7 %copy-start.12 = (s32[1,8]{1,0:T(1,128)S(1)}, s32[1,8]{1,0:T(1,128)}, u32[]{:S(2)}) copy-start(s32[1,8]{1,0:T(1,128)} %sun.5) | copy-start | bytes 100
  0.0 15.7 %copy-start.6 = (f32[7,16,128]{2,1,0:T(8,128)S(1)}, f32[7,16,128]{2,1,0:T(8,128)}, u32[]{:S(2)}) copy-start(f32[7,16,128]{2,1,0:T(8,128)} %mixing.5) | copy-start | bytes 172036
  0.0 15.7 %copy-start.5 = (f32[8,16,128]{2,1,0:T(8,128)S(1)}, f32[8,16,128]{2,1,0:T(8,128)}, u32[]{:S(2)}) copy-start(f32[8,16,128]{2,1,0:T(8,128)} %north_c.5) | copy-start | bytes 196612
  0.0 15.7 %copy-start.4 = (f32[8,16,128]{2,1,0:T(8,128)S(1)}, f32[8,16,128]{2,1,0:T(8,128)}, u32[]{:S(2)}) copy-start(f32[8,16,128]{2,1,0:T(8,128)} %east_c.5) | copy-start | bytes 196612
  0.0 15.7 %copy-start = (f32[32,8,16,128]{3,2,1,0:T(8,128)S(1)}, f32[32,8,16,128]{3,2,1,0:T(8,128)}, u32[]{:S(2)}) copy-start(f32[32,8,16,128]{3,2,1,0:T(8,128)} %field.1) | copy-start | bytes 6291460
  0.0 15.7 %copy-start.11 = (f32[256]{0:T(256)S(1)}, f32[256]{0:T(256)}, u32[]{:S(2)}) copy-start(f32[256]{0:T(256)} %param.21) | copy-start | bytes 3076
  0.0 15.7 %copy-start.10 = (bf16[32,224]{1,0:T(8,128)(2,1)S(1)}, bf16[32,224]{1,0:T(8,128)(2,1)}, u32[]{:S(2)}) copy-start(bf16[32,224]{1,0:T(8,128)(2,1)} %refs_4_.1) | copy-start | bytes 43012
  0.0 15.7 %copy-start.3 = (bf16[224,256]{1,0:T(8,128)(2,1)S(1)}, bf16[224,256]{1,0:T(8,128)(2,1)}, u32[]{:S(2)}) copy-start(bf16[224,256]{1,0:T(8,128)(2,1)} %refs_3_.1) | copy-start | bytes 344068
  0.0 15.7 %copy-start.2 = (bf16[256,224]{0,1:T(8,128)(2,1)S(1)}, bf16[256,224]{0,1:T(8,128)(2,1)}, u32[]{:S(2)}) copy-start(bf16[256,224]{0,1:T(8,128)(2,1)} %param.18) | copy-start | bytes 344068
  0.1 15.7 %copy-start.1 = (bf16[256,224]{0,1:T(8,128)(2,1)S(1)}, bf16[256,224]{0,1:T(8,128)(2,1)}, u32[]{:S(2)}) copy-start(bf16[256,224]{0,1:T(8,128)(2,1)} %param.17) | copy-start | bytes 344068
  0.1 15.7 %copy-start.9 = (bf16[224,32]{0,1:T(8,128)(2,1)S(1)}, bf16[224,32]{0,1:T(8,128)(2,1)}, u32[]{:S(2)}) copy-start(bf16[224,32]{0,1:T(8,128)(2,1)} %param.16) | copy-start | bytes 43012
  4.1 11.6 %collective-permute-start.2 = (bf16[8,32,128]{2,1,0:T(8,128)(2,1)}, bf16[8,32,128]{2,1,0:T(8,128)(2,1)S(1)}, u32[]{:S(2)}, u32[]{:S(2)}) collective-permute-start(bf16[8,32,128]{2,1,0:T(8,128)(2,1)} %get-tuple-element.16), channel_id=1, source_target_pairs={{0,8},{16,24},{8,0},{24,16},{1,9},{17,25},{9,1},{25,17},{2,10},{18... | collective-permute-start | bytes 196616 | tf_op jit(solution)/shard_map/ppermute | solution.py:426
  4.6 11.1 %collective-permute-start.3 = (bf16[8,32,128]{2,1,0:T(8,128)(2,1)}, bf16[8,32,128]{2,1,0:T(8,128)(2,1)S(1)}, u32[]{:S(2)}, u32[]{:S(2)}) collective-permute-start(bf16[8,32,128]{2,1,0:T(8,128)(2,1)} %get-tuple-element.17), channel_id=1, source_target_pairs={{8,16},{24,0},{16,8},{0,24},{9,17},{25,1},{17,9},{1,25},{10,18},{2... | collective-permute-start | bytes 196616 | tf_op jit(solution)/shard_map/ppermute | solution.py:426
  7.2 5.1 %collective-permute-start = (f32[80,128]{1,0:T(8,128)}, f32[80,128]{1,0:T(8,128)S(1)}, u32[]{:S(2)}, u32[]{:S(2)}) collective-permute-start(f32[80,128]{1,0:T(8,128)} %get-tuple-element.14.refs_0_), channel_id=1, source_target_pairs={{0,1},{2,3},{4,5},{6,7},{1,0},{3,2},{5,4},{7,6},{8,9},{10,11},{12,... | collective-permute-start | bytes 122888 | tf_op jit(solution)/shard_map/ppermute | solution.py:426
  8.8 6.9 %collective-permute-start.1 = (f32[80,128]{1,0:T(8,128)}, f32[80,128]{1,0:T(8,128)S(1)}, u32[]{:S(2)}, u32[]{:S(2)}) collective-permute-start(f32[80,128]{1,0:T(8,128)} %get-tuple-element.15.refs_1_), channel_id=1, source_target_pairs={{1,2},{3,4},{5,6},{7,0},{2,1},{4,3},{6,5},{0,7},{9,10},{11,12},{13... | collective-permute-start | bytes 122888 | tf_op jit(solution)/shard_map/ppermute | solution.py:426
  15.8 15.7 %copy-start.7 = (f32[80,128]{1,0:T(8,128)S(1)}, f32[80,128]{1,0:T(8,128)}, u32[]{:S(2)}) copy-start(f32[80,128]{1,0:T(8,128)} %get-tuple-element.14.refs_0_) | copy-start | bytes 122884
  15.8 15.7 %copy-start.8 = (f32[80,128]{1,0:T(8,128)S(1)}, f32[80,128]{1,0:T(8,128)}, u32[]{:S(2)}) copy-start(f32[80,128]{1,0:T(8,128)} %get-tuple-element.15.refs_1_) | copy-start | bytes 122884
  27.1 1.3 %collective-permute-start.4 = (bf16[10,32,128]{2,1,0:T(8,128)(2,1)S(1)}, bf16[10,32,128]{2,1,0:T(8,128)(2,1)S(1)}, u32[]{:S(2)}, u32[]{:S(2)}) collective-permute-start(bf16[10,32,128]{2,1,0:T(8,128)(2,1)S(1)} %get-tuple-element.19), channel_id=1, source_target_pairs={{0,8},{16,24},{8,0},{24,16},{1,9},{17,25},{9,1},{25,17},{2,10},{18... | collective-permute-start | bytes 245768 | tf_op jit(solution)/shard_map/ppermute | solution.py:426
  27.2 4.2 %collective-permute-start.5 = (bf16[10,32,128]{2,1,0:T(8,128)(2,1)S(1)}, bf16[10,32,128]{2,1,0:T(8,128)(2,1)S(1)}, u32[]{:S(2)}, u32[]{:S(2)}) collective-permute-start(bf16[10,32,128]{2,1,0:T(8,128)(2,1)S(1)} %get-tuple-element.20), channel_id=1, source_target_pairs={{8,16},{24,0},{16,8},{0,24},{9,17},{25,1},{17,9},{1,25},{10,18},{2... | collective-permute-start | bytes 245768 | tf_op jit(solution)/shard_map/ppermute | solution.py:426

commit v2 on v1

--- a/solution.py
+++ b/solution.py
@@ -81,8 +81,7 @@
         copy.start()
     for copy in copies:
         copy.wait()
-    turns = (0, 1, -2, -1)
-    columns = [jnp.zeros((COLUMN_ROWS, n_cols), F32) for _ in turns]
+    gathered = [jnp.zeros((COLUMN_ROWS, n_cols), F32) for _ in range(4)]
     for level in range(n_levels):
         levels[level].wait()
         extra = [east_v[level], north_v[level]]
@@ -94,25 +93,25 @@
         )
         for r in range(n_rows):
             at = level * n_rows + r
-            turned = pltpu.roll(tile[r], at, 1)
-            columns = [
-                jnp.where(lanes == (at + turn) % n_cols, turned, column)
-                for turn, column in zip(turns, columns)
-            ]
+            turned = pltpu.roll(tile[r], at // 4 * 4 + 2, 1)
+            gathered[at % 4] = jnp.where(lanes // 4 == at // 4, turned, gathered[at % 4])
         ends = []
         for r, closed, clip in ((0, is_first, jnp.minimum), (n_rows - 1, is_last, jnp.maximum)):
             speed = clip(north_v[level, r : r + 1, :], 0.0)
             ends.append((tile[r, :n_species] * jnp.where(closed, 0.0, speed)).astype(BF16))
         by_parity("lat", ends[1], ends[0], lat_a.at[level], lat_b.at[level])
-    columns = [
-        column if turn == 0 else pltpu.roll(column, -turn % n_cols, 1)
-        for turn, column in zip(turns, columns)
-    ]
+    columns = []
+    for slot in range(4):
+        column = gathered[0]
+        for place, part in enumerate(gathered):
+            part = pltpu.roll(part, (place - slot) % n_cols, 1) if place != slot else part
+            column = part if place == 0 else jnp.where(lanes % 4 == place, part, column)
+        columns.append(column)
     kinds = lax.broadcasted_iota(jnp.int32, (COLUMN_ROWS, n_cols), 0)
     lit_west = sun[0, 0].astype(F32)
     lit_east = sun[0, n_cols // BLOCK - 1].astype(F32)
-    west = [jnp.where(kinds == LIT_ROW, lit_west, columns[at]) for at in (0, 1)]
-    east = [jnp.where(kinds == LIT_ROW, lit_east, columns[at]) for at in (3, 2)]
+    west = [jnp.where(kinds == LIT_ROW, lit_west, columns[at]) for at in (2, 3)]
+    east = [jnp.where(kinds == LIT_ROW, lit_east, columns[at]) for at in (1, 0)]
     by_parity("lon", jnp.concatenate(east, axis=0), jnp.concatenate(west, axis=0), lon_a, lon_b)
 
 
@@ -128,10 +127,9 @@
     return column[:n_species] * clip(column[NORTH_ROW : NORTH_ROW + 1], 0.0)
 
 
-def diffused_column(column, west, east, south, north, n_species, n_levels, n_rows, ends):
+def moved_column(column, west, east, south, north, n_species, n_rows, ends):
     n_cols = column.shape[1]
-    lanes = lane_ids((1, n_cols))
-    levels, rows = lanes // n_rows, lanes % n_rows
+    rows = lane_ids((1, n_cols)) % n_rows
     is_first, is_last = ends
     speed = column[EAST_ROW : EAST_ROW + 1]
     lat_speed = column[NORTH_ROW : NORTH_ROW + 1]
@@ -141,23 +139,55 @@
     from_south = jnp.where(rows == 0, south, pltpu.roll(value * up, 1, 1))
     from_north = jnp.where(rows == n_rows - 1, north, pltpu.roll(value * down, n_cols - 1, 1))
     centre = 1.0 - jnp.abs(speed) - up + down
-    moved = value * centre + (west - east) + (from_south - from_north)
-    above = column[MIXING_ROW : MIXING_ROW + 1]
-    below = jnp.where(levels == 0, 0.0, pltpu.roll(above, n_rows, 1))
-    upper = jnp.zeros((1, n_cols), F32)
-    scale = upper
-    for level in range(n_levels):
-        pivot = 1.0 + below + above - below * pltpu.roll(upper, n_rows, 1)
-        scale = jnp.where(levels == level, 1.0 / pivot, scale)
-        upper = above * scale
-    solved = jnp.zeros_like(moved)
-    for level in range(n_levels):
-        swept = (moved + below * pltpu.roll(solved, n_rows, 1)) * scale
-        solved = jnp.where(levels == level, swept, solved)
-    for level in range(n_levels - 2, -1, -1):
-        swept = solved + upper * pltpu.roll(solved, n_cols - n_rows, 1)
-        solved = jnp.where(levels == level, swept, solved)
-    return solved
+    return value * centre + (west - east) + (from_south - from_north)
+
+
+def by_level(west, east, n_levels, n_rows):
+    n_cols = west.shape[1]
+    of_west = lane_ids((1, n_cols)) < n_rows
+    return [
+        jnp.where(
+            of_west,
+            pltpu.roll(west, (n_cols - level * n_rows) % n_cols, 1),
+            pltpu.roll(east, (n_cols - (level - 1) * n_rows) % n_cols, 1),
+        )
+        for level in range(n_levels)
+    ]
+
+
+def joined(levels, n_rows):
+    n_cols = levels[0].shape[1]
+    width = 2 * n_rows
+    lanes = lane_ids((1, n_cols))
+    arrays = []
+    for at, array in enumerate(levels):
+        turn = at * width % n_cols
+        if turn == 0:
+            arrays.append(array)
+        else:
+            arrays[-1] = jnp.where(lanes // width == turn // width, pltpu.roll(array, turn, 1), arrays[-1])
+    return arrays
+
+
+def diffused_columns(moved, mixing):
+    upper, swept = None, []
+    uppers = []
+    for level, value in enumerate(moved):
+        pivot = 1.0
+        if level > 0:
+            below = mixing[level - 1]
+            pivot = pivot + below - below * upper
+            value = value + below * swept[-1]
+        if level < len(moved) - 1:
+            pivot = pivot + mixing[level]
+        scale = 1.0 / pivot
+        if level < len(moved) - 1:
+            upper = mixing[level] * scale
+            uppers.append(upper)
+        swept.append(value * scale)
+    for level in range(len(moved) - 2, -1, -1):
+        swept[level] = swept[level] + uppers[level] * swept[level + 1]
+    return swept
 
 
 def step_kernel(
@@ -182,18 +212,18 @@
     else:
         (lon_a_own, lon_b_own, linear, encode), refs = refs[:4], refs[4:]
     half_rows = n_rows // 2
-    south_in, north_in, west_in, east_in, coefs, diffused = refs[-6:]
+    south_in, north_in, lon_in, coefs, diffused = refs[-5:]
     if last:
-        staged, sems = refs[-8:-6]
+        staged, sems = refs[-7:-5]
     by_parity("lat", lat_a_in[...], lat_b_in[...], north_in, south_in)
-    n_species, n_cols = west_in.shape
+    _, n_species, n_cols = lon_in.shape
     n_reactions = encode.shape[1]
     cells = n_levels * n_rows
     lanes = lane_ids((1, n_cols))
     row_ids = lax.broadcasted_iota(jnp.int32, (n_rows, n_cols), 0)
     is_first, is_last = at_ends()
     if first:
-        latent, field = field, refs[-7]
+        latent, field = field, refs[-6]
         fold_weights(*weights, linear, encode)
         for level in range(n_levels):
             field[level] = jnp.transpose(latent[:, level], (1, 0, 2))
@@ -241,16 +271,17 @@
         before, after = jnp.maximum(r - 1, 0), jnp.minimum(r + 1, n_rows - 1)
         right = None
         for level in range(n_levels):
-            at = level * n_rows + r
             value = field[level, r]
+            spot = level * 2 * n_rows % n_cols
+            halo = lon_in[level * 2 * n_rows // n_cols]
             from_west = jnp.where(
                 lanes == 0,
-                pltpu.roll(west_in[...], (n_cols - at) % n_cols, 1),
+                pltpu.roll(halo, (n_cols - spot - r) % n_cols, 1),
                 pltpu.roll(value * coef(EAST, level, r), 1, 1),
             )
             from_east = jnp.where(
                 lanes == n_cols - 1,
-                pltpu.roll(east_in[...], n_cols - 1 - at, 1),
+                pltpu.roll(halo, n_cols - 1 - spot - n_rows - r, 1),
                 pltpu.roll(value * coef(WEST, level, r), n_cols - 1, 1),
             )
             from_south = jnp.where(
@@ -281,37 +312,44 @@
         ]
         return jnp.concatenate(parts, axis=0).astype(BF16)
 
+    def levels_of(west, east):
+        return by_level(west, east, n_levels, n_rows)
+
+    def kind_of(kind):
+        return levels_of(west_near[kind : kind + 1], east_near[kind : kind + 1])
+
     if first:
-        west_in[...] = inflow(west_near, n_species, jnp.maximum)
-        east_in[...] = inflow(east_near, n_species, jnp.minimum)
+        halos = joined(
+            levels_of(
+                inflow(west_near, n_species, jnp.maximum), inflow(east_near, n_species, jnp.minimum)
+            ),
+            n_rows,
+        )
     else:
         own_west, _ = split_columns(jnp.where(even, lon_b_own[...], lon_a_own[...]))
         own_east, _ = split_columns(jnp.where(even, lon_a_own[...], lon_b_own[...]))
-        ends = is_first, is_last
 
         def corner(edge, at, turn):
             return pltpu.roll(edge[n_levels + at].astype(F32), turn, 1)
 
         def column_after(at, near, west, east):
-            return diffused_column(
+            return moved_column(
                 near,
                 inflow(west, n_species, jnp.maximum),
                 inflow(east, n_species, jnp.minimum),
                 corner(south_in, at, n_cols - (n_rows - 1)),
                 corner(north_in, at, n_rows - 1),
                 n_species,
-                n_levels,
                 n_rows,
-                ends,
+                (is_first, is_last),
             )
 
-        pair = jnp.concatenate(
-            [
-                column_after(0, west_near, west_far, own_west),
-                column_after(1, east_near, own_east, east_far),
-            ],
-            axis=1,
-        )
+        moved = levels_of(
+            column_after(0, west_near, west_far, own_west),
+            column_after(1, east_near, own_east, east_far),
+        )
+        pair = joined(diffused_columns(moved, kind_of(MIXING_ROW)), n_rows)
+        pair = jnp.concatenate(pair, axis=1)
         rounded = pair.astype(BF16)
         current, summed = rounded.astype(F32), None
         for substep in range(SUBSTEPS):
@@ -319,14 +357,16 @@
             summed = change if summed is None else summed + change
             current = current + change
             rounded = current.astype(BF16)
-        pair_lit = jnp.concatenate(
-            [near[LIT_ROW : LIT_ROW + 1] for near in (west_near, east_near)], axis=1
-        )
+        pair_lit = jnp.concatenate(joined(kind_of(LIT_ROW), n_rows), axis=1)
         pair = pair + jnp.where(pair_lit > 0.0, summed, 0.0)
-        west_speed = west_near[EAST_ROW : EAST_ROW + 1]
-        east_speed = east_near[EAST_ROW : EAST_ROW + 1]
-        west_in[...] = pair[:, :n_cols] * jnp.maximum(west_speed, 0.0)
-        east_in[...] = pair[:, n_cols:] * jnp.minimum(east_speed, 0.0)
+        halos = []
+        for at, speed in enumerate(joined(kind_of(EAST_ROW), n_rows)):
+            clipped = jnp.where(
+                lanes // n_rows % 2 == 0, jnp.maximum(speed, 0.0), jnp.minimum(speed, 0.0)
+            )
+            halos.append(pair[:, at * n_cols : (at + 1) * n_cols] * clipped)
+    for at, halo in enumerate(halos):
+        lon_in[at] = halo
 
     for r in range(ROWS_IN_FLIGHT):
         for _ in transport(r):
@@ -420,9 +460,9 @@
     return [pl.BlockSpec(memory_space=pltpu.VMEM)] * count
 
 
-def swapped(array, axis, first):
+def swapped(array, axis, first, closed=False):
     size = lax.axis_size(axis)
-    pairs = [(i % size, (i + 1) % size) for i in range(first, size + first, 2)]
+    pairs = [(i % size, (i + 1) % size) for i in range(first, size + first - closed, 2)]
     return lax.ppermute(array, axis, pairs + [(j, i) for i, j in pairs])
 
 
@@ -442,7 +482,6 @@
     n_species, n_levels, n_rows, n_cols = latent_field.shape
     layered = jax.ShapeDtypeStruct((n_levels, n_rows, n_species, n_cols), F32)
     column = jax.ShapeDtypeStruct((2 * COLUMN_ROWS, n_cols), F32)
-    side = jax.ShapeDtypeStruct((n_species, n_cols), F32)
     edge = jax.ShapeDtypeStruct((n_levels, n_species, n_cols), BF16)
     cornered = jax.ShapeDtypeStruct((n_levels + 2, n_species, n_cols), BF16)
     params = pltpu.CompilerParams(vmem_limit_bytes=VMEM_BYTES)
@@ -474,15 +513,16 @@
     field = latent_field
     for step in range(STEPS):
         first, last = step == 0, step == STEPS - 1
-        lat_halos = swapped(lat_a, "lat", 0), swapped(lat_b, "lat", 1)
+        lat_halos = swapped(lat_a, "lat", 0), swapped(lat_b, "lat", 1, closed=True)
         scratch = [pltpu.VMEM(layered.shape, F32)] if first else []
         if last:
             scratch += [
                 pltpu.VMEM((2, n_levels, n_species, n_rows // 2, n_cols), F32),
                 pltpu.SemaphoreType.DMA((2, n_levels)),
             ]
-        scratch += [pltpu.VMEM(array.shape, array.dtype) for array in (*lat_halos, side, side)]
+        scratch += [pltpu.VMEM(array.shape, array.dtype) for array in lat_halos]
         scratch += [
+            pltpu.VMEM((2 * n_levels * n_rows // n_cols, n_species, n_cols), F32),
             pltpu.VMEM((8, n_levels, n_rows, n_cols), F32),
             pltpu.VMEM((n_levels, n_rows + ROWS_IN_FLIGHT, n_species, n_cols), F32),
         ]

time: 46 us -> 44.8 us (0.974)
  Pallas kernels: 29.6 us -> 28.4 us
    pallas_call x2, Pallas kernels: 25.6 us -> 24.4 us  [on_device(): pl.pallas_call(functools.partial(step_kernel, n_levels, n_rows, first, la...]
where the time goes in v2:
time: 44.8 us; the launch traced here: 44.7 us
  Pallas kernels  28.4 us (63%)
  starting transfers between devices  8.93 us (20%)
  waiting for transfers between devices  6.95 us (16%)
    pallas_call x2, Pallas kernels, on_device(): pl.pallas_call(functools.partial(step_kernel, n_levels, n_rows, first, la...  24.4 us
    ppermute x6, starting transfers between devices, swapped(): return lax.ppermute(array, axis, pairs + [(j, i) for i, j in pairs])  8.93 us
    ppermute x6, waiting for transfers between devices, swapped(): return lax.ppermute(array, axis, pairs + [(j, i) for i, j in pairs])  6.95 us
    pallas_call x1, Pallas kernels, on_device(): pl.pallas_call(first_kernel, out_shape=(column, column, edge, edge), in_s...  4.04 us
  transfers between devices with their start and end apart: 6, of which 3 were waited for; matrix products, arithmetic and copies ran while one was open for 0% of the time, Pallas kernels for 0%

profile of v2, /device:TPU:0, one launch (start us, length us, event | category | flops | bytes accessed | tf_op | source)
XLA Modules:
  0.0 44.7 jit_solution(10814995627445833168)
XLA Ops:
  0.0 0.0 copy-start.12
  0.0 0.0 copy-start.6
  0.0 0.0 copy-start.5
  0.0 0.0 copy-start.4
  0.0 0.0 copy-start
  0.0 0.0 copy-start.11
  0.0 0.0 copy-start.10
  0.0 0.0 copy-start.3
  0.0 0.0 copy-start.2
  0.1 0.0 copy-start.1
  0.1 0.0 copy-start.9
  0.1 4.0 %first_sends.1 = (f32[80,128]{1,0:T(8,128)}, f32[80,128]{1,0:T(8,128)}, bf16[8,32,128]{2,1,0:T(8,128)(2,1)}, bf16[8,32,128]{2,1,0:T(8,128)(2,1)}) custom-call(s32[1,8]{1,0:T(1,128)} %sun.5, f32[32,8,16,128]{3,2,1,0:T(8,128)} %field.1, f32[8,16,128]{2,1,0:T(8,128)} %east_c.5, f32[8,16,128]{2,1,0:T(8,128)} %north_c.5, f32[7,16,128]{2,1,0:T(8,128)} %mixing.5), custom_call_target="tpu_custom_call" | custom-call | flops 4000000000 | bytes 2000000 | tf_op jit(solution)/shard_map/first_sends/pallas_call | solution.py:491
  4.1 0.5 %collective-permute-start.2 = (bf16[8,32,128]{2,1,0:T(8,128)(2,1)}, bf16[8,32,128]{2,1,0:T(8,128)(2,1)S(1)}, u32[]{:S(2)}, u32[]{:S(2)}) collective-permute-start(bf16[8,32,128]{2,1,0:T(8,128)(2,1)} %get-tuple-element.16), channel_id=1, source_target_pairs={{0,8},{16,24},{8,0},{24,16},{1,9},{17,25},{9,1},{25,17},{2,10},{18... | collective-permute-start | bytes 196616 | tf_op jit(solution)/shard_map/ppermute | solution.py:466
  4.7 2.6 %collective-permute-start.3 = (bf16[8,32,128]{2,1,0:T(8,128)(2,1)}, bf16[8,32,128]{2,1,0:T(8,128)(2,1)S(1)}, u32[]{:S(2)}, u32[]{:S(2)}) collective-permute-start(bf16[8,32,128]{2,1,0:T(8,128)(2,1)} %get-tuple-element.17), channel_id=1, source_target_pairs={{8,16},{24,0},{16,8},{0,24},{9,17},{25,1},{17,9},{1,25},{10,18},{2... | collective-permute-start | bytes 196616 | tf_op jit(solution)/shard_map/ppermute | solution.py:466
  7.3 1.5 %collective-permute-start = (f32[80,128]{1,0:T(8,128)}, f32[80,128]{1,0:T(8,128)S(1)}, u32[]{:S(2)}, u32[]{:S(2)}) collective-permute-start(f32[80,128]{1,0:T(8,128)} %get-tuple-element.14.refs_0_), channel_id=1, source_target_pairs={{0,1},{2,3},{4,5},{6,7},{1,0},{3,2},{5,4},{7,6},{8,9},{10,11},{12,... | collective-permute-start | bytes 122888 | tf_op jit(solution)/shard_map/ppermute | solution.py:466
  8.8 3.5 %collective-permute-start.1 = (f32[80,128]{1,0:T(8,128)}, f32[80,128]{1,0:T(8,128)S(1)}, u32[]{:S(2)}, u32[]{:S(2)}) collective-permute-start(f32[80,128]{1,0:T(8,128)} %get-tuple-element.15.refs_1_), channel_id=1, source_target_pairs={{1,2},{3,4},{5,6},{7,0},{2,1},{4,3},{6,5},{0,7},{9,10},{11,12},{13... | collective-permute-start | bytes 122888 | tf_op jit(solution)/shard_map/ppermute | solution.py:466
  12.3 0.0 collective-permute-done.lon_a_in
  12.3 3.4 %collective-permute-done.1.lon_b_in = f32[80,128]{1,0:T(8,128)S(1)} collective-permute-done((f32[80,128]{1,0:T(8,128)}, f32[80,128]{1,0:T(8,128)S(1)}, u32[]{:S(2)}, u32[]{:S(2)}) %collective-permute-start.1) | collective-permute-done | bytes 40992 | tf_op jit(solution)/shard_map/ppermute | solution.py:466
  15.7 0.0 collective-permute-done.2.lat_a_in
  15.7 0.0 collective-permute-done.3.lat_b_in
  15.7 0.0 copy-done.12
  15.7 0.0 copy-done.6
  15.7 0.0 copy-done.5
  15.7 0.0 copy-done.4
  15.7 0.0 copy-done
  15.8 0.0 copy-done.11
  15.8 0.0 copy-done.10
  15.8 0.0 copy-done.3
  15.8 0.0 copy-done.2
  15.8 0.0 copy-done.1
  15.8 0.0 copy-done.9
  15.8 0.0 copy-start.7
  15.8 0.0 copy-start.8
  15.8 11.5 %splitting_step.2 = (f32[8,16,32,128]{3,2,1,0:T(8,128)S(1)}, bf16[10,32,128]{2,1,0:T(8,128)(2,1)S(1)}, bf16[10,32,128]{2,1,0:T(8,128)(2,1)S(1)}, bf16[512,32]{1,0:T(8,128)(2,1)S(1)}, bf16[32,256]{1,0:T(8,128)(2,1)S(1)}) custom-call(s32[1,8]{1,0:T(1,128)S(1)} %copy-done.12, f32[32,8,16,128]{3,2,1,0:T(8,128)S(1)} %copy-done, f32[8,16,128]{2,1,0:T(8,128)S(1)} %copy-done.4, ...), custom_call_target="tpu_custom_call" | custom-call | flops 20000000000 | bytes 1 | tf_op jit(solution)/shard_map/splitting_step/pallas_call | solution.py:530
  27.3 0.1 collective-permute-start.4
  27.4 0.7 %collective-permute-start.5 = (bf16[10,32,128]{2,1,0:T(8,128)(2,1)S(1)}, bf16[10,32,128]{2,1,0:T(8,128)(2,1)S(1)}, u32[]{:S(2)}, u32[]{:S(2)}) collective-permute-start(bf16[10,32,128]{2,1,0:T(8,128)(2,1)S(1)} %get-tuple-element.20), channel_id=1, source_target_pairs={{8,16},{24,0},{16,8},{0,24},{9,17},{25,1},{17,9},{1,25},{10,18},{2... | collective-permute-start | bytes 245768 | tf_op jit(solution)/shard_map/ppermute | solution.py:466
  28.0 0.6 %collective-permute-done.4.lat_a_in = bf16[10,32,128]{2,1,0:T(8,128)(2,1)S(1)} collective-permute-done((bf16[10,32,128]{2,1,0:T(8,128)(2,1)S(1)}, bf16[10,32,128]{2,1,0:T(8,128)(2,1)S(1)}, u32[]{:S(2)}, u32[]{:S(2)}) %collective-permute-start.4) | collective-permute-done | bytes 81952 | tf_op jit(solution)/shard_map/ppermute | solution.py:466
  28.6 3.0 %collective-permute-done.5.lat_b_in = bf16[10,32,128]{2,1,0:T(8,128)(2,1)S(1)} collective-permute-done((bf16[10,32,128]{2,1,0:T(8,128)(2,1)S(1)}, bf16[10,32,128]{2,1,0:T(8,128)(2,1)S(1)}, u32[]{:S(2)}, u32[]{:S(2)}) %collective-permute-start.5) | collective-permute-done | bytes 81952 | tf_op jit(solution)/shard_map/ppermute | solution.py:466
  31.6 0.0 copy-done.7
  31.6 0.0 copy-done.8
  31.6 12.9 %splitting_step.3 = f32[32,8,16,128]{3,2,1,0:T(8,128)} custom-call(s32[1,8]{1,0:T(1,128)S(1)} %copy-done.12, f32[8,16,32,128]{3,2,1,0:T(8,128)S(1)} %get-tuple-element.18.field, f32[8,16,128]{2,1,0:T(8,128)S(1)} %copy-done.4, f32[8,16,128]{2,1,0:T(8,128)S(1)} %copy-done.5, f32[7,16,128]{2,1,0:T(8,128)S(1)} %copy-done.6, ...), custom_call_target="tpu_custom_call" | custom-call | flops 20000000000 | bytes 1 | tf_op jit(solution)/shard_map/splitting_step/pallas_call | solution.py:530
Async XLA Ops:
  0.0 15.7 %copy-start.12 = (s32[1,8]{1,0:T(1,128)S(1)}, s32[1,8]{1,0:T(1,128)}, u32[]{:S(2)}) copy-start(s32[1,8]{1,0:T(1,128)} %sun.5) | copy-start | bytes 100
  0.0 15.7 %copy-start.6 = (f32[7,16,128]{2,1,0:T(8,128)S(1)}, f32[7,16,128]{2,1,0:T(8,128)}, u32[]{:S(2)}) copy-start(f32[7,16,128]{2,1,0:T(8,128)} %mixing.5) | copy-start | bytes 172036
  0.0 15.7 %copy-start.5 = (f32[8,16,128]{2,1,0:T(8,128)S(1)}, f32[8,16,128]{2,1,0:T(8,128)}, u32[]{:S(2)}) copy-start(f32[8,16,128]{2,1,0:T(8,128)} %north_c.5) | copy-start | bytes 196612
  0.0 15.7 %copy-start.4 = (f32[8,16,128]{2,1,0:T(8,128)S(1)}, f32[8,16,128]{2,1,0:T(8,128)}, u32[]{:S(2)}) copy-start(f32[8,16,128]{2,1,0:T(8,128)} %east_c.5) | copy-start | bytes 196612
  0.0 15.7 %copy-start = (f32[32,8,16,128]{3,2,1,0:T(8,128)S(1)}, f32[32,8,16,128]{3,2,1,0:T(8,128)}, u32[]{:S(2)}) copy-start(f32[32,8,16,128]{3,2,1,0:T(8,128)} %field.1) | copy-start | bytes 6291460
  0.0 15.7 %copy-start.11 = (f32[256]{0:T(256)S(1)}, f32[256]{0:T(256)}, u32[]{:S(2)}) copy-start(f32[256]{0:T(256)} %param.21) | copy-start | bytes 3076
  0.0 15.7 %copy-start.10 = (bf16[32,224]{1,0:T(8,128)(2,1)S(1)}, bf16[32,224]{1,0:T(8,128)(2,1)}, u32[]{:S(2)}) copy-start(bf16[32,224]{1,0:T(8,128)(2,1)} %refs_4_.1) | copy-start | bytes 43012
  0.0 15.7 %copy-start.3 = (bf16[224,256]{1,0:T(8,128)(2,1)S(1)}, bf16[224,256]{1,0:T(8,128)(2,1)}, u32[]{:S(2)}) copy-start(bf16[224,256]{1,0:T(8,128)(2,1)} %refs_3_.1) | copy-start | bytes 344068
  0.0 15.7 %copy-start.2 = (bf16[256,224]{0,1:T(8,128)(2,1)S(1)}, bf16[256,224]{0,1:T(8,128)(2,1)}, u32[]{:S(2)}) copy-start(bf16[256,224]{0,1:T(8,128)(2,1)} %param.18) | copy-start | bytes 344068
  0.1 15.7 %copy-start.1 = (bf16[256,224]{0,1:T(8,128)(2,1)S(1)}, bf16[256,224]{0,1:T(8,128)(2,1)}, u32[]{:S(2)}) copy-start(bf16[256,224]{0,1:T(8,128)(2,1)} %param.17) | copy-start | bytes 344068
  0.1 15.7 %copy-start.9 = (bf16[224,32]{0,1:T(8,128)(2,1)S(1)}, bf16[224,32]{0,1:T(8,128)(2,1)}, u32[]{:S(2)}) copy-start(bf16[224,32]{0,1:T(8,128)(2,1)} %param.16) | copy-start | bytes 43012
  4.1 11.6 %collective-permute-start.2 = (bf16[8,32,128]{2,1,0:T(8,128)(2,1)}, bf16[8,32,128]{2,1,0:T(8,128)(2,1)S(1)}, u32[]{:S(2)}, u32[]{:S(2)}) collective-permute-start(bf16[8,32,128]{2,1,0:T(8,128)(2,1)} %get-tuple-element.16), channel_id=1, source_target_pairs={{0,8},{16,24},{8,0},{24,16},{1,9},{17,25},{9,1},{25,17},{2,10},{18... | collective-permute-start | bytes 196616 | tf_op jit(solution)/shard_map/ppermute | solution.py:466
  4.7 11.1 %collective-permute-start.3 = (bf16[8,32,128]{2,1,0:T(8,128)(2,1)}, bf16[8,32,128]{2,1,0:T(8,128)(2,1)S(1)}, u32[]{:S(2)}, u32[]{:S(2)}) collective-permute-start(bf16[8,32,128]{2,1,0:T(8,128)(2,1)} %get-tuple-element.17), channel_id=1, source_target_pairs={{8,16},{24,0},{16,8},{0,24},{9,17},{25,1},{17,9},{1,25},{10,18},{2... | collective-permute-start | bytes 196616 | tf_op jit(solution)/shard_map/ppermute | solution.py:466
  7.3 5.1 %collective-permute-start = (f32[80,128]{1,0:T(8,128)}, f32[80,128]{1,0:T(8,128)S(1)}, u32[]{:S(2)}, u32[]{:S(2)}) collective-permute-start(f32[80,128]{1,0:T(8,128)} %get-tuple-element.14.refs_0_), channel_id=1, source_target_pairs={{0,1},{2,3},{4,5},{6,7},{1,0},{3,2},{5,4},{7,6},{8,9},{10,11},{12,... | collective-permute-start | bytes 122888 | tf_op jit(solution)/shard_map/ppermute | solution.py:466
  8.8 6.9 %collective-permute-start.1 = (f32[80,128]{1,0:T(8,128)}, f32[80,128]{1,0:T(8,128)S(1)}, u32[]{:S(2)}, u32[]{:S(2)}) collective-permute-start(f32[80,128]{1,0:T(8,128)} %get-tuple-element.15.refs_1_), channel_id=1, source_target_pairs={{1,2},{3,4},{5,6},{7,0},{2,1},{4,3},{6,5},{0,7},{9,10},{11,12},{13... | collective-permute-start | bytes 122888 | tf_op jit(solution)/shard_map/ppermute | solution.py:466
  15.8 15.8 %copy-start.7 = (f32[80,128]{1,0:T(8,128)S(1)}, f32[80,128]{1,0:T(8,128)}, u32[]{:S(2)}) copy-start(f32[80,128]{1,0:T(8,128)} %get-tuple-element.14.refs_0_) | copy-start | bytes 122884
  15.8 15.8 %copy-start.8 = (f32[80,128]{1,0:T(8,128)S(1)}, f32[80,128]{1,0:T(8,128)}, u32[]{:S(2)}) copy-start(f32[80,128]{1,0:T(8,128)} %get-tuple-element.15.refs_1_) | copy-start | bytes 122884
  27.3 1.3 %collective-permute-start.4 = (bf16[10,32,128]{2,1,0:T(8,128)(2,1)S(1)}, bf16[10,32,128]{2,1,0:T(8,128)(2,1)S(1)}, u32[]{:S(2)}, u32[]{:S(2)}) collective-permute-start(bf16[10,32,128]{2,1,0:T(8,128)(2,1)S(1)} %get-tuple-element.19), channel_id=1, source_target_pairs={{0,8},{16,24},{8,0},{24,16},{1,9},{17,25},{9,1},{25,17},{2,10},{18... | collective-permute-start | bytes 245768 | tf_op jit(solution)/shard_map/ppermute | solution.py:466
  27.4 4.2 %collective-permute-start.5 = (bf16[10,32,128]{2,1,0:T(8,128)(2,1)S(1)}, bf16[10,32,128]{2,1,0:T(8,128)(2,1)S(1)}, u32[]{:S(2)}, u32[]{:S(2)}) collective-permute-start(bf16[10,32,128]{2,1,0:T(8,128)(2,1)S(1)} %get-tuple-element.20), channel_id=1, source_target_pairs={{8,16},{24,0},{16,8},{0,24},{9,17},{25,1},{17,9},{1,25},{10,18},{2... | collective-permute-start | bytes 245768 | tf_op jit(solution)/shard_map/ppermute | solution.py:466

commit v3 on v2

--- a/solution.py
+++ b/solution.py
@@ -63,7 +63,7 @@
 
 
 def first_kernel(sun, latent, east_c, north_c, mixing, lon_a, lon_b, lat_a, lat_b, *scratch):
-    tiles, east_v, north_v, mixing_v, sems = scratch
+    tiles, east_v, north_v, mixing_v, faces, turned_faces, sems = scratch
     n_levels, n_species, n_rows, n_cols = tiles.shape
     lanes = lane_ids((1, n_cols))
     is_first, is_last = at_ends()
@@ -81,32 +81,41 @@
         copy.start()
     for copy in copies:
         copy.wait()
-    gathered = [jnp.zeros((COLUMN_ROWS, n_cols), F32) for _ in range(4)]
+    def face_lanes(planes):
+        packed = None
+        for at, plane in enumerate(planes):
+            turned = pltpu.roll(plane, (4 * at + 2) % n_cols, 1)
+            packed = turned if packed is None else jnp.where(lanes // 4 == at, turned, packed)
+        return packed
+
     for level in range(n_levels):
         levels[level].wait()
-        extra = [east_v[level], north_v[level]]
+        within = slice(level * n_rows, (level + 1) * n_rows)
+        faces[0, within] = face_lanes([tiles[level, at] for at in range(n_species)])
+        planes = [east_v[level], north_v[level]]
         if level < n_levels - 1:
-            extra.append(mixing_v[level])
-        extra += [jnp.zeros((n_rows, n_cols), F32)] * (COLUMN_ROWS - n_species - len(extra))
-        tile = jnp.transpose(
-            jnp.concatenate([tiles[level]] + [plane[None] for plane in extra], axis=0), (1, 0, 2)
-        )
-        for r in range(n_rows):
-            at = level * n_rows + r
-            turned = pltpu.roll(tile[r], at // 4 * 4 + 2, 1)
-            gathered[at % 4] = jnp.where(lanes // 4 == at // 4, turned, gathered[at % 4])
+            planes.append(mixing_v[level])
+        zero = jnp.zeros((n_rows, n_cols), F32)
+        faces[1, within] = face_lanes(planes + [zero] * (COLUMN_ROWS - n_species - len(planes)))
+        rows = tiles.at[level].reshape(n_species * n_rows, n_cols)
         ends = []
         for r, closed, clip in ((0, is_first, jnp.minimum), (n_rows - 1, is_last, jnp.maximum)):
             speed = clip(north_v[level, r : r + 1, :], 0.0)
-            ends.append((tile[r, :n_species] * jnp.where(closed, 0.0, speed)).astype(BF16))
+            value = rows[pl.ds(r, n_species, stride=n_rows), :]
+            ends.append((value * jnp.where(closed, 0.0, speed)).astype(BF16))
         by_parity("lat", ends[1], ends[0], lat_a.at[level], lat_b.at[level])
-    columns = []
-    for slot in range(4):
-        column = gathered[0]
-        for place, part in enumerate(gathered):
-            part = pltpu.roll(part, (place - slot) % n_cols, 1) if place != slot else part
-            column = part if place == 0 else jnp.where(lanes % 4 == place, part, column)
-        columns.append(column)
+    turned_faces[0] = faces[0].T
+    turned_faces[1] = faces[1].T
+    columns = [
+        jnp.concatenate(
+            [
+                turned_faces[0, pl.ds(slot, n_species, stride=4), :],
+                turned_faces[1, pl.ds(slot, COLUMN_ROWS - n_species, stride=4), :],
+            ],
+            axis=0,
+        )
+        for slot in range(4)
+    ]
     kinds = lax.broadcasted_iota(jnp.int32, (COLUMN_ROWS, n_cols), 0)
     lit_west = sun[0, 0].astype(F32)
     lit_east = sun[0, n_cols // BLOCK - 1].astype(F32)
@@ -462,7 +471,7 @@
 
 def swapped(array, axis, first, closed=False):
     size = lax.axis_size(axis)
-    pairs = [(i % size, (i + 1) % size) for i in range(first, size + first - closed, 2)]
+    pairs = [(i % size, (i + 1) % size) for i in range(first, size + first - 2 * closed, 2)]
     return lax.ppermute(array, axis, pairs + [(j, i) for i, j in pairs])
 
 
@@ -498,6 +507,8 @@
             pltpu.VMEM(east_courant.shape, F32),
             pltpu.VMEM(north_courant.shape, F32),
             pltpu.VMEM(mixing.shape, F32),
+            pltpu.VMEM((2, n_levels * n_rows, n_cols), F32),
+            pltpu.VMEM((2, n_cols, n_levels * n_rows), F32),
             pltpu.SemaphoreType.DMA((n_levels + 3,)),
         ],
         compiler_params=pltpu.CompilerParams(vmem_limit_bytes=FIRST_VMEM_BYTES),

time: 44.8 us -> 46.5 us (1.038)
  the two profiles are of different devices: /device:TPU:0 before, /device:TPU:1 now
where the time goes in v3:
time: 46.5 us; the launch traced here: 46.3 us
  Pallas kernels  28.1 us (60%)
  starting transfers between devices  13.4 us (29%)
  waiting for transfers between devices  4.42 us (10%)
    pallas_call x2, Pallas kernels, on_device(): pl.pallas_call(functools.partial(step_kernel, n_levels, n_rows, first, la...  24.2 us
    ppermute x6, starting transfers between devices, swapped(): return lax.ppermute(array, axis, pairs + [(j, i) for i, j in pairs])  13.4 us
    ppermute x6, waiting for transfers between devices, swapped(): return lax.ppermute(array, axis, pairs + [(j, i) for i, j in pairs])  4.42 us
    pallas_call x1, Pallas kernels, on_device(): pl.pallas_call(first_kernel, out_shape=(column, column, edge, edge), in_s...  3.88 us
  transfers between devices with their start and end apart: 6, of which 2 were waited for; matrix products, arithmetic and copies ran while one was open for 0% of the time, Pallas kernels for 0%

profile of v3, /device:TPU:1, one launch (start us, length us, event | category | flops | bytes accessed | tf_op | source)
XLA Modules:
  0.0 46.3 jit_solution(3887426267213946373)
XLA Ops:
  0.0 0.0 copy-start.12
  0.0 0.0 copy-start.6
  0.0 0.0 copy-start.5
  0.0 0.0 copy-start.4
  0.0 0.0 copy-start
  0.0 0.0 copy-start.11
  0.0 0.0 copy-start.10
  0.0 0.0 copy-start.3
  0.1 0.0 copy-start.2
  0.1 0.0 copy-start.1
  0.1 0.0 copy-start.9
  0.1 3.9 %first_sends.1 = (f32[80,128]{1,0:T(8,128)}, f32[80,128]{1,0:T(8,128)}, bf16[8,32,128]{2,1,0:T(8,128)(2,1)}, bf16[8,32,128]{2,1,0:T(8,128)(2,1)}) custom-call(s32[1,8]{1,0:T(1,128)} %sun.5, f32[32,8,16,128]{3,2,1,0:T(8,128)} %field.1, f32[8,16,128]{2,1,0:T(8,128)} %east_c.5, f32[8,16,128]{2,1,0:T(8,128)} %north_c.5, f32[7,16,128]{2,1,0:T(8,128)} %mixing.5), custom_call_target="tpu_custom_call" | custom-call | flops 4000000000 | bytes 2000000 | tf_op jit(solution)/shard_map/first_sends/pallas_call | solution.py:500
  4.0 0.1 collective-permute-start.2
  4.1 4.5 %collective-permute-start.3 = (bf16[8,32,128]{2,1,0:T(8,128)(2,1)}, bf16[8,32,128]{2,1,0:T(8,128)(2,1)S(1)}, u32[]{:S(2)}, u32[]{:S(2)}) collective-permute-start(bf16[8,32,128]{2,1,0:T(8,128)(2,1)} %get-tuple-element.17), channel_id=1, source_target_pairs={{8,16},{16,8},{9,17},{17,9},{10,18},{18,10},{11,19},{19,11},{12,20... | collective-permute-start | bytes 196616 | tf_op jit(solution)/shard_map/ppermute | solution.py:475
  8.6 1.3 %collective-permute-start = (f32[80,128]{1,0:T(8,128)}, f32[80,128]{1,0:T(8,128)S(1)}, u32[]{:S(2)}, u32[]{:S(2)}) collective-permute-start(f32[80,128]{1,0:T(8,128)} %get-tuple-element.14.refs_0_), channel_id=1, source_target_pairs={{0,1},{2,3},{4,5},{6,7},{1,0},{3,2},{5,4},{7,6},{8,9},{10,11},{12,... | collective-permute-start | bytes 122888 | tf_op jit(solution)/shard_map/ppermute | solution.py:475
  9.9 3.3 %collective-permute-start.1 = (f32[80,128]{1,0:T(8,128)}, f32[80,128]{1,0:T(8,128)S(1)}, u32[]{:S(2)}, u32[]{:S(2)}) collective-permute-start(f32[80,128]{1,0:T(8,128)} %get-tuple-element.15.refs_1_), channel_id=1, source_target_pairs={{1,2},{3,4},{5,6},{7,0},{2,1},{4,3},{6,5},{0,7},{9,10},{11,12},{13... | collective-permute-start | bytes 122888 | tf_op jit(solution)/shard_map/ppermute | solution.py:475
  13.1 0.0 collective-permute-done.lon_a_in
  13.1 2.5 %collective-permute-done.1.lon_b_in = f32[80,128]{1,0:T(8,128)S(1)} collective-permute-done((f32[80,128]{1,0:T(8,128)}, f32[80,128]{1,0:T(8,128)S(1)}, u32[]{:S(2)}, u32[]{:S(2)}) %collective-permute-start.1) | collective-permute-done | bytes 40992 | tf_op jit(solution)/shard_map/ppermute | solution.py:475
  15.6 0.0 collective-permute-done.2.lat_a_in
  15.6 0.0 collective-permute-done.3.lat_b_in
  15.6 0.0 copy-done.12
  15.7 0.0 copy-done.6
  15.7 0.0 copy-done.5
  15.7 0.0 copy-done.4
  15.7 0.0 copy-done
  15.7 0.0 copy-done.11
  15.7 0.0 copy-done.10
  15.7 0.0 copy-done.3
  15.7 0.0 copy-done.2
  15.7 0.0 copy-done.1
  15.7 0.0 copy-done.9
  15.8 0.0 copy-start.7
  15.8 0.0 copy-start.8
  15.8 11.3 %splitting_step.2 = (f32[8,16,32,128]{3,2,1,0:T(8,128)S(1)}, bf16[10,32,128]{2,1,0:T(8,128)(2,1)S(1)}, bf16[10,32,128]{2,1,0:T(8,128)(2,1)S(1)}, bf16[512,32]{1,0:T(8,128)(2,1)S(1)}, bf16[32,256]{1,0:T(8,128)(2,1)S(1)}) custom-call(s32[1,8]{1,0:T(1,128)S(1)} %copy-done.12, f32[32,8,16,128]{3,2,1,0:T(8,128)S(1)} %copy-done, f32[8,16,128]{2,1,0:T(8,128)S(1)} %copy-done.4, ...), custom_call_target="tpu_custom_call" | custom-call | flops 20000000000 | bytes 1 | tf_op jit(solution)/shard_map/splitting_step/pallas_call | solution.py:541
  27.1 0.1 collective-permute-start.4
  27.2 4.1 %collective-permute-start.5 = (bf16[10,32,128]{2,1,0:T(8,128)(2,1)S(1)}, bf16[10,32,128]{2,1,0:T(8,128)(2,1)S(1)}, u32[]{:S(2)}, u32[]{:S(2)}) collective-permute-start(bf16[10,32,128]{2,1,0:T(8,128)(2,1)S(1)} %get-tuple-element.20), channel_id=1, source_target_pairs={{8,16},{16,8},{9,17},{17,9},{10,18},{18,10},{11,19},{19,11},{12,20... | collective-permute-start | bytes 245768 | tf_op jit(solution)/shard_map/ppermute | solution.py:475
  31.3 0.0 collective-permute-done.4.lat_a_in
  31.3 1.9 %collective-permute-done.5.lat_b_in = bf16[10,32,128]{2,1,0:T(8,128)(2,1)S(1)} collective-permute-done((bf16[10,32,128]{2,1,0:T(8,128)(2,1)S(1)}, bf16[10,32,128]{2,1,0:T(8,128)(2,1)S(1)}, u32[]{:S(2)}, u32[]{:S(2)}) %collective-permute-start.5) | collective-permute-done | bytes 81952 | tf_op jit(solution)/shard_map/ppermute | solution.py:475
  33.2 0.0 copy-done.7
  33.2 0.0 copy-done.8
  33.2 12.9 %splitting_step.3 = f32[32,8,16,128]{3,2,1,0:T(8,128)} custom-call(s32[1,8]{1,0:T(1,128)S(1)} %copy-done.12, f32[8,16,32,128]{3,2,1,0:T(8,128)S(1)} %get-tuple-element.18.field, f32[8,16,128]{2,1,0:T(8,128)S(1)} %copy-done.4, f32[8,16,128]{2,1,0:T(8,128)S(1)} %copy-done.5, f32[7,16,128]{2,1,0:T(8,128)S(1)} %copy-done.6, ...), custom_call_target="tpu_custom_call" | custom-call | flops 20000000000 | bytes 1 | tf_op jit(solution)/shard_map/splitting_step/pallas_call | solution.py:541
Async XLA Ops:
  0.0 15.6 %copy-start.12 = (s32[1,8]{1,0:T(1,128)S(1)}, s32[1,8]{1,0:T(1,128)}, u32[]{:S(2)}) copy-start(s32[1,8]{1,0:T(1,128)} %sun.5) | copy-start | bytes 100
  0.0 15.7 %copy-start.6 = (f32[7,16,128]{2,1,0:T(8,128)S(1)}, f32[7,16,128]{2,1,0:T(8,128)}, u32[]{:S(2)}) copy-start(f32[7,16,128]{2,1,0:T(8,128)} %mixing.5) | copy-start | bytes 172036
  0.0 15.7 %copy-start.5 = (f32[8,16,128]{2,1,0:T(8,128)S(1)}, f32[8,16,128]{2,1,0:T(8,128)}, u32[]{:S(2)}) copy-start(f32[8,16,128]{2,1,0:T(8,128)} %north_c.5) | copy-start | bytes 196612
  0.0 15.7 %copy-start.4 = (f32[8,16,128]{2,1,0:T(8,128)S(1)}, f32[8,16,128]{2,1,0:T(8,128)}, u32[]{:S(2)}) copy-start(f32[8,16,128]{2,1,0:T(8,128)} %east_c.5) | copy-start | bytes 196612
  0.0 15.7 %copy-start = (f32[32,8,16,128]{3,2,1,0:T(8,128)S(1)}, f32[32,8,16,128]{3,2,1,0:T(8,128)}, u32[]{:S(2)}) copy-start(f32[32,8,16,128]{3,2,1,0:T(8,128)} %field.1) | copy-start | bytes 6291460
  0.0 15.7 %copy-start.11 = (f32[256]{0:T(256)S(1)}, f32[256]{0:T(256)}, u32[]{:S(2)}) copy-start(f32[256]{0:T(256)} %param.21) | copy-start | bytes 3076
  0.0 15.7 %copy-start.10 = (bf16[32,224]{1,0:T(8,128)(2,1)S(1)}, bf16[32,224]{1,0:T(8,128)(2,1)}, u32[]{:S(2)}) copy-start(bf16[32,224]{1,0:T(8,128)(2,1)} %refs_4_.1) | copy-start | bytes 43012
  0.0 15.7 %copy-start.3 = (bf16[224,256]{1,0:T(8,128)(2,1)S(1)}, bf16[224,256]{1,0:T(8,128)(2,1)}, u32[]{:S(2)}) copy-start(bf16[224,256]{1,0:T(8,128)(2,1)} %refs_3_.1) | copy-start | bytes 344068
  0.1 15.7 %copy-start.2 = (bf16[256,224]{0,1:T(8,128)(2,1)S(1)}, bf16[256,224]{0,1:T(8,128)(2,1)}, u32[]{:S(2)}) copy-start(bf16[256,224]{0,1:T(8,128)(2,1)} %param.18) | copy-start | bytes 344068
  0.1 15.7 %copy-start.1 = (bf16[256,224]{0,1:T(8,128)(2,1)S(1)}, bf16[256,224]{0,1:T(8,128)(2,1)}, u32[]{:S(2)}) copy-start(bf16[256,224]{0,1:T(8,128)(2,1)} %param.17) | copy-start | bytes 344068
  0.1 15.7 %copy-start.9 = (bf16[224,32]{0,1:T(8,128)(2,1)S(1)}, bf16[224,32]{0,1:T(8,128)(2,1)}, u32[]{:S(2)}) copy-start(bf16[224,32]{0,1:T(8,128)(2,1)} %param.16) | copy-start | bytes 43012
  4.0 11.7 %collective-permute-start.2 = (bf16[8,32,128]{2,1,0:T(8,128)(2,1)}, bf16[8,32,128]{2,1,0:T(8,128)(2,1)S(1)}, u32[]{:S(2)}, u32[]{:S(2)}) collective-permute-start(bf16[8,32,128]{2,1,0:T(8,128)(2,1)} %get-tuple-element.16), channel_id=1, source_target_pairs={{0,8},{16,24},{8,0},{24,16},{1,9},{17,25},{9,1},{25,17},{2,10},{18... | collective-permute-start | bytes 196616 | tf_op jit(solution)/shard_map/ppermute | solution.py:475
  4.1 11.6 %collective-permute-start.3 = (bf16[8,32,128]{2,1,0:T(8,128)(2,1)}, bf16[8,32,128]{2,1,0:T(8,128)(2,1)S(1)}, u32[]{:S(2)}, u32[]{:S(2)}) collective-permute-start(bf16[8,32,128]{2,1,0:T(8,128)(2,1)} %get-tuple-element.17), channel_id=1, source_target_pairs={{8,16},{16,8},{9,17},{17,9},{10,18},{18,10},{11,19},{19,11},{12,20... | collective-permute-start | bytes 196616 | tf_op jit(solution)/shard_map/ppermute | solution.py:475
  8.6 4.6 %collective-permute-start = (f32[80,128]{1,0:T(8,128)}, f32[80,128]{1,0:T(8,128)S(1)}, u32[]{:S(2)}, u32[]{:S(2)}) collective-permute-start(f32[80,128]{1,0:T(8,128)} %get-tuple-element.14.refs_0_), channel_id=1, source_target_pairs={{0,1},{2,3},{4,5},{6,7},{1,0},{3,2},{5,4},{7,6},{8,9},{10,11},{12,... | collective-permute-start | bytes 122888 | tf_op jit(solution)/shard_map/ppermute | solution.py:475
  9.9 5.8 %collective-permute-start.1 = (f32[80,128]{1,0:T(8,128)}, f32[80,128]{1,0:T(8,128)S(1)}, u32[]{:S(2)}, u32[]{:S(2)}) collective-permute-start(f32[80,128]{1,0:T(8,128)} %get-tuple-element.15.refs_1_), channel_id=1, source_target_pairs={{1,2},{3,4},{5,6},{7,0},{2,1},{4,3},{6,5},{0,7},{9,10},{11,12},{13... | collective-permute-start | bytes 122888 | tf_op jit(solution)/shard_map/ppermute | solution.py:475
  15.8 17.5 %copy-start.7 = (f32[80,128]{1,0:T(8,128)S(1)}, f32[80,128]{1,0:T(8,128)}, u32[]{:S(2)}) copy-start(f32[80,128]{1,0:T(8,128)} %get-tuple-element.14.refs_0_) | copy-start | bytes 122884
  15.8 17.5 %copy-start.8 = (f32[80,128]{1,0:T(8,128)S(1)}, f32[80,128]{1,0:T(8,128)}, u32[]{:S(2)}) copy-start(f32[80,128]{1,0:T(8,128)} %get-tuple-element.15.refs_1_) | copy-start | bytes 122884
  27.1 4.2 %collective-permute-start.4 = (bf16[10,32,128]{2,1,0:T(8,128)(2,1)S(1)}, bf16[10,32,128]{2,1,0:T(8,128)(2,1)S(1)}, u32[]{:S(2)}, u32[]{:S(2)}) collective-permute-start(bf16[10,32,128]{2,1,0:T(8,128)(2,1)S(1)} %get-tuple-element.19), channel_id=1, source_target_pairs={{0,8},{16,24},{8,0},{24,16},{1,9},{17,25},{9,1},{25,17},{2,10},{18... | collective-permute-start | bytes 245768 | tf_op jit(solution)/shard_map/ppermute | solution.py:475
  27.2 6.1 %collective-permute-start.5 = (bf16[10,32,128]{2,1,0:T(8,128)(2,1)S(1)}, bf16[10,32,128]{2,1,0:T(8,128)(2,1)S(1)}, u32[]{:S(2)}, u32[]{:S(2)}) collective-permute-start(bf16[10,32,128]{2,1,0:T(8,128)(2,1)S(1)} %get-tuple-element.20), channel_id=1, source_target_pairs={{8,16},{16,8},{9,17},{17,9},{10,18},{18,10},{11,19},{19,11},{12,20... | collective-permute-start | bytes 245768 | tf_op jit(solution)/shard_map/ppermute | solution.py:475

commit v4 on v3

--- a/solution.py
+++ b/solution.py
@@ -12,7 +12,6 @@
 SUBSTEPS = 2
 STEPS = 2
 GROUP = 16
-ROWS_AT_ONCE = 8
 ROWS_IN_FLIGHT = 2
 LEVELS_AT_ONCE = 4
 LAG = 1
@@ -63,14 +62,14 @@
 
 
 def first_kernel(sun, latent, east_c, north_c, mixing, lon_a, lon_b, lat_a, lat_b, *scratch):
-    tiles, east_v, north_v, mixing_v, faces, turned_faces, sems = scratch
+    tiles, sun_v, east_v, north_v, mixing_v, faces, turned_faces, sems = scratch
     n_levels, n_species, n_rows, n_cols = tiles.shape
     lanes = lane_ids((1, n_cols))
     is_first, is_last = at_ends()
     copies = [
         pltpu.make_async_copy(source, held, sems.at[n_levels + at])
         for at, (source, held) in enumerate(
-            ((east_c, east_v), (north_c, north_v), (mixing, mixing_v))
+            ((sun, sun_v), (east_c, east_v), (north_c, north_v), (mixing, mixing_v))
         )
     ]
     levels = [
@@ -117,8 +116,8 @@
         for slot in range(4)
     ]
     kinds = lax.broadcasted_iota(jnp.int32, (COLUMN_ROWS, n_cols), 0)
-    lit_west = sun[0, 0].astype(F32)
-    lit_east = sun[0, n_cols // BLOCK - 1].astype(F32)
+    lit_west = sun_v[:, :1].astype(F32)
+    lit_east = sun_v[:, n_cols // BLOCK - 1 :].astype(F32)
     west = [jnp.where(kinds == LIT_ROW, lit_west, columns[at]) for at in (2, 3)]
     east = [jnp.where(kinds == LIT_ROW, lit_east, columns[at]) for at in (1, 0)]
     by_parity("lon", jnp.concatenate(east, axis=0), jnp.concatenate(west, axis=0), lon_a, lon_b)
@@ -234,8 +233,15 @@
     if first:
         latent, field = field, refs[-6]
         fold_weights(*weights, linear, encode)
-        for level in range(n_levels):
-            field[level] = jnp.transpose(latent[:, level], (1, 0, 2))
+
+        def gather(half):
+            within = slice(half * half_rows, (half + 1) * half_rows)
+            for level in range(n_levels):
+                field[level, within] = jnp.transpose(latent[:, level, within], (1, 0, 2))
+                yield
+
+        for _ in gather(0):
+            pass
     CENTRE, EAST, WEST, NORTH, SOUTH, SCALE, LOWER, UPPER = range(8)
 
     upper = None
@@ -269,15 +275,14 @@
 
     lit = jnp.zeros((1, n_cols), jnp.int32)
     for block in range(n_cols // BLOCK):
-        lit = jnp.where(lanes // BLOCK == block, sun[0, block], lit)
+        lit = jnp.where(lanes // BLOCK == block, sun[:, block : block + 1], lit)
     lit = lit > 0
 
     def coef(kind, level, r):
-        return coefs[kind, level, pl.ds(r, 1), :]
-
-    def transport(slot):
-        r = jnp.minimum(slot, n_rows - 1)
-        before, after = jnp.maximum(r - 1, 0), jnp.minimum(r + 1, n_rows - 1)
+        return coefs[kind, level, r : r + 1, :]
+
+    def transport(r):
+        before, after = max(r - 1, 0), min(r + 1, n_rows - 1)
         right = None
         for level in range(n_levels):
             value = field[level, r]
@@ -293,24 +298,22 @@
                 pltpu.roll(halo, n_cols - 1 - spot - n_rows - r, 1),
                 pltpu.roll(value * coef(WEST, level, r), n_cols - 1, 1),
             )
-            from_south = jnp.where(
-                r == 0,
-                south_in[level].astype(F32),
-                field[level, before] * coef(NORTH, level, before),
-            )
-            from_north = jnp.where(
-                r == n_rows - 1,
-                north_in[level].astype(F32),
-                field[level, after] * coef(SOUTH, level, after),
-            )
+            if r == 0:
+                from_south = south_in[level].astype(F32)
+            else:
+                from_south = field[level, before] * coef(NORTH, level, before)
+            if r == n_rows - 1:
+                from_north = north_in[level].astype(F32)
+            else:
+                from_north = field[level, after] * coef(SOUTH, level, after)
             moved = value * coef(CENTRE, level, r) + (from_west - from_east) + (from_south - from_north)
             scaled = moved * coef(SCALE, level, r)
             right = scaled if level == 0 else scaled + coef(LOWER, level, r) * right
-            diffused[level, slot] = right
+            diffused[level, r] = right
             yield
         for level in range(n_levels - 2, -1, -1):
-            right = diffused[level, slot] + coef(UPPER, level, r) * right
-            diffused[level, slot] = right
+            right = diffused[level, r] + coef(UPPER, level, r) * right
+            diffused[level, r] = right
             yield
 
     def product_of(rounded):
@@ -387,74 +390,68 @@
             [diffused[level + extra, r] for extra in range(LEVELS_AT_ONCE)], axis=1
         )
 
-    def rows(turn, carry):
-        units, ahead = [], {}
-        for first_row in range(0, ROWS_AT_ONCE, ROWS_IN_FLIGHT):
-            in_flight = [turn * ROWS_AT_ONCE + first_row + extra for extra in range(ROWS_IN_FLIGHT)]
-            places = [
-                (level, r) for r in in_flight for level in range(0, n_levels, LEVELS_AT_ONCE)
-            ]
-            steps = itertools.chain(*[transport(r + ROWS_IN_FLIGHT) for r in in_flight])
-            share = -(-(2 * n_levels - 1) * ROWS_IN_FLIGHT // (SUBSTEPS * len(places)))
-            for substep in range(SUBSTEPS):
-                for place in places:
-                    ahead[len(units)] = (steps, share)
-                    units.append((substep, place))
-        rounded, rates = {}, {}
-        for at in range(len(units) + LAG):
-            if at < len(units):
-                substep, (level, r) = units[at]
-                if substep == 0:
-                    rounded[at] = tile_at(level, r).astype(BF16)
-                rates[at] = product_of(rounded.pop(at))
-                steps, share = ahead[at]
-                for _ in itertools.islice(steps, share):
-                    pass
-            if at >= LAG:
-                done = at - LAG
-                substep, (level, r) = units[done]
-                change = jnp.dot(encode[...], rates.pop(done), preferred_element_type=F32)
-                tile = tile_at(level, r)
-                value = tile + jnp.where(lit_tile, change, 0.0)
-                if substep < SUBSTEPS - 1:
-                    later = done + ROWS_IN_FLIGHT * (n_levels // LEVELS_AT_ONCE)
-                    rounded[later] = (tile.astype(BF16).astype(F32) + change).astype(BF16)
-                for extra in range(LEVELS_AT_ONCE):
-                    part = value[:, extra * n_cols : (extra + 1) * n_cols]
-                    at_level = level + extra
-                    if last or substep < SUBSTEPS - 1:
-                        diffused[at_level, r] = part
-                    else:
-                        refs[0][at_level, r] = part
-        return carry
-
+    def send(half):
+        within = slice(half * half_rows, (half + 1) * half_rows)
+        for level in range(n_levels):
+            staged[half, level] = jnp.transpose(diffused[level, within], (1, 0, 2))
+            copy = pltpu.make_async_copy(
+                staged.at[half, level], refs[0].at[:, level, within], sems.at[half, level]
+            )
+            copy.start()
+            copies.append(copy)
+            yield
+
+    units, beside, copies = [], [], []
+    for first_row in range(0, n_rows, ROWS_IN_FLIGHT):
+        in_flight = range(first_row, first_row + ROWS_IN_FLIGHT)
+        places = [(level, r) for r in in_flight for level in range(0, n_levels, LEVELS_AT_ONCE)]
+        steps = itertools.chain(
+            *[transport(r + ROWS_IN_FLIGHT) for r in in_flight if r + ROWS_IN_FLIGHT < n_rows]
+        )
+        share = -(-(2 * n_levels - 1) * ROWS_IN_FLIGHT // (SUBSTEPS * len(places)))
+        for substep in range(SUBSTEPS):
+            for place in places:
+                beside.append((steps, share))
+                units.append((substep, place))
+    period = len(units) * ROWS_IN_FLIGHT // n_rows
+    passage, passage_from = iter(()), 0
+    if first:
+        passage = gather(1)
+    elif last:
+        passage, passage_from = send(0), len(units) // 2 + LAG + 1
+    rounded, rates = {}, {}
+    for at in range(len(units) + LAG):
+        if at < len(units):
+            substep, (level, r) = units[at]
+            if substep == 0:
+                rounded[at] = tile_at(level, r).astype(BF16)
+            rates[at] = product_of(rounded.pop(at))
+            if at >= passage_from:
+                next(passage, None)
+            for _ in itertools.islice(*beside[at]):
+                pass
+        if at >= LAG:
+            done = at - LAG
+            substep, (level, r) = units[done]
+            change = jnp.dot(encode[...], rates.pop(done), preferred_element_type=F32)
+            tile = tile_at(level, r)
+            value = tile + jnp.where(lit_tile, change, 0.0)
+            if substep < SUBSTEPS - 1:
+                later = done + period // SUBSTEPS
+                rounded[later] = (tile.astype(BF16).astype(F32) + change).astype(BF16)
+            for extra in range(LEVELS_AT_ONCE):
+                part = value[:, extra * n_cols : (extra + 1) * n_cols]
+                if last or substep < SUBSTEPS - 1:
+                    diffused[level + extra, r] = part
+                else:
+                    refs[0][level + extra, r] = part
     if last:
-
-        def sends(half):
-            within = pl.ds(pl.multiple_of(half * half_rows, half_rows), half_rows)
-            return [
-                pltpu.make_async_copy(
-                    staged.at[half, level], refs[0].at[:, level, within], sems.at[half, level]
-                )
-                for level in range(n_levels)
-            ]
-
-        def half_done(half, carry):
-            for turn in range(half_rows // ROWS_AT_ONCE):
-                rows(half * (half_rows // ROWS_AT_ONCE) + turn, None)
-            for level, copy in enumerate(sends(half)):
-                within = pl.ds(half * half_rows, half_rows)
-                staged[half, level] = jnp.transpose(diffused[level, within], (1, 0, 2))
-                copy.start()
-            return carry
-
-        lax.fori_loop(0, 2, half_done, 0)
-        for half in range(2):
-            for copy in sends(half):
-                copy.wait()
+        for _ in send(1):
+            pass
+        for copy in copies:
+            copy.wait()
         return
     out, lat_a, lat_b = refs[:3]
-    lax.fori_loop(0, n_rows // ROWS_AT_ONCE, rows, 0)
     for level in range(n_levels):
         south = (out[level, 0] * coefs[SOUTH, level, :1]).astype(BF16)
         north = (out[level, n_rows - 1] * coefs[NORTH, level, n_rows - 1 :]).astype(BF16)
@@ -472,7 +469,10 @@
 def swapped(array, axis, first, closed=False):
     size = lax.axis_size(axis)
     pairs = [(i % size, (i + 1) % size) for i in range(first, size + first - 2 * closed, 2)]
-    return lax.ppermute(array, axis, pairs + [(j, i) for i, j in pairs])
+    pairs += [(j, i) for i, j in pairs]
+    if closed:
+        pairs += [(0, 0), (size - 1, size - 1)]
+    return lax.ppermute(array, axis, pairs)
 
 
 def on_device(
@@ -494,22 +494,22 @@
     edge = jax.ShapeDtypeStruct((n_levels, n_species, n_cols), BF16)
     cornered = jax.ShapeDtypeStruct((n_levels + 2, n_species, n_cols), BF16)
     params = pltpu.CompilerParams(vmem_limit_bytes=VMEM_BYTES)
-    smem = pl.BlockSpec(memory_space=pltpu.SMEM)
     hbm = pl.BlockSpec(memory_space=pltpu.HBM)
     n_reactions = react_a.shape[0]
     lon_a, lon_b, lat_a, lat_b = pl.pallas_call(
         first_kernel,
         out_shape=(column, column, edge, edge),
-        in_specs=[smem] + [hbm] * 4,
+        in_specs=[hbm] * 5,
         out_specs=tuple(vmem(4)),
         scratch_shapes=[
             pltpu.VMEM((n_levels, n_species, n_rows, n_cols), F32),
+            pltpu.VMEM(sunlit.shape, sunlit.dtype),
             pltpu.VMEM(east_courant.shape, F32),
             pltpu.VMEM(north_courant.shape, F32),
             pltpu.VMEM(mixing.shape, F32),
             pltpu.VMEM((2, n_levels * n_rows, n_cols), F32),
             pltpu.VMEM((2, n_cols, n_levels * n_rows), F32),
-            pltpu.SemaphoreType.DMA((n_levels + 3,)),
+            pltpu.SemaphoreType.DMA((n_levels + 4,)),
         ],
         compiler_params=pltpu.CompilerParams(vmem_limit_bytes=FIRST_VMEM_BYTES),
         name="first_sends",
@@ -535,7 +535,7 @@
         scratch += [
             pltpu.VMEM((2 * n_levels * n_rows // n_cols, n_species, n_cols), F32),
             pltpu.VMEM((8, n_levels, n_rows, n_cols), F32),
-            pltpu.VMEM((n_levels, n_rows + ROWS_IN_FLIGHT, n_species, n_cols), F32),
+            pltpu.VMEM((n_levels, n_rows, n_species, n_cols), F32),
         ]
         operands = weights if first else (lon_a, lon_b, *weights)
         outs = pl.pallas_call(
@@ -543,7 +543,7 @@
             out_shape=(jax.ShapeDtypeStruct(latent_field.shape, F32),)
             if last
             else (layered, cornered, cornered, *folded),
-            in_specs=[smem] + vmem(8 + len(operands)),
+            in_specs=vmem(9 + len(operands)),
             out_specs=(hbm,) if last else tuple(vmem(5)),
             scratch_shapes=scratch,
             compiler_params=params,

time: 46.5 us -> 44.1 us (0.948)
  Pallas kernels: 28.1 us -> 25.7 us
    pallas_call x2, Pallas kernels: 24.2 us -> 22.5 us  [on_device(): pl.pallas_call(functools.partial(step_kernel, n_levels, n_rows, first, la...]
    pallas_call x1, Pallas kernels: 3.88 us -> 3.23 us  [on_device(): pl.pallas_call(first_kernel, out_shape=(column, column, edge, edge), in_s...]
where the time goes in v4:
time: 44.1 us; the launch traced here: 44 us
  Pallas kernels  25.7 us (58%)
  starting transfers between devices  13.4 us (30%)
  waiting for transfers between devices  4.42 us (10%)
    pallas_call x2, Pallas kernels, on_device(): pl.pallas_call(functools.partial(step_kernel, n_levels, n_rows, first, la...  22.5 us
    ppermute x6, starting transfers between devices, swapped(): return lax.ppermute(array, axis, pairs)  13.4 us
    ppermute x6, waiting for transfers between devices, swapped(): return lax.ppermute(array, axis, pairs)  4.42 us
    pallas_call x1, Pallas kernels, on_device(): pl.pallas_call(first_kernel, out_shape=(column, column, edge, edge), in_s...  3.23 us
  transfers between devices with their start and end apart: 6, of which 2 were waited for; matrix products, arithmetic and copies ran while one was open for 0% of the time, Pallas kernels for 0%

profile of v4, /device:TPU:1, one launch (start us, length us, event | category | flops | bytes accessed | tf_op | source)
XLA Modules:
  0.0 44.0 jit_solution(5386552605873502078)
XLA Ops:
  0.0 0.0 copy-start.12
  0.0 0.0 copy-start.6
  0.0 0.0 copy-start.5
  0.0 0.0 copy-start.4
  0.0 0.0 copy-start
  0.0 0.0 copy-start.11
  0.0 0.0 copy-start.10
  0.0 0.0 copy-start.3
  0.1 0.0 copy-start.2
  0.1 0.0 copy-start.1
  0.1 0.0 copy-start.9
  0.1 3.2 %first_sends.1 = (f32[80,128]{1,0:T(8,128)}, f32[80,128]{1,0:T(8,128)}, bf16[8,32,128]{2,1,0:T(8,128)(2,1)}, bf16[8,32,128]{2,1,0:T(8,128)(2,1)}) custom-call(s32[1,8]{1,0:T(1,128)} %sun.5, f32[32,8,16,128]{3,2,1,0:T(8,128)} %field.1, f32[8,16,128]{2,1,0:T(8,128)} %east_c.5, f32[8,16,128]{2,1,0:T(8,128)} %north_c.5, f32[7,16,128]{2,1,0:T(8,128)} %mixing.5), custom_call_target="tpu_custom_call" | custom-call | flops 4000000000 | bytes 2000000 | tf_op jit(solution)/shard_map/first_sends/pallas_call | solution.py:499
  3.3 0.1 collective-permute-start.2
  3.4 4.5 %collective-permute-start.3 = (bf16[8,32,128]{2,1,0:T(8,128)(2,1)}, bf16[8,32,128]{2,1,0:T(8,128)(2,1)S(1)}, u32[]{:S(2)}, u32[]{:S(2)}) collective-permute-start(bf16[8,32,128]{2,1,0:T(8,128)(2,1)} %get-tuple-element.17), channel_id=1, source_target_pairs={{8,16},{16,8},{0,0},{24,24},{9,17},{17,9},{1,1},{25,25},{10,18},{1... | collective-permute-start | bytes 196616 | tf_op jit(solution)/shard_map/ppermute | solution.py:475
  7.9 1.3 %collective-permute-start = (f32[80,128]{1,0:T(8,128)}, f32[80,128]{1,0:T(8,128)S(1)}, u32[]{:S(2)}, u32[]{:S(2)}) collective-permute-start(f32[80,128]{1,0:T(8,128)} %get-tuple-element.14.refs_0_), channel_id=1, source_target_pairs={{0,1},{2,3},{4,5},{6,7},{1,0},{3,2},{5,4},{7,6},{8,9},{10,11},{12,... | collective-permute-start | bytes 122888 | tf_op jit(solution)/shard_map/ppermute | solution.py:475
  9.2 3.3 %collective-permute-start.1 = (f32[80,128]{1,0:T(8,128)}, f32[80,128]{1,0:T(8,128)S(1)}, u32[]{:S(2)}, u32[]{:S(2)}) collective-permute-start(f32[80,128]{1,0:T(8,128)} %get-tuple-element.15.refs_1_), channel_id=1, source_target_pairs={{1,2},{3,4},{5,6},{7,0},{2,1},{4,3},{6,5},{0,7},{9,10},{11,12},{13... | collective-permute-start | bytes 122888 | tf_op jit(solution)/shard_map/ppermute | solution.py:475
  12.5 0.0 collective-permute-done.lon_a_in
  12.5 2.5 %collective-permute-done.1.lon_b_in = f32[80,128]{1,0:T(8,128)S(1)} collective-permute-done((f32[80,128]{1,0:T(8,128)}, f32[80,128]{1,0:T(8,128)S(1)}, u32[]{:S(2)}, u32[]{:S(2)}) %collective-permute-start.1) | collective-permute-done | bytes 40992 | tf_op jit(solution)/shard_map/ppermute | solution.py:475
  15.0 0.0 collective-permute-done.2.lat_a_in
  15.0 0.0 collective-permute-done.3.lat_b_in
  15.0 0.0 copy-done.12
  15.0 0.0 copy-done.6
  15.0 0.0 copy-done.5
  15.0 0.0 copy-done.4
  15.0 0.0 copy-done
  15.0 0.0 copy-done.11
  15.0 0.0 copy-done.10
  15.1 0.0 copy-done.3
  15.1 0.0 copy-done.2
  15.1 0.0 copy-done.1
  15.1 0.0 copy-done.9
  15.1 0.0 copy-start.7
  15.1 0.0 copy-start.8
  15.1 10.3 %splitting_step.2 = (f32[8,16,32,128]{3,2,1,0:T(8,128)S(1)}, bf16[10,32,128]{2,1,0:T(8,128)(2,1)S(1)}, bf16[10,32,128]{2,1,0:T(8,128)(2,1)S(1)}, bf16[512,32]{1,0:T(8,128)(2,1)S(1)}, bf16[32,256]{1,0:T(8,128)(2,1)S(1)}) custom-call(s32[1,8]{1,0:T(1,128)S(1)} %copy-done.12, f32[32,8,16,128]{3,2,1,0:T(8,128)S(1)} %copy-done, f32[8,16,128]{2,1,0:T(8,128)S(1)} %copy-done.4, ...), custom_call_target="tpu_custom_call" | custom-call | flops 20000000000 | bytes 1 | tf_op jit(solution)/shard_map/splitting_step/pallas_call | solution.py:541
  25.4 0.1 collective-permute-start.4
  25.5 4.1 %collective-permute-start.5 = (bf16[10,32,128]{2,1,0:T(8,128)(2,1)S(1)}, bf16[10,32,128]{2,1,0:T(8,128)(2,1)S(1)}, u32[]{:S(2)}, u32[]{:S(2)}) collective-permute-start(bf16[10,32,128]{2,1,0:T(8,128)(2,1)S(1)} %get-tuple-element.20), channel_id=1, source_target_pairs={{8,16},{16,8},{0,0},{24,24},{9,17},{17,9},{1,1},{25,25},{10,18},{1... | collective-permute-start | bytes 245768 | tf_op jit(solution)/shard_map/ppermute | solution.py:475
  29.6 0.0 collective-permute-done.4.lat_a_in
  29.6 1.9 %collective-permute-done.5.lat_b_in = bf16[10,32,128]{2,1,0:T(8,128)(2,1)S(1)} collective-permute-done((bf16[10,32,128]{2,1,0:T(8,128)(2,1)S(1)}, bf16[10,32,128]{2,1,0:T(8,128)(2,1)S(1)}, u32[]{:S(2)}, u32[]{:S(2)}) %collective-permute-start.5) | collective-permute-done | bytes 81952 | tf_op jit(solution)/shard_map/ppermute | solution.py:475
  31.6 0.0 copy-done.7
  31.6 0.0 copy-done.8
  31.6 12.2 %splitting_step.3 = f32[32,8,16,128]{3,2,1,0:T(8,128)} custom-call(s32[1,8]{1,0:T(1,128)S(1)} %copy-done.12, f32[8,16,32,128]{3,2,1,0:T(8,128)S(1)} %get-tuple-element.18.field, f32[8,16,128]{2,1,0:T(8,128)S(1)} %copy-done.4, f32[8,16,128]{2,1,0:T(8,128)S(1)} %copy-done.5, f32[7,16,128]{2,1,0:T(8,128)S(1)} %copy-done.6, ...), custom_call_target="tpu_custom_call" | custom-call | flops 20000000000 | bytes 1 | tf_op jit(solution)/shard_map/splitting_step/pallas_call | solution.py:541
Async XLA Ops:
  0.0 15.0 %copy-start.12 = (s32[1,8]{1,0:T(1,128)S(1)}, s32[1,8]{1,0:T(1,128)}, u32[]{:S(2)}) copy-start(s32[1,8]{1,0:T(1,128)} %sun.5) | copy-start | bytes 100
  0.0 15.0 %copy-start.6 = (f32[7,16,128]{2,1,0:T(8,128)S(1)}, f32[7,16,128]{2,1,0:T(8,128)}, u32[]{:S(2)}) copy-start(f32[7,16,128]{2,1,0:T(8,128)} %mixing.5) | copy-start | bytes 172036
  0.0 15.0 %copy-start.5 = (f32[8,16,128]{2,1,0:T(8,128)S(1)}, f32[8,16,128]{2,1,0:T(8,128)}, u32[]{:S(2)}) copy-start(f32[8,16,128]{2,1,0:T(8,128)} %north_c.5) | copy-start | bytes 196612
  0.0 15.0 %copy-start.4 = (f32[8,16,128]{2,1,0:T(8,128)S(1)}, f32[8,16,128]{2,1,0:T(8,128)}, u32[]{:S(2)}) copy-start(f32[8,16,128]{2,1,0:T(8,128)} %east_c.5) | copy-start | bytes 196612
  0.0 15.0 %copy-start = (f32[32,8,16,128]{3,2,1,0:T(8,128)S(1)}, f32[32,8,16,128]{3,2,1,0:T(8,128)}, u32[]{:S(2)}) copy-start(f32[32,8,16,128]{3,2,1,0:T(8,128)} %field.1) | copy-start | bytes 6291460
  0.0 15.0 %copy-start.11 = (f32[256]{0:T(256)S(1)}, f32[256]{0:T(256)}, u32[]{:S(2)}) copy-start(f32[256]{0:T(256)} %param.21) | copy-start | bytes 3076
  0.0 15.0 %copy-start.10 = (bf16[32,224]{1,0:T(8,128)(2,1)S(1)}, bf16[32,224]{1,0:T(8,128)(2,1)}, u32[]{:S(2)}) copy-start(bf16[32,224]{1,0:T(8,128)(2,1)} %refs_4_.1) | copy-start | bytes 43012
  0.0 15.0 %copy-start.3 = (bf16[224,256]{1,0:T(8,128)(2,1)S(1)}, bf16[224,256]{1,0:T(8,128)(2,1)}, u32[]{:S(2)}) copy-start(bf16[224,256]{1,0:T(8,128)(2,1)} %refs_3_.1) | copy-start | bytes 344068
  0.1 15.0 %copy-start.2 = (bf16[256,224]{0,1:T(8,128)(2,1)S(1)}, bf16[256,224]{0,1:T(8,128)(2,1)}, u32[]{:S(2)}) copy-start(bf16[256,224]{0,1:T(8,128)(2,1)} %param.18) | copy-start | bytes 344068
  0.1 15.0 %copy-start.1 = (bf16[256,224]{0,1:T(8,128)(2,1)S(1)}, bf16[256,224]{0,1:T(8,128)(2,1)}, u32[]{:S(2)}) copy-start(bf16[256,224]{0,1:T(8,128)(2,1)} %param.17) | copy-start | bytes 344068
  0.1 15.0 %copy-start.9 = (bf16[224,32]{0,1:T(8,128)(2,1)S(1)}, bf16[224,32]{0,1:T(8,128)(2,1)}, u32[]{:S(2)}) copy-start(bf16[224,32]{0,1:T(8,128)(2,1)} %param.16) | copy-start | bytes 43012
  3.3 11.7 %collective-permute-start.2 = (bf16[8,32,128]{2,1,0:T(8,128)(2,1)}, bf16[8,32,128]{2,1,0:T(8,128)(2,1)S(1)}, u32[]{:S(2)}, u32[]{:S(2)}) collective-permute-start(bf16[8,32,128]{2,1,0:T(8,128)(2,1)} %get-tuple-element.16), channel_id=1, source_target_pairs={{0,8},{16,24},{8,0},{24,16},{1,9},{17,25},{9,1},{25,17},{2,10},{18... | collective-permute-start | bytes 196616 | tf_op jit(solution)/shard_map/ppermute | solution.py:475
  3.4 11.6 %collective-permute-start.3 = (bf16[8,32,128]{2,1,0:T(8,128)(2,1)}, bf16[8,32,128]{2,1,0:T(8,128)(2,1)S(1)}, u32[]{:S(2)}, u32[]{:S(2)}) collective-permute-start(bf16[8,32,128]{2,1,0:T(8,128)(2,1)} %get-tuple-element.17), channel_id=1, source_target_pairs={{8,16},{16,8},{0,0},{24,24},{9,17},{17,9},{1,1},{25,25},{10,18},{1... | collective-permute-start | bytes 196616 | tf_op jit(solution)/shard_map/ppermute | solution.py:475
  7.9 4.6 %collective-permute-start = (f32[80,128]{1,0:T(8,128)}, f32[80,128]{1,0:T(8,128)S(1)}, u32[]{:S(2)}, u32[]{:S(2)}) collective-permute-start(f32[80,128]{1,0:T(8,128)} %get-tuple-element.14.refs_0_), channel_id=1, source_target_pairs={{0,1},{2,3},{4,5},{6,7},{1,0},{3,2},{5,4},{7,6},{8,9},{10,11},{12,... | collective-permute-start | bytes 122888 | tf_op jit(solution)/shard_map/ppermute | solution.py:475
  9.2 5.8 %collective-permute-start.1 = (f32[80,128]{1,0:T(8,128)}, f32[80,128]{1,0:T(8,128)S(1)}, u32[]{:S(2)}, u32[]{:S(2)}) collective-permute-start(f32[80,128]{1,0:T(8,128)} %get-tuple-element.15.refs_1_), channel_id=1, source_target_pairs={{1,2},{3,4},{5,6},{7,0},{2,1},{4,3},{6,5},{0,7},{9,10},{11,12},{13... | collective-permute-start | bytes 122888 | tf_op jit(solution)/shard_map/ppermute | solution.py:475
  15.1 16.5 %copy-start.7 = (f32[80,128]{1,0:T(8,128)S(1)}, f32[80,128]{1,0:T(8,128)}, u32[]{:S(2)}) copy-start(f32[80,128]{1,0:T(8,128)} %get-tuple-element.14.refs_0_) | copy-start | bytes 122884
  15.1 16.5 %copy-start.8 = (f32[80,128]{1,0:T(8,128)S(1)}, f32[80,128]{1,0:T(8,128)}, u32[]{:S(2)}) copy-start(f32[80,128]{1,0:T(8,128)} %get-tuple-element.15.refs_1_) | copy-start | bytes 122884
  25.4 4.2 %collective-permute-start.4 = (bf16[10,32,128]{2,1,0:T(8,128)(2,1)S(1)}, bf16[10,32,128]{2,1,0:T(8,128)(2,1)S(1)}, u32[]{:S(2)}, u32[]{:S(2)}) collective-permute-start(bf16[10,32,128]{2,1,0:T(8,128)(2,1)S(1)} %get-tuple-element.19), channel_id=1, source_target_pairs={{0,8},{16,24},{8,0},{24,16},{1,9},{17,25},{9,1},{25,17},{2,10},{18... | collective-permute-start | bytes 245768 | tf_op jit(solution)/shard_map/ppermute | solution.py:475
  25.5 6.1 %collective-permute-start.5 = (bf16[10,32,128]{2,1,0:T(8,128)(2,1)S(1)}, bf16[10,32,128]{2,1,0:T(8,128)(2,1)S(1)}, u32[]{:S(2)}, u32[]{:S(2)}) collective-permute-start(bf16[10,32,128]{2,1,0:T(8,128)(2,1)S(1)} %get-tuple-element.20), channel_id=1, source_target_pairs={{8,16},{16,8},{0,0},{24,24},{9,17},{17,9},{1,1},{25,25},{10,18},{1... | collective-permute-start | bytes 245768 | tf_op jit(solution)/shard_map/ppermute | solution.py:475

commit v5 on v4

--- a/solution.py
+++ b/solution.py
@@ -10,7 +10,6 @@
 
 BLOCK = 16
 SUBSTEPS = 2
-STEPS = 2
 GROUP = 16
 ROWS_IN_FLIGHT = 2
 LEVELS_AT_ONCE = 4
@@ -198,54 +197,18 @@
     return swept
 
 
-def step_kernel(
-    n_levels,
-    n_rows,
-    first,
-    last,
-    sun,
-    field,
-    east_c,
-    north_c,
-    mixing,
-    lon_a_in,
-    lon_b_in,
-    lat_a_in,
-    lat_b_in,
-    *refs,
-):
-    if first:
-        weights, refs = refs[:6], refs[6:]
-        linear, encode = refs[3:5]
-    else:
-        (lon_a_own, lon_b_own, linear, encode), refs = refs[:4], refs[4:]
-    half_rows = n_rows // 2
-    south_in, north_in, lon_in, coefs, diffused = refs[-5:]
-    if last:
-        staged, sems = refs[-7:-5]
-    by_parity("lat", lat_a_in[...], lat_b_in[...], north_in, south_in)
-    _, n_species, n_cols = lon_in.shape
-    n_reactions = encode.shape[1]
-    cells = n_levels * n_rows
-    lanes = lane_ids((1, n_cols))
+COEFFICIENTS = CENTRE, EAST, WEST, NORTH, SOUTH, SCALE, LOWER, UPPER = range(8)
+
+
+def prepare_kernel(latent, east_c, north_c, mixing, *refs):
+    weights, (field, coefs, linear, encode) = refs[:6], refs[6:]
+    n_levels, n_rows, _, n_cols = field.shape
+    fold_weights(*weights, linear, encode)
+    is_first, is_last = at_ends()
     row_ids = lax.broadcasted_iota(jnp.int32, (n_rows, n_cols), 0)
-    is_first, is_last = at_ends()
-    if first:
-        latent, field = field, refs[-6]
-        fold_weights(*weights, linear, encode)
-
-        def gather(half):
-            within = slice(half * half_rows, (half + 1) * half_rows)
-            for level in range(n_levels):
-                field[level, within] = jnp.transpose(latent[:, level, within], (1, 0, 2))
-                yield
-
-        for _ in gather(0):
-            pass
-    CENTRE, EAST, WEST, NORTH, SOUTH, SCALE, LOWER, UPPER = range(8)
-
     upper = None
     for level in range(n_levels):
+        field[level] = jnp.transpose(latent[:, level], (1, 0, 2))
         ce, cn = east_c[level], north_c[level]
         east, west = jnp.maximum(ce, 0.0), jnp.minimum(ce, 0.0)
         north = jnp.where((row_ids == n_rows - 1) & is_last, 0.0, jnp.maximum(cn, 0.0))
@@ -269,20 +232,33 @@
             upper = mixing[level] * scale
             coefs[UPPER, level] = upper
 
-    even = is_even("lon")
-    west_near, west_far = split_columns(jnp.where(even, lon_b_in[...], lon_a_in[...]))
-    east_near, east_far = split_columns(jnp.where(even, lon_a_in[...], lon_b_in[...]))
-
+
+def product_of(linear, rounded):
+    n_reactions = linear.shape[0] // 2
+    both = jnp.dot(linear[...], rounded, preferred_element_type=F32)
+    parts = [
+        both[at : at + GROUP] * both[at + GROUP : at + 2 * GROUP]
+        for at in range(0, 2 * n_reactions, 2 * GROUP)
+    ]
+    return jnp.concatenate(parts, axis=0).astype(BF16)
+
+
+def lit_lanes(sun, n_cols):
+    lanes = lane_ids((1, n_cols))
     lit = jnp.zeros((1, n_cols), jnp.int32)
     for block in range(n_cols // BLOCK):
         lit = jnp.where(lanes // BLOCK == block, sun[:, block : block + 1], lit)
-    lit = lit > 0
+    return lit > 0
+
+
+def step_rows(order, sun, field, coefs, linear, encode, lon_in, south_in, north_in, diffused, finish, passage=None):
+    n_levels, n_rows, _, n_cols = field.shape
+    lanes = lane_ids((1, n_cols))
 
     def coef(kind, level, r):
         return coefs[kind, level, r : r + 1, :]
 
     def transport(r):
-        before, after = max(r - 1, 0), min(r + 1, n_rows - 1)
         right = None
         for level in range(n_levels):
             value = field[level, r]
@@ -301,11 +277,11 @@
             if r == 0:
                 from_south = south_in[level].astype(F32)
             else:
-                from_south = field[level, before] * coef(NORTH, level, before)
+                from_south = field[level, r - 1] * coef(NORTH, level, r - 1)
             if r == n_rows - 1:
                 from_north = north_in[level].astype(F32)
             else:
-                from_north = field[level, after] * coef(SOUTH, level, after)
+                from_north = field[level, r + 1] * coef(SOUTH, level, r + 1)
             moved = value * coef(CENTRE, level, r) + (from_west - from_east) + (from_south - from_north)
             scaled = moved * coef(SCALE, level, r)
             right = scaled if level == 0 else scaled + coef(LOWER, level, r) * right
@@ -316,117 +292,35 @@
             diffused[level, r] = right
             yield
 
-    def product_of(rounded):
-        both = jnp.dot(linear[...], rounded, preferred_element_type=F32)
-        parts = [
-            both[at : at + GROUP] * both[at + GROUP : at + 2 * GROUP]
-            for at in range(0, 2 * n_reactions, 2 * GROUP)
-        ]
-        return jnp.concatenate(parts, axis=0).astype(BF16)
-
-    def levels_of(west, east):
-        return by_level(west, east, n_levels, n_rows)
-
-    def kind_of(kind):
-        return levels_of(west_near[kind : kind + 1], east_near[kind : kind + 1])
-
-    if first:
-        halos = joined(
-            levels_of(
-                inflow(west_near, n_species, jnp.maximum), inflow(east_near, n_species, jnp.minimum)
-            ),
-            n_rows,
-        )
-    else:
-        own_west, _ = split_columns(jnp.where(even, lon_b_own[...], lon_a_own[...]))
-        own_east, _ = split_columns(jnp.where(even, lon_a_own[...], lon_b_own[...]))
-
-        def corner(edge, at, turn):
-            return pltpu.roll(edge[n_levels + at].astype(F32), turn, 1)
-
-        def column_after(at, near, west, east):
-            return moved_column(
-                near,
-                inflow(west, n_species, jnp.maximum),
-                inflow(east, n_species, jnp.minimum),
-                corner(south_in, at, n_cols - (n_rows - 1)),
-                corner(north_in, at, n_rows - 1),
-                n_species,
-                n_rows,
-                (is_first, is_last),
-            )
-
-        moved = levels_of(
-            column_after(0, west_near, west_far, own_west),
-            column_after(1, east_near, own_east, east_far),
-        )
-        pair = joined(diffused_columns(moved, kind_of(MIXING_ROW)), n_rows)
-        pair = jnp.concatenate(pair, axis=1)
-        rounded = pair.astype(BF16)
-        current, summed = rounded.astype(F32), None
-        for substep in range(SUBSTEPS):
-            change = jnp.dot(encode[...], product_of(rounded), preferred_element_type=F32)
-            summed = change if summed is None else summed + change
-            current = current + change
-            rounded = current.astype(BF16)
-        pair_lit = jnp.concatenate(joined(kind_of(LIT_ROW), n_rows), axis=1)
-        pair = pair + jnp.where(pair_lit > 0.0, summed, 0.0)
-        halos = []
-        for at, speed in enumerate(joined(kind_of(EAST_ROW), n_rows)):
-            clipped = jnp.where(
-                lanes // n_rows % 2 == 0, jnp.maximum(speed, 0.0), jnp.minimum(speed, 0.0)
-            )
-            halos.append(pair[:, at * n_cols : (at + 1) * n_cols] * clipped)
-    for at, halo in enumerate(halos):
-        lon_in[at] = halo
-
-    for r in range(ROWS_IN_FLIGHT):
-        for _ in transport(r):
-            pass
-    lit_tile = jnp.concatenate([lit] * LEVELS_AT_ONCE, axis=1)
-
     def tile_at(level, r):
         return jnp.concatenate(
             [diffused[level + extra, r] for extra in range(LEVELS_AT_ONCE)], axis=1
         )
 
-    def send(half):
-        within = slice(half * half_rows, (half + 1) * half_rows)
-        for level in range(n_levels):
-            staged[half, level] = jnp.transpose(diffused[level, within], (1, 0, 2))
-            copy = pltpu.make_async_copy(
-                staged.at[half, level], refs[0].at[:, level, within], sems.at[half, level]
-            )
-            copy.start()
-            copies.append(copy)
-            yield
-
-    units, beside, copies = [], [], []
-    for first_row in range(0, n_rows, ROWS_IN_FLIGHT):
-        in_flight = range(first_row, first_row + ROWS_IN_FLIGHT)
+    lit_tile = jnp.concatenate([lit_lanes(sun, n_cols)] * LEVELS_AT_ONCE, axis=1)
+    for r in order[:ROWS_IN_FLIGHT]:
+        for _ in transport(r):
+            pass
+    units, beside = [], []
+    for first in range(0, len(order), ROWS_IN_FLIGHT):
+        in_flight = order[first : first + ROWS_IN_FLIGHT]
         places = [(level, r) for r in in_flight for level in range(0, n_levels, LEVELS_AT_ONCE)]
-        steps = itertools.chain(
-            *[transport(r + ROWS_IN_FLIGHT) for r in in_flight if r + ROWS_IN_FLIGHT < n_rows]
-        )
+        ahead = order[first + ROWS_IN_FLIGHT : first + 2 * ROWS_IN_FLIGHT]
+        steps = itertools.chain(*[transport(r) for r in ahead])
         share = -(-(2 * n_levels - 1) * ROWS_IN_FLIGHT // (SUBSTEPS * len(places)))
         for substep in range(SUBSTEPS):
             for place in places:
                 beside.append((steps, share))
                 units.append((substep, place))
-    period = len(units) * ROWS_IN_FLIGHT // n_rows
-    passage, passage_from = iter(()), 0
-    if first:
-        passage = gather(1)
-    elif last:
-        passage, passage_from = send(0), len(units) // 2 + LAG + 1
+    later_by = ROWS_IN_FLIGHT * (n_levels // LEVELS_AT_ONCE)
     rounded, rates = {}, {}
     for at in range(len(units) + LAG):
         if at < len(units):
             substep, (level, r) = units[at]
             if substep == 0:
                 rounded[at] = tile_at(level, r).astype(BF16)
-            rates[at] = product_of(rounded.pop(at))
-            if at >= passage_from:
+            rates[at] = product_of(linear, rounded.pop(at))
+            if passage is not None and at > len(units) // 2 + LAG:
                 next(passage, None)
             for _ in itertools.islice(*beside[at]):
                 pass
@@ -437,42 +331,165 @@
             tile = tile_at(level, r)
             value = tile + jnp.where(lit_tile, change, 0.0)
             if substep < SUBSTEPS - 1:
-                later = done + period // SUBSTEPS
-                rounded[later] = (tile.astype(BF16).astype(F32) + change).astype(BF16)
+                rounded[done + later_by] = (tile.astype(BF16).astype(F32) + change).astype(BF16)
             for extra in range(LEVELS_AT_ONCE):
                 part = value[:, extra * n_cols : (extra + 1) * n_cols]
-                if last or substep < SUBSTEPS - 1:
+                if substep < SUBSTEPS - 1:
                     diffused[level + extra, r] = part
                 else:
-                    refs[0][level + extra, r] = part
-    if last:
-        for _ in send(1):
-            pass
-        for copy in copies:
-            copy.wait()
-        return
-    out, lat_a, lat_b = refs[:3]
+                    finish(level + extra, r, part)
+
+
+def near_and_far(lon_b_in, lon_a_in):
+    even = is_even("lon")
+    west = split_columns(jnp.where(even, lon_b_in[...], lon_a_in[...]))
+    east = split_columns(jnp.where(even, lon_a_in[...], lon_b_in[...]))
+    return west, east
+
+
+def edge_rows_kernel(
+    sun, field, coefs, linear, encode, lat_b_in, lat_a_in, lon_b_in, lon_a_in,
+    done, lat_a, lat_b, lon_in, south_in, north_in, diffused,
+):
+    n_levels, n_rows, n_species, n_cols = field.shape
+    lanes = lane_ids((1, n_cols))
+    is_first, is_last = at_ends()
+    by_parity("lat", lat_a_in[...], lat_b_in[...], north_in, south_in)
+    (west_near, _), (east_near, _) = near_and_far(lon_b_in, lon_a_in)
+    halos = by_level(
+        inflow(west_near, n_species, jnp.maximum),
+        inflow(east_near, n_species, jnp.minimum),
+        n_levels,
+        n_rows,
+    )
+    for at, halo in enumerate(joined(halos, n_rows)):
+        lon_in[at] = halo
+    order = [0, n_rows - 1]
+
+    def finish(level, r, value):
+        done[level, order.index(r)] = value
+
+    step_rows(order, sun, field, coefs, linear, encode, lon_in, south_in, north_in, diffused, finish)
     for level in range(n_levels):
-        south = (out[level, 0] * coefs[SOUTH, level, :1]).astype(BF16)
-        north = (out[level, n_rows - 1] * coefs[NORTH, level, n_rows - 1 :]).astype(BF16)
+        south = (done[level, 0] * coefs[SOUTH, level, :1]).astype(BF16)
+        north = (done[level, 1] * coefs[NORTH, level, n_rows - 1 :]).astype(BF16)
         by_parity("lat", north, south, lat_a.at[level], lat_b.at[level])
-    for at, near in enumerate((west_near, east_near)):
-        south = jnp.where(is_first, 0.0, lat_inflow(near, n_species, jnp.minimum)).astype(BF16)
-        north = jnp.where(is_last, 0.0, lat_inflow(near, n_species, jnp.maximum)).astype(BF16)
-        by_parity("lat", north, south, lat_a.at[n_levels + at], lat_b.at[n_levels + at])
+    rows_of = lanes % n_rows
+    corners = []
+    for closed, clip, turn, row in (
+        (is_first, jnp.minimum, 1, 0),
+        (is_last, jnp.maximum, n_cols - 1, n_rows - 1),
+    ):
+        of_west = lat_inflow(west_near, n_species, clip)
+        of_east = pltpu.roll(lat_inflow(east_near, n_species, clip), turn, 1)
+        corners.append(jnp.where(closed, 0.0, jnp.where(rows_of == row, of_west, of_east)))
+    south, north = (value.astype(BF16) for value in corners)
+    by_parity("lat", north, south, lat_a.at[n_levels], lat_b.at[n_levels])
+
+
+def inner_rows_kernel(sun, field, coefs, linear, encode, done, lon_in, out, diffused):
+    n_levels, n_rows, _, _ = field.shape
+    for level in range(n_levels):
+        out[level, 0] = done[level, 0]
+        out[level, n_rows - 1] = done[level, 1]
+
+    def finish(level, r, value):
+        out[level, r] = value
+
+    order = list(range(1, n_rows - 1))
+    step_rows(order, sun, field, coefs, linear, encode, lon_in, None, None, diffused, finish)
+
+
+def last_step_kernel(
+    sun, field, coefs, linear, encode, lat_b_in, lat_a_in, lon_b_in, lon_a_in, lon_a_own, lon_b_own,
+    out, staged, sems, south_in, north_in, lon_in, diffused,
+):
+    n_levels, n_rows, n_species, n_cols = field.shape
+    half_rows = n_rows // 2
+    lanes = lane_ids((1, n_cols))
+    ends = at_ends()
+    by_parity("lat", lat_a_in[...], lat_b_in[...], north_in, south_in)
+    (west_near, west_far), (east_near, east_far) = near_and_far(lon_b_in, lon_a_in)
+    even = is_even("lon")
+    own_west, _ = split_columns(jnp.where(even, lon_b_own[...], lon_a_own[...]))
+    own_east, _ = split_columns(jnp.where(even, lon_a_own[...], lon_b_own[...]))
+
+    def levels_of(west, east):
+        return by_level(west, east, n_levels, n_rows)
+
+    def kind_of(kind):
+        return levels_of(west_near[kind : kind + 1], east_near[kind : kind + 1])
+
+    def corner(edge, at, turn):
+        shift = turn if at == 0 else (turn + (1 if turn > n_rows else n_cols - 1)) % n_cols
+        return pltpu.roll(edge[n_levels].astype(F32), shift, 1)
+
+    def column_after(at, near, west, east):
+        return moved_column(
+            near,
+            inflow(west, n_species, jnp.maximum),
+            inflow(east, n_species, jnp.minimum),
+            corner(south_in, at, n_cols - (n_rows - 1)),
+            corner(north_in, at, n_rows - 1),
+            n_species,
+            n_rows,
+            ends,
+        )
+
+    moved = levels_of(
+        column_after(0, west_near, west_far, own_west),
+        column_after(1, east_near, own_east, east_far),
+    )
+    pair = jnp.concatenate(joined(diffused_columns(moved, kind_of(MIXING_ROW)), n_rows), axis=1)
+    rounded = pair.astype(BF16)
+    current, summed = rounded.astype(F32), None
+    for substep in range(SUBSTEPS):
+        change = jnp.dot(encode[...], product_of(linear, rounded), preferred_element_type=F32)
+        summed = change if summed is None else summed + change
+        current = current + change
+        rounded = current.astype(BF16)
+    pair_lit = jnp.concatenate(joined(kind_of(LIT_ROW), n_rows), axis=1)
+    pair = pair + jnp.where(pair_lit > 0.0, summed, 0.0)
+    for at, speed in enumerate(joined(kind_of(EAST_ROW), n_rows)):
+        clipped = jnp.where(
+            lanes // n_rows % 2 == 0, jnp.maximum(speed, 0.0), jnp.minimum(speed, 0.0)
+        )
+        lon_in[at] = pair[:, at * n_cols : (at + 1) * n_cols] * clipped
+
+    copies = []
+
+    def send(half):
+        within = slice(half * half_rows, (half + 1) * half_rows)
+        for level in range(n_levels):
+            staged[half, level] = jnp.transpose(diffused[level, within], (1, 0, 2))
+            copy = pltpu.make_async_copy(
+                staged.at[half, level], out.at[:, level, within], sems.at[half, level]
+            )
+            copy.start()
+            copies.append(copy)
+            yield
+
+    def finish(level, r, value):
+        diffused[level, r] = value
+
+    step_rows(
+        list(range(n_rows)), sun, field, coefs, linear, encode, lon_in, south_in, north_in, diffused,
+        finish, send(0),
+    )
+    for _ in send(1):
+        pass
+    for copy in copies:
+        copy.wait()
 
 
 def vmem(count):
     return [pl.BlockSpec(memory_space=pltpu.VMEM)] * count
 
 
-def swapped(array, axis, first, closed=False):
+def swapped(array, axis, first):
     size = lax.axis_size(axis)
-    pairs = [(i % size, (i + 1) % size) for i in range(first, size + first - 2 * closed, 2)]
-    pairs += [(j, i) for i, j in pairs]
-    if closed:
-        pairs += [(0, 0), (size - 1, size - 1)]
-    return lax.ppermute(array, axis, pairs)
+    pairs = [(i % size, (i + 1) % size) for i in range(first, size + first, 2)]
+    return lax.ppermute(array, axis, pairs + [(j, i) for i, j in pairs])
 
 
 def on_device(
@@ -492,7 +509,7 @@
     layered = jax.ShapeDtypeStruct((n_levels, n_rows, n_species, n_cols), F32)
     column = jax.ShapeDtypeStruct((2 * COLUMN_ROWS, n_cols), F32)
     edge = jax.ShapeDtypeStruct((n_levels, n_species, n_cols), BF16)
-    cornered = jax.ShapeDtypeStruct((n_levels + 2, n_species, n_cols), BF16)
+    cornered = jax.ShapeDtypeStruct((n_levels + 1, n_species, n_cols), BF16)
     params = pltpu.CompilerParams(vmem_limit_bytes=VMEM_BYTES)
     hbm = pl.BlockSpec(memory_space=pltpu.HBM)
     n_reactions = react_a.shape[0]
@@ -516,43 +533,69 @@
         cost_estimate=pl.CostEstimate(flops=4_000_000_000, bytes_accessed=2_000_000, transcendentals=0),
     )(sunlit, latent_field, east_courant, north_courant, mixing)
     weights = (decode_w.T, react_a.T, react_b.T, stoich, encode_w, rate_const[None])
-    folded = (
-        jax.ShapeDtypeStruct((2 * n_reactions, n_species), BF16),
-        jax.ShapeDtypeStruct((n_species, n_reactions), BF16),
-    )
-    lon_halos = swapped(lon_a, "lon", 0), swapped(lon_b, "lon", 1)
-    field = latent_field
-    for step in range(STEPS):
-        first, last = step == 0, step == STEPS - 1
-        lat_halos = swapped(lat_a, "lat", 0), swapped(lat_b, "lat", 1, closed=True)
-        scratch = [pltpu.VMEM(layered.shape, F32)] if first else []
-        if last:
-            scratch += [
-                pltpu.VMEM((2, n_levels, n_species, n_rows // 2, n_cols), F32),
-                pltpu.SemaphoreType.DMA((2, n_levels)),
-            ]
-        scratch += [pltpu.VMEM(array.shape, array.dtype) for array in lat_halos]
-        scratch += [
-            pltpu.VMEM((2 * n_levels * n_rows // n_cols, n_species, n_cols), F32),
-            pltpu.VMEM((8, n_levels, n_rows, n_cols), F32),
-            pltpu.VMEM((n_levels, n_rows, n_species, n_cols), F32),
-        ]
-        operands = weights if first else (lon_a, lon_b, *weights)
-        outs = pl.pallas_call(
-            functools.partial(step_kernel, n_levels, n_rows, first, last),
-            out_shape=(jax.ShapeDtypeStruct(latent_field.shape, F32),)
-            if last
-            else (layered, cornered, cornered, *folded),
-            in_specs=vmem(9 + len(operands)),
-            out_specs=(hbm,) if last else tuple(vmem(5)),
-            scratch_shapes=scratch,
+    field, coefs, linear, encode = pl.pallas_call(
+        prepare_kernel,
+        out_shape=(
+            layered,
+            jax.ShapeDtypeStruct((len(COEFFICIENTS), n_levels, n_rows, n_cols), F32),
+            jax.ShapeDtypeStruct((2 * n_reactions, n_species), BF16),
+            jax.ShapeDtypeStruct((n_species, n_reactions), BF16),
+        ),
+        in_specs=vmem(4 + len(weights)),
+        out_specs=tuple(vmem(4)),
+        compiler_params=params,
+        name="prepare",
+        cost_estimate=pl.CostEstimate(flops=4_000_000_000, bytes_accessed=1, transcendentals=0),
+    )(latent_field, east_courant, north_courant, mixing, *weights)
+    lon_halos = swapped(lon_b, "lon", 1), swapped(lon_a, "lon", 0)
+    hint = pl.CostEstimate(flops=20_000_000_000, bytes_accessed=1, transcendentals=0)
+    halo = jax.ShapeDtypeStruct((2 * n_levels * n_rows // n_cols, n_species, n_cols), F32)
+
+    def call(kernel, name, operands, out_shape, out_specs, *scratch):
+        return pl.pallas_call(
+            kernel,
+            out_shape=out_shape,
+            in_specs=vmem(len(operands)),
+            out_specs=out_specs,
+            scratch_shapes=[
+                pltpu.VMEM(a.shape, a.dtype) if isinstance(a, jax.ShapeDtypeStruct) else a
+                for a in scratch
+            ],
             compiler_params=params,
-            name="splitting_step",
-            cost_estimate=pl.CostEstimate(flops=20_000_000_000, bytes_accessed=1, transcendentals=0),
-        )(sunlit, field, east_courant, north_courant, mixing, *lon_halos, *lat_halos, *operands)
-        if not last:
-            field, lat_a, lat_b, *weights = outs
-    return outs[0]
+            name=name,
+            cost_estimate=hint,
+        )(*operands)
+
+    lat_halos = swapped(lat_b, "lat", 1), swapped(lat_a, "lat", 0)
+    shared = sunlit, field, coefs, linear, encode
+    done, lat_a, lat_b, lon_in = call(
+        edge_rows_kernel,
+        "edge_rows",
+        (*shared, *lat_halos, *lon_halos),
+        (jax.ShapeDtypeStruct((n_levels, 2, n_species, n_cols), F32), cornered, cornered, halo),
+        tuple(vmem(4)),
+        edge,
+        edge,
+        layered,
+    )
+    lat_halos = swapped(lat_b, "lat", 1), swapped(lat_a, "lat", 0)
+    (field,) = call(
+        inner_rows_kernel, "inner_rows", (*shared, done, lon_in), (layered,), tuple(vmem(1)), layered
+    )
+    (advanced,) = call(
+        last_step_kernel,
+        "last_step",
+        (sunlit, field, coefs, linear, encode, *lat_halos, *lon_halos, lon_a, lon_b),
+        (jax.ShapeDtypeStruct(latent_field.shape, F32),),
+        (hbm,),
+        pltpu.VMEM((2, n_levels, n_species, n_rows // 2, n_cols), F32),
+        pltpu.SemaphoreType.DMA((2, n_levels)),
+        cornered,
+        cornered,
+        halo,
+        layered,
+    )
+    return advanced
 
 
 def solution(mesh):

time: 44.1 us -> 38.8 us (0.88)
  the two profiles are of different devices: /device:TPU:1 before, /device:TPU:0 now
where the time goes in v5:
time: 38.8 us; the launch traced here: 38.7 us
  Pallas kernels  26.9 us (69%)
  starting transfers between devices  9.14 us (24%)
  waiting for transfers between devices  2.22 us (6%)
    pallas_call x3, Pallas kernels, call(): pl.pallas_call(kernel, out_shape=out_shape, in_specs=vmem(len(operands)),...  23.1 us
    ppermute x6, starting transfers between devices, swapped(): return lax.ppermute(array, axis, pairs + [(j, i) for i, j in pairs])  9.14 us
    pallas_call x1, Pallas kernels, on_device(): pl.pallas_call(first_kernel, out_shape=(column, column, edge, edge), in_s...  3.23 us
    ppermute x6, waiting for transfers between devices, swapped(): return lax.ppermute(array, axis, pairs + [(j, i) for i, j in pairs])  2.22 us
  transfers between devices with their start and end apart: 6, of which 2 were waited for; matrix products, arithmetic and copies ran while one was open for 0% of the time, Pallas kernels for 25%

profile of v5, /device:TPU:0, one launch (start us, length us, event | category | flops | bytes accessed | tf_op | source)
XLA Modules:
  0.0 38.7 jit_solution(1216627259325828235)
XLA Ops:
  0.0 0.0 copy-start.6
  0.0 0.0 copy-start.5
  0.0 0.0 copy-start.4
  0.0 0.0 copy-start
  0.0 0.0 copy-start.11
  0.0 0.0 copy-start.10
  0.0 0.0 copy-start.3
  0.0 0.0 copy-start.2
  0.0 0.0 copy-start.1
  0.1 0.0 copy-start.9
  0.1 3.2 %first_sends.1 = (f32[80,128]{1,0:T(8,128)}, f32[80,128]{1,0:T(8,128)}, bf16[8,32,128]{2,1,0:T(8,128)(2,1)}, bf16[8,32,128]{2,1,0:T(8,128)(2,1)}) custom-call(s32[1,8]{1,0:T(1,128)} %sun.7, f32[32,8,16,128]{3,2,1,0:T(8,128)} %latent.3, f32[8,16,128]{2,1,0:T(8,128)} %east_c.3, f32[8,16,128]{2,1,0:T(8,128)} %north_c.3, f32[7,16,128]{2,1,0:T(8,128)} %mixing.3), custom_call_target="tpu_custom_call" | custom-call | flops 4000000000 | bytes 2000000 | tf_op jit(solution)/shard_map/first_sends/pallas_call | solution.py:516
  3.3 6.1 %collective-permute-start.2 = (f32[80,128]{1,0:T(8,128)}, f32[80,128]{1,0:T(8,128)S(1)}, u32[]{:S(2)}, u32[]{:S(2)}) collective-permute-start(f32[80,128]{1,0:T(8,128)} %get-tuple-element.23.lon_b_own), channel_id=1, source_target_pairs={{1,2},{3,4},{5,6},{7,0},{2,1},{4,3},{6,5},{0,7},{9,10},{11,12},{13... | collective-permute-start | bytes 122888 | tf_op jit(solution)/shard_map/ppermute | solution.py:492
  9.4 0.0 collective-permute-start.3
  9.4 0.7 %collective-permute-start = (bf16[8,32,128]{2,1,0:T(8,128)(2,1)}, bf16[8,32,128]{2,1,0:T(8,128)(2,1)S(1)}, u32[]{:S(2)}, u32[]{:S(2)}) collective-permute-start(bf16[8,32,128]{2,1,0:T(8,128)(2,1)} %get-tuple-element.21), channel_id=1, source_target_pairs={{8,16},{24,0},{16,8},{0,24},{9,17},{25,1},{17,9},{1,25},{10,18},{2... | collective-permute-start | bytes 196616 | tf_op jit(solution)/shard_map/ppermute | solution.py:492
  10.0 1.0 %collective-permute-start.1 = (bf16[8,32,128]{2,1,0:T(8,128)(2,1)}, bf16[8,32,128]{2,1,0:T(8,128)(2,1)S(1)}, u32[]{:S(2)}, u32[]{:S(2)}) collective-permute-start(bf16[8,32,128]{2,1,0:T(8,128)(2,1)} %get-tuple-element.22), channel_id=1, source_target_pairs={{0,8},{16,24},{8,0},{24,16},{1,9},{17,25},{9,1},{25,17},{2,10},{18... | collective-permute-start | bytes 196616 | tf_op jit(solution)/shard_map/ppermute | solution.py:492
  11.0 0.0 copy-done.6
  11.0 0.0 copy-done.5
  11.0 0.0 copy-done.4
  11.0 0.0 copy-done
  11.0 0.0 copy-done.11
  11.0 0.0 copy-done.10
  11.0 0.0 copy-done.3
  11.0 0.0 copy-done.2
  11.0 0.0 copy-done.1
  11.1 0.0 copy-done.9
  11.1 0.0 copy-start.12
  11.1 0.6 %prepare.1 = (f32[8,16,32,128]{3,2,1,0:T(8,128)S(1)}, f32[8,8,16,128]{3,2,1,0:T(8,128)S(1)}, bf16[512,32]{1,0:T(8,128)(2,1)S(1)}, bf16[32,256]{1,0:T(8,128)(2,1)S(1)}) custom-call(f32[32,8,16,128]{3,2,1,0:T(8,128)S(1)} %copy-done, f32[8,16,128]{2,1,0:T(8,128)S(1)} %copy-done.4, f32[8,16,128]{2,1,0:T(8,128)S(1)} %copy-done.5, f32[7,16,128]{2,1,0:T(8,128)S(1)} %copy-done.6, ...), custom_call_target="tpu_custom_call" | custom-call | flops 4000000000 | bytes 1 | tf_op jit(solution)/shard_map/prepare/pallas_call | solution.py:536
  11.7 0.0 collective-permute-done.2.lon_b_in
  11.7 1.9 %collective-permute-done.3.lon_a_in = f32[80,128]{1,0:T(8,128)S(1)} collective-permute-done((f32[80,128]{1,0:T(8,128)}, f32[80,128]{1,0:T(8,128)S(1)}, u32[]{:S(2)}, u32[]{:S(2)}) %collective-permute-start.3) | collective-permute-done | bytes 40992 | tf_op jit(solution)/shard_map/ppermute | solution.py:492
  13.6 0.3 collective-permute-done.lat_b_in
  13.9 0.0 collective-permute-done.1.lat_a_in
  14.0 0.0 copy-done.12
  14.0 1.8 %edge_rows.1 = (f32[8,2,32,128]{3,2,1,0:T(8,128)S(1)}, bf16[9,32,128]{2,1,0:T(8,128)(2,1)S(1)}, bf16[9,32,128]{2,1,0:T(8,128)(2,1)S(1)}, f32[2,32,128]{2,1,0:T(8,128)S(1)}) custom-call(s32[1,8]{1,0:T(1,128)S(1)} %copy-done.12, f32[8,16,32,128]{3,2,1,0:T(8,128)S(1)} %get-tuple-element.17.field, f32[8,8,16,128]{3,2,1,0:T(8,128)S(1)} %get-tuple-element.18.coefs, ...), custom_call_target="tpu_custom_call" | custom-call | flops 20000000000 | bytes 1 | tf_op jit(solution)/shard_map/edge_rows/pallas_call | solution.py:555
  15.7 0.8 %collective-permute-start.4 = (bf16[9,32,128]{2,1,0:T(8,128)(2,1)S(1)}, bf16[9,32,128]{2,1,0:T(8,128)(2,1)S(1)}, u32[]{:S(2)}, u32[]{:S(2)}) collective-permute-start(bf16[9,32,128]{2,1,0:T(8,128)(2,1)S(1)} %get-tuple-element.27), channel_id=1, source_target_pairs={{8,16},{24,0},{16,8},{0,24},{9,17},{25,1},{17,9},{1,25},{10,18},{2... | collective-permute-start | bytes 221192 | tf_op jit(solution)/shard_map/ppermute | solution.py:492
  16.5 0.7 %collective-permute-start.5 = (bf16[9,32,128]{2,1,0:T(8,128)(2,1)S(1)}, bf16[9,32,128]{2,1,0:T(8,128)(2,1)S(1)}, u32[]{:S(2)}, u32[]{:S(2)}) collective-permute-start(bf16[9,32,128]{2,1,0:T(8,128)(2,1)S(1)} %get-tuple-element.28), channel_id=1, source_target_pairs={{0,8},{16,24},{8,0},{24,16},{1,9},{17,25},{9,1},{25,17},{2,10},{18... | collective-permute-start | bytes 221192 | tf_op jit(solution)/shard_map/ppermute | solution.py:492
  17.2 0.0 copy-start.7
  17.2 0.0 copy-start.8
  17.2 9.1 %inner_rows.1.field = f32[8,16,32,128]{3,2,1,0:T(8,128)S(1)} custom-call(s32[1,8]{1,0:T(1,128)S(1)} %copy-done.12, f32[8,16,32,128]{3,2,1,0:T(8,128)S(1)} %get-tuple-element.17.field, f32[8,8,16,128]{3,2,1,0:T(8,128)S(1)} %get-tuple-element.18.coefs, bf16[512,32]{1,0:T(8,128)(2,1)S(1)} %get-tuple-element.19.linear, ...), custom_call_target="tpu_custom_call" | custom-call | flops 20000000000 | bytes 1 | tf_op jit(solution)/shard_map/inner_rows/pallas_call | solution.py:555
  26.3 0.0 collective-permute-done.4.lat_b_in
  26.3 0.0 collective-permute-done.5.lat_a_in
  26.3 0.0 copy-done.7
  26.3 0.0 copy-done.8
  26.3 12.2 %last_step.1 = f32[32,8,16,128]{3,2,1,0:T(8,128)} custom-call(s32[1,8]{1,0:T(1,128)S(1)} %copy-done.12, f32[8,16,32,128]{3,2,1,0:T(8,128)S(1)} %inner_rows.1.field, f32[8,8,16,128]{3,2,1,0:T(8,128)S(1)} %get-tuple-element.18.coefs, bf16[512,32]{1,0:T(8,128)(2,1)S(1)} %get-tuple-element.19.linear, bf16[32,256]{1,0:T(8,128)(2,1)S(1)} %get-tuple-element.20.encode, ...), custom_call_target="tpu_custom_call" | custom-call | flops 20000000000 | bytes 1 | tf_op jit(solution)/shard_map/last_step/pallas_call | solution.py:555
Async XLA Ops:
  0.0 11.0 %copy-start.6 = (f32[7,16,128]{2,1,0:T(8,128)S(1)}, f32[7,16,128]{2,1,0:T(8,128)}, u32[]{:S(2)}) copy-start(f32[7,16,128]{2,1,0:T(8,128)} %mixing.3) | copy-start | bytes 172036
  0.0 11.0 %copy-start.5 = (f32[8,16,128]{2,1,0:T(8,128)S(1)}, f32[8,16,128]{2,1,0:T(8,128)}, u32[]{:S(2)}) copy-start(f32[8,16,128]{2,1,0:T(8,128)} %north_c.3) | copy-start | bytes 196612
  0.0 11.0 %copy-start.4 = (f32[8,16,128]{2,1,0:T(8,128)S(1)}, f32[8,16,128]{2,1,0:T(8,128)}, u32[]{:S(2)}) copy-start(f32[8,16,128]{2,1,0:T(8,128)} %east_c.3) | copy-start | bytes 196612
  0.0 11.0 %copy-start = (f32[32,8,16,128]{3,2,1,0:T(8,128)S(1)}, f32[32,8,16,128]{3,2,1,0:T(8,128)}, u32[]{:S(2)}) copy-start(f32[32,8,16,128]{3,2,1,0:T(8,128)} %latent.3) | copy-start | bytes 6291460
  0.0 11.0 %copy-start.11 = (f32[256]{0:T(256)S(1)}, f32[256]{0:T(256)}, u32[]{:S(2)}) copy-start(f32[256]{0:T(256)} %param.21) | copy-start | bytes 3076
  0.0 11.0 %copy-start.10 = (bf16[32,224]{1,0:T(8,128)(2,1)S(1)}, bf16[32,224]{1,0:T(8,128)(2,1)}, u32[]{:S(2)}) copy-start(bf16[32,224]{1,0:T(8,128)(2,1)} %refs_4_.1) | copy-start | bytes 43012
  0.0 11.0 %copy-start.3 = (bf16[224,256]{1,0:T(8,128)(2,1)S(1)}, bf16[224,256]{1,0:T(8,128)(2,1)}, u32[]{:S(2)}) copy-start(bf16[224,256]{1,0:T(8,128)(2,1)} %refs_3_.1) | copy-start | bytes 344068
  0.0 11.0 %copy-start.2 = (bf16[256,224]{0,1:T(8,128)(2,1)S(1)}, bf16[256,224]{0,1:T(8,128)(2,1)}, u32[]{:S(2)}) copy-start(bf16[256,224]{0,1:T(8,128)(2,1)} %param.18) | copy-start | bytes 344068
  0.0 11.0 %copy-start.1 = (bf16[256,224]{0,1:T(8,128)(2,1)S(1)}, bf16[256,224]{0,1:T(8,128)(2,1)}, u32[]{:S(2)}) copy-start(bf16[256,224]{0,1:T(8,128)(2,1)} %param.17) | copy-start | bytes 344068
  0.1 11.0 %copy-start.9 = (bf16[224,32]{0,1:T(8,128)(2,1)S(1)}, bf16[224,32]{0,1:T(8,128)(2,1)}, u32[]{:S(2)}) copy-start(bf16[224,32]{0,1:T(8,128)(2,1)} %param.16) | copy-start | bytes 43012
  3.3 8.4 %collective-permute-start.2 = (f32[80,128]{1,0:T(8,128)}, f32[80,128]{1,0:T(8,128)S(1)}, u32[]{:S(2)}, u32[]{:S(2)}) collective-permute-start(f32[80,128]{1,0:T(8,128)} %get-tuple-element.23.lon_b_own), channel_id=1, source_target_pairs={{1,2},{3,4},{5,6},{7,0},{2,1},{4,3},{6,5},{0,7},{9,10},{11,12},{13... | collective-permute-start | bytes 122888 | tf_op jit(solution)/shard_map/ppermute | solution.py:492
  9.4 4.2 %collective-permute-start.3 = (f32[80,128]{1,0:T(8,128)}, f32[80,128]{1,0:T(8,128)S(1)}, u32[]{:S(2)}, u32[]{:S(2)}) collective-permute-start(f32[80,128]{1,0:T(8,128)} %get-tuple-element.24.lon_a_own), channel_id=1, source_target_pairs={{0,1},{2,3},{4,5},{6,7},{1,0},{3,2},{5,4},{7,6},{8,9},{10,11},{12,... | collective-permute-start | bytes 122888 | tf_op jit(solution)/shard_map/ppermute | solution.py:492
  9.4 4.6 %collective-permute-start = (bf16[8,32,128]{2,1,0:T(8,128)(2,1)}, bf16[8,32,128]{2,1,0:T(8,128)(2,1)S(1)}, u32[]{:S(2)}, u32[]{:S(2)}) collective-permute-start(bf16[8,32,128]{2,1,0:T(8,128)(2,1)} %get-tuple-element.21), channel_id=1, source_target_pairs={{8,16},{24,0},{16,8},{0,24},{9,17},{25,1},{17,9},{1,25},{10,18},{2... | collective-permute-start | bytes 196616 | tf_op jit(solution)/shard_map/ppermute | solution.py:492
  10.0 3.9 %collective-permute-start.1 = (bf16[8,32,128]{2,1,0:T(8,128)(2,1)}, bf16[8,32,128]{2,1,0:T(8,128)(2,1)S(1)}, u32[]{:S(2)}, u32[]{:S(2)}) collective-permute-start(bf16[8,32,128]{2,1,0:T(8,128)(2,1)} %get-tuple-element.22), channel_id=1, source_target_pairs={{0,8},{16,24},{8,0},{24,16},{1,9},{17,25},{9,1},{25,17},{2,10},{18... | collective-permute-start | bytes 196616 | tf_op jit(solution)/shard_map/ppermute | solution.py:492
  11.1 2.9 %copy-start.12 = (s32[1,8]{1,0:T(1,128)S(1)}, s32[1,8]{1,0:T(1,128)}, u32[]{:S(2)}) copy-start(s32[1,8]{1,0:T(1,128)} %sun.7) | copy-start | bytes 100
  15.7 10.5 %collective-permute-start.4 = (bf16[9,32,128]{2,1,0:T(8,128)(2,1)S(1)}, bf16[9,32,128]{2,1,0:T(8,128)(2,1)S(1)}, u32[]{:S(2)}, u32[]{:S(2)}) collective-permute-start(bf16[9,32,128]{2,1,0:T(8,128)(2,1)S(1)} %get-tuple-element.27), channel_id=1, source_target_pairs={{8,16},{24,0},{16,8},{0,24},{9,17},{25,1},{17,9},{1,25},{10,18},{2... | collective-permute-start | bytes 221192 | tf_op jit(solution)/shard_map/ppermute | solution.py:492
  16.5 9.8 %collective-permute-start.5 = (bf16[9,32,128]{2,1,0:T(8,128)(2,1)S(1)}, bf16[9,32,128]{2,1,0:T(8,128)(2,1)S(1)}, u32[]{:S(2)}, u32[]{:S(2)}) collective-permute-start(bf16[9,32,128]{2,1,0:T(8,128)(2,1)S(1)} %get-tuple-element.28), channel_id=1, source_target_pairs={{0,8},{16,24},{8,0},{24,16},{1,9},{17,25},{9,1},{25,17},{2,10},{18... | collective-permute-start | bytes 221192 | tf_op jit(solution)/shard_map/ppermute | solution.py:492
  17.2 9.1 %copy-start.7 = (f32[80,128]{1,0:T(8,128)S(1)}, f32[80,128]{1,0:T(8,128)}, u32[]{:S(2)}) copy-start(f32[80,128]{1,0:T(8,128)} %get-tuple-element.24.lon_a_own) | copy-start | bytes 122884
  17.2 9.1 %copy-start.8 = (f32[80,128]{1,0:T(8,128)S(1)}, f32[80,128]{1,0:T(8,128)}, u32[]{:S(2)}) copy-start(f32[80,128]{1,0:T(8,128)} %get-tuple-element.23.lon_b_own) | copy-start | bytes 122884

commit v6 on v5

--- a/solution.py
+++ b/solution.py
@@ -10,7 +10,7 @@
 
 BLOCK = 16
 SUBSTEPS = 2
-GROUP = 16
+GROUP = 8
 ROWS_IN_FLIGHT = 2
 LEVELS_AT_ONCE = 4
 LAG = 1
@@ -19,6 +19,7 @@
 BF16 = jnp.bfloat16
 VMEM_BYTES = 48 * 1024 * 1024
 FIRST_VMEM_BYTES = 56 * 1024 * 1024
+PREPARE_VMEM_BYTES = 50 * 1024 * 1024
 
 
 def lane_ids(shape):
@@ -28,15 +29,18 @@
 def fold_weights(decode_t, react_a_t, react_b_t, stoich, encode, rate, linear_out, encode_out):
     n_reactions = react_a_t.shape[1]
     contract = (((0,), (1,)), ((), ()))
-    for part, react in enumerate((react_a_t, react_b_t)):
-        product = lax.dot_general(
-            react[...], decode_t[...], contract, preferred_element_type=F32
-        )
-        for group in range(n_reactions // GROUP):
-            at = (2 * group + part) * GROUP
-            linear_out[at : at + GROUP, :] = product[
-                group * GROUP : (group + 1) * GROUP
-            ].astype(BF16)
+    products = [
+        lax.dot_general(react[...], decode_t[...], contract, preferred_element_type=F32)
+        for react in (react_a_t, react_b_t)
+    ]
+    linear_out[...] = jnp.concatenate(
+        [
+            product[at : at + GROUP]
+            for at in range(0, n_reactions, GROUP)
+            for product in products
+        ],
+        axis=0,
+    ).astype(BF16)
     folded = jnp.dot(encode[...], stoich[...], preferred_element_type=F32)
     encode_out[...] = (folded * rate[...]).astype(BF16)
 
@@ -201,14 +205,21 @@
 
 
 def prepare_kernel(latent, east_c, north_c, mixing, *refs):
-    weights, (field, coefs, linear, encode) = refs[:6], refs[6:]
+    weights, (field, coefs, linear, encode, tiles, sems) = refs[:6], refs[6:]
     n_levels, n_rows, _, n_cols = field.shape
+    copies = [
+        pltpu.make_async_copy(latent.at[:, level], tiles.at[level], sems.at[level])
+        for level in range(n_levels)
+    ]
+    for copy in copies:
+        copy.start()
     fold_weights(*weights, linear, encode)
     is_first, is_last = at_ends()
     row_ids = lax.broadcasted_iota(jnp.int32, (n_rows, n_cols), 0)
     upper = None
     for level in range(n_levels):
-        field[level] = jnp.transpose(latent[:, level], (1, 0, 2))
+        copies[level].wait()
+        field[level] = jnp.transpose(tiles[level], (1, 0, 2))
         ce, cn = east_c[level], north_c[level]
         east, west = jnp.maximum(ce, 0.0), jnp.minimum(ce, 0.0)
         north = jnp.where((row_ids == n_rows - 1) & is_last, 0.0, jnp.maximum(cn, 0.0))
@@ -541,9 +552,13 @@
             jax.ShapeDtypeStruct((2 * n_reactions, n_species), BF16),
             jax.ShapeDtypeStruct((n_species, n_reactions), BF16),
         ),
-        in_specs=vmem(4 + len(weights)),
+        in_specs=[hbm] + vmem(3 + len(weights)),
         out_specs=tuple(vmem(4)),
-        compiler_params=params,
+        scratch_shapes=[
+            pltpu.VMEM((n_levels, n_species, n_rows, n_cols), F32),
+            pltpu.SemaphoreType.DMA((n_levels,)),
+        ],
+        compiler_params=pltpu.CompilerParams(vmem_limit_bytes=PREPARE_VMEM_BYTES),
         name="prepare",
         cost_estimate=pl.CostEstimate(flops=4_000_000_000, bytes_accessed=1, transcendentals=0),
     )(latent_field, east_courant, north_courant, mixing, *weights)

time: 38.8 us -> 38.8 us (level)
  Pallas kernels: 26.9 us -> 28 us
  waiting for transfers between devices: 2.22 us -> 1.12 us
    pallas_call x1, Pallas kernels: 0.64 us -> 1.75 us  [on_device(): pl.pallas_call(prepare_kernel, out_shape=(layered, jax.ShapeDtypeStruct((...]
    ppermute x6, waiting for transfers between devices: 2.22 us -> 1.12 us  [swapped(): return lax.ppermute(array, axis, pairs + [(j, i) for i, j in pairs])]
  transfers between devices with their start and end apart: 6 -> 6, of which waited for: 2 -> 2; matrix products, arithmetic and copies ran while one was open for 0% -> 0% of each run, Pallas kernels for 25% -> 28%
where the time goes in v6:
time: 38.8 us; the launch traced here: 38.6 us
  Pallas kernels  28 us (72%)
  starting transfers between devices  9.16 us (24%)
  waiting for transfers between devices  1.12 us (3%)
    pallas_call x3, Pallas kernels, call(): pl.pallas_call(kernel, out_shape=out_shape, in_specs=vmem(len(operands)),...  23 us
    ppermute x6, starting transfers between devices, swapped(): return lax.ppermute(array, axis, pairs + [(j, i) for i, j in pairs])  9.16 us
    pallas_call x1, Pallas kernels, on_device(): pl.pallas_call(first_kernel, out_shape=(column, column, edge, edge), in_s...  3.2 us
    pallas_call x1, Pallas kernels, on_device(): pl.pallas_call(prepare_kernel, out_shape=(layered, jax.ShapeDtypeStruct((...  1.75 us
    ppermute x6, waiting for transfers between devices, swapped(): return lax.ppermute(array, axis, pairs + [(j, i) for i, j in pairs])  1.12 us
  transfers between devices with their start and end apart: 6, of which 2 were waited for; matrix products, arithmetic and copies ran while one was open for 0% of the time, Pallas kernels for 28%

profile of v6, /device:TPU:0, one launch (start us, length us, event | category | flops | bytes accessed | tf_op | source)
XLA Modules:
  0.0 38.6 jit_solution(11698522121971340398)
XLA Ops:
  0.0 0.0 copy-start.5
  0.0 0.0 copy-start.4
  0.0 0.0 copy-start.3
  0.0 0.0 copy-start.10
  0.0 0.0 copy-start.9
  0.0 0.0 copy-start.2
  0.0 0.0 copy-start.1
  0.0 0.0 copy-start
  0.0 0.0 copy-start.8
  0.1 3.2 %first_sends.1 = (f32[80,128]{1,0:T(8,128)}, f32[80,128]{1,0:T(8,128)}, bf16[8,32,128]{2,1,0:T(8,128)(2,1)}, bf16[8,32,128]{2,1,0:T(8,128)(2,1)}) custom-call(s32[1,8]{1,0:T(1,128)} %sun.7, f32[32,8,16,128]{3,2,1,0:T(8,128)} %latent.3, f32[8,16,128]{2,1,0:T(8,128)} %east_c.3, f32[8,16,128]{2,1,0:T(8,128)} %north_c.3, f32[7,16,128]{2,1,0:T(8,128)} %mixing.3), custom_call_target="tpu_custom_call" | custom-call | flops 4000000000 | bytes 2000000 | tf_op jit(solution)/shard_map/first_sends/pallas_call | solution.py:527
  3.3 6.1 %collective-permute-start.2 = (f32[80,128]{1,0:T(8,128)}, f32[80,128]{1,0:T(8,128)S(1)}, u32[]{:S(2)}, u32[]{:S(2)}) collective-permute-start(f32[80,128]{1,0:T(8,128)} %get-tuple-element.23.lon_b_own), channel_id=1, source_target_pairs={{1,2},{3,4},{5,6},{7,0},{2,1},{4,3},{6,5},{0,7},{9,10},{11,12},{13... | collective-permute-start | bytes 122888 | tf_op jit(solution)/shard_map/ppermute | solution.py:503
  9.4 0.0 collective-permute-start.3
  9.4 0.7 %collective-permute-start = (bf16[8,32,128]{2,1,0:T(8,128)(2,1)}, bf16[8,32,128]{2,1,0:T(8,128)(2,1)S(1)}, u32[]{:S(2)}, u32[]{:S(2)}) collective-permute-start(bf16[8,32,128]{2,1,0:T(8,128)(2,1)} %get-tuple-element.21), channel_id=1, source_target_pairs={{8,16},{24,0},{16,8},{0,24},{9,17},{25,1},{17,9},{1,25},{10,18},{2... | collective-permute-start | bytes 196616 | tf_op jit(solution)/shard_map/ppermute | solution.py:503
  10.0 1.0 %collective-permute-start.1 = (bf16[8,32,128]{2,1,0:T(8,128)(2,1)}, bf16[8,32,128]{2,1,0:T(8,128)(2,1)S(1)}, u32[]{:S(2)}, u32[]{:S(2)}) collective-permute-start(bf16[8,32,128]{2,1,0:T(8,128)(2,1)} %get-tuple-element.22), channel_id=1, source_target_pairs={{0,8},{16,24},{8,0},{24,16},{1,9},{17,25},{9,1},{25,17},{2,10},{18... | collective-permute-start | bytes 196616 | tf_op jit(solution)/shard_map/ppermute | solution.py:503
  11.0 0.0 copy-done.5
  11.0 0.0 copy-done.4
  11.0 0.0 copy-done.3
  11.0 0.0 copy-done.10
  11.0 0.0 copy-done.9
  11.0 0.0 copy-done.2
  11.0 0.0 copy-done.1
  11.0 0.0 copy-done
  11.0 0.0 copy-done.8
  11.0 0.0 copy-start.11
  11.1 1.7 %prepare.1 = (f32[8,16,32,128]{3,2,1,0:T(8,128)S(1)}, f32[8,8,16,128]{3,2,1,0:T(8,128)S(1)}, bf16[512,32]{1,0:T(8,128)(2,1)S(1)}, bf16[32,256]{1,0:T(8,128)(2,1)S(1)}) custom-call(f32[32,8,16,128]{3,2,1,0:T(8,128)} %latent.3, f32[8,16,128]{2,1,0:T(8,128)S(1)} %copy-done.3, f32[8,16,128]{2,1,0:T(8,128)S(1)} %copy-done.4, f32[7,16,128]{2,1,0:T(8,128)S(1)} %copy-done.5, ...), custom_call_target="tpu_custom_call" | custom-call | flops 4000000000 | bytes 1 | tf_op jit(solution)/shard_map/prepare/pallas_call | solution.py:547
  12.8 0.0 collective-permute-done.2.lon_b_in
  12.8 0.8 %collective-permute-done.3.lon_a_in = f32[80,128]{1,0:T(8,128)S(1)} collective-permute-done((f32[80,128]{1,0:T(8,128)}, f32[80,128]{1,0:T(8,128)S(1)}, u32[]{:S(2)}, u32[]{:S(2)}) %collective-permute-start.3) | collective-permute-done | bytes 40992 | tf_op jit(solution)/shard_map/ppermute | solution.py:503
  13.6 0.3 collective-permute-done.lat_b_in
  13.9 0.0 collective-permute-done.1.lat_a_in
  13.9 0.0 copy-done.11
  13.9 1.8 %edge_rows.1 = (f32[8,2,32,128]{3,2,1,0:T(8,128)S(1)}, bf16[9,32,128]{2,1,0:T(8,128)(2,1)S(1)}, bf16[9,32,128]{2,1,0:T(8,128)(2,1)S(1)}, f32[2,32,128]{2,1,0:T(8,128)S(1)}) custom-call(s32[1,8]{1,0:T(1,128)S(1)} %copy-done.11, f32[8,16,32,128]{3,2,1,0:T(8,128)S(1)} %get-tuple-element.17.field, f32[8,8,16,128]{3,2,1,0:T(8,128)S(1)} %get-tuple-element.18.coefs, ...), custom_call_target="tpu_custom_call" | custom-call | flops 20000000000 | bytes 1 | tf_op jit(solution)/shard_map/edge_rows/pallas_call | solution.py:570
  15.7 0.8 %collective-permute-start.4 = (bf16[9,32,128]{2,1,0:T(8,128)(2,1)S(1)}, bf16[9,32,128]{2,1,0:T(8,128)(2,1)S(1)}, u32[]{:S(2)}, u32[]{:S(2)}) collective-permute-start(bf16[9,32,128]{2,1,0:T(8,128)(2,1)S(1)} %get-tuple-element.27), channel_id=1, source_target_pairs={{8,16},{24,0},{16,8},{0,24},{9,17},{25,1},{17,9},{1,25},{10,18},{2... | collective-permute-start | bytes 221192 | tf_op jit(solution)/shard_map/ppermute | solution.py:503
  16.5 0.7 %collective-permute-start.5 = (bf16[9,32,128]{2,1,0:T(8,128)(2,1)S(1)}, bf16[9,32,128]{2,1,0:T(8,128)(2,1)S(1)}, u32[]{:S(2)}, u32[]{:S(2)}) collective-permute-start(bf16[9,32,128]{2,1,0:T(8,128)(2,1)S(1)} %get-tuple-element.28), channel_id=1, source_target_pairs={{0,8},{16,24},{8,0},{24,16},{1,9},{17,25},{9,1},{25,17},{2,10},{18... | collective-permute-start | bytes 221192 | tf_op jit(solution)/shard_map/ppermute | solution.py:503
  17.2 0.0 copy-start.6
  17.2 0.0 copy-start.7
  17.2 9.1 %inner_rows.1.field = f32[8,16,32,128]{3,2,1,0:T(8,128)S(1)} custom-call(s32[1,8]{1,0:T(1,128)S(1)} %copy-done.11, f32[8,16,32,128]{3,2,1,0:T(8,128)S(1)} %get-tuple-element.17.field, f32[8,8,16,128]{3,2,1,0:T(8,128)S(1)} %get-tuple-element.18.coefs, bf16[512,32]{1,0:T(8,128)(2,1)S(1)} %get-tuple-element.19.linear, ...), custom_call_target="tpu_custom_call" | custom-call | flops 20000000000 | bytes 1 | tf_op jit(solution)/shard_map/inner_rows/pallas_call | solution.py:570
  26.3 0.0 collective-permute-done.4.lat_b_in
  26.3 0.0 collective-permute-done.5.lat_a_in
  26.3 0.0 copy-done.6
  26.3 0.0 copy-done.7
  26.3 12.2 %last_step.1 = f32[32,8,16,128]{3,2,1,0:T(8,128)} custom-call(s32[1,8]{1,0:T(1,128)S(1)} %copy-done.11, f32[8,16,32,128]{3,2,1,0:T(8,128)S(1)} %inner_rows.1.field, f32[8,8,16,128]{3,2,1,0:T(8,128)S(1)} %get-tuple-element.18.coefs, bf16[512,32]{1,0:T(8,128)(2,1)S(1)} %get-tuple-element.19.linear, bf16[32,256]{1,0:T(8,128)(2,1)S(1)} %get-tuple-element.20.encode, ...), custom_call_target="tpu_custom_call" | custom-call | flops 20000000000 | bytes 1 | tf_op jit(solution)/shard_map/last_step/pallas_call | solution.py:570
Async XLA Ops:
  0.0 11.0 %copy-start.5 = (f32[7,16,128]{2,1,0:T(8,128)S(1)}, f32[7,16,128]{2,1,0:T(8,128)}, u32[]{:S(2)}) copy-start(f32[7,16,128]{2,1,0:T(8,128)} %mixing.3) | copy-start | bytes 172036
  0.0 11.0 %copy-start.4 = (f32[8,16,128]{2,1,0:T(8,128)S(1)}, f32[8,16,128]{2,1,0:T(8,128)}, u32[]{:S(2)}) copy-start(f32[8,16,128]{2,1,0:T(8,128)} %north_c.3) | copy-start | bytes 196612
  0.0 11.0 %copy-start.3 = (f32[8,16,128]{2,1,0:T(8,128)S(1)}, f32[8,16,128]{2,1,0:T(8,128)}, u32[]{:S(2)}) copy-start(f32[8,16,128]{2,1,0:T(8,128)} %east_c.3) | copy-start | bytes 196612
  0.0 11.0 %copy-start.10 = (f32[256]{0:T(256)S(1)}, f32[256]{0:T(256)}, u32[]{:S(2)}) copy-start(f32[256]{0:T(256)} %param.21) | copy-start | bytes 3076
  0.0 11.0 %copy-start.9 = (bf16[32,224]{1,0:T(8,128)(2,1)S(1)}, bf16[32,224]{1,0:T(8,128)(2,1)}, u32[]{:S(2)}) copy-start(bf16[32,224]{1,0:T(8,128)(2,1)} %refs_4_.1) | copy-start | bytes 43012
  0.0 11.0 %copy-start.2 = (bf16[224,256]{1,0:T(8,128)(2,1)S(1)}, bf16[224,256]{1,0:T(8,128)(2,1)}, u32[]{:S(2)}) copy-start(bf16[224,256]{1,0:T(8,128)(2,1)} %refs_3_.1) | copy-start | bytes 344068
  0.0 11.0 %copy-start.1 = (bf16[256,224]{0,1:T(8,128)(2,1)S(1)}, bf16[256,224]{0,1:T(8,128)(2,1)}, u32[]{:S(2)}) copy-start(bf16[256,224]{0,1:T(8,128)(2,1)} %param.18) | copy-start | bytes 344068
  0.0 11.0 %copy-start = (bf16[256,224]{0,1:T(8,128)(2,1)S(1)}, bf16[256,224]{0,1:T(8,128)(2,1)}, u32[]{:S(2)}) copy-start(bf16[256,224]{0,1:T(8,128)(2,1)} %param.17) | copy-start | bytes 344068
  0.0 11.0 %copy-start.8 = (bf16[224,32]{0,1:T(8,128)(2,1)S(1)}, bf16[224,32]{0,1:T(8,128)(2,1)}, u32[]{:S(2)}) copy-start(bf16[224,32]{0,1:T(8,128)(2,1)} %param.16) | copy-start | bytes 43012
  3.3 9.6 %collective-permute-start.2 = (f32[80,128]{1,0:T(8,128)}, f32[80,128]{1,0:T(8,128)S(1)}, u32[]{:S(2)}, u32[]{:S(2)}) collective-permute-start(f32[80,128]{1,0:T(8,128)} %get-tuple-element.23.lon_b_own), channel_id=1, source_target_pairs={{1,2},{3,4},{5,6},{7,0},{2,1},{4,3},{6,5},{0,7},{9,10},{11,12},{13... | collective-permute-start | bytes 122888 | tf_op jit(solution)/shard_map/ppermute | solution.py:503
  9.4 4.2 %collective-permute-start.3 = (f32[80,128]{1,0:T(8,128)}, f32[80,128]{1,0:T(8,128)S(1)}, u32[]{:S(2)}, u32[]{:S(2)}) collective-permute-start(f32[80,128]{1,0:T(8,128)} %get-tuple-element.24.lon_a_own), channel_id=1, source_target_pairs={{0,1},{2,3},{4,5},{6,7},{1,0},{3,2},{5,4},{7,6},{8,9},{10,11},{12,... | collective-permute-start | bytes 122888 | tf_op jit(solution)/shard_map/ppermute | solution.py:503
  9.4 4.6 %collective-permute-start = (bf16[8,32,128]{2,1,0:T(8,128)(2,1)}, bf16[8,32,128]{2,1,0:T(8,128)(2,1)S(1)}, u32[]{:S(2)}, u32[]{:S(2)}) collective-permute-start(bf16[8,32,128]{2,1,0:T(8,128)(2,1)} %get-tuple-element.21), channel_id=1, source_target_pairs={{8,16},{24,0},{16,8},{0,24},{9,17},{25,1},{17,9},{1,25},{10,18},{2... | collective-permute-start | bytes 196616 | tf_op jit(solution)/shard_map/ppermute | solution.py:503
  10.0 3.9 %collective-permute-start.1 = (bf16[8,32,128]{2,1,0:T(8,128)(2,1)}, bf16[8,32,128]{2,1,0:T(8,128)(2,1)S(1)}, u32[]{:S(2)}, u32[]{:S(2)}) collective-permute-start(bf16[8,32,128]{2,1,0:T(8,128)(2,1)} %get-tuple-element.22), channel_id=1, source_target_pairs={{0,8},{16,24},{8,0},{24,16},{1,9},{17,25},{9,1},{25,17},{2,10},{18... | collective-permute-start | bytes 196616 | tf_op jit(solution)/shard_map/ppermute | solution.py:503
  11.0 2.9 %copy-start.11 = (s32[1,8]{1,0:T(1,128)S(1)}, s32[1,8]{1,0:T(1,128)}, u32[]{:S(2)}) copy-start(s32[1,8]{1,0:T(1,128)} %sun.7) | copy-start | bytes 100
  15.7 10.5 %collective-permute-start.4 = (bf16[9,32,128]{2,1,0:T(8,128)(2,1)S(1)}, bf16[9,32,128]{2,1,0:T(8,128)(2,1)S(1)}, u32[]{:S(2)}, u32[]{:S(2)}) collective-permute-start(bf16[9,32,128]{2,1,0:T(8,128)(2,1)S(1)} %get-tuple-element.27), channel_id=1, source_target_pairs={{8,16},{24,0},{16,8},{0,24},{9,17},{25,1},{17,9},{1,25},{10,18},{2... | collective-permute-start | bytes 221192 | tf_op jit(solution)/shard_map/ppermute | solution.py:503
  16.5 9.8 %collective-permute-start.5 = (bf16[9,32,128]{2,1,0:T(8,128)(2,1)S(1)}, bf16[9,32,128]{2,1,0:T(8,128)(2,1)S(1)}, u32[]{:S(2)}, u32[]{:S(2)}) collective-permute-start(bf16[9,32,128]{2,1,0:T(8,128)(2,1)S(1)} %get-tuple-element.28), channel_id=1, source_target_pairs={{0,8},{16,24},{8,0},{24,16},{1,9},{17,25},{9,1},{25,17},{2,10},{18... | collective-permute-start | bytes 221192 | tf_op jit(solution)/shard_map/ppermute | solution.py:503
  17.2 9.1 %copy-start.6 = (f32[80,128]{1,0:T(8,128)S(1)}, f32[80,128]{1,0:T(8,128)}, u32[]{:S(2)}) copy-start(f32[80,128]{1,0:T(8,128)} %get-tuple-element.24.lon_a_own) | copy-start | bytes 122884
  17.2 9.1 %copy-start.7 = (f32[80,128]{1,0:T(8,128)S(1)}, f32[80,128]{1,0:T(8,128)}, u32[]{:S(2)}) copy-start(f32[80,128]{1,0:T(8,128)} %get-tuple-element.23.lon_b_own) | copy-start | bytes 122884

commit v7 on v6

--- a/solution.py
+++ b/solution.py
@@ -262,7 +262,9 @@
     return lit > 0
 
 
-def step_rows(order, sun, field, coefs, linear, encode, lon_in, south_in, north_in, diffused, finish, passage=None):
+def step_rows(
+    order, sun, field, coefs, linear, encode, lon_of, south_in, north_in, diffused, finish, early=None, passage=None
+):
     n_levels, n_rows, _, n_cols = field.shape
     lanes = lane_ids((1, n_cols))
 
@@ -274,7 +276,7 @@
         for level in range(n_levels):
             value = field[level, r]
             spot = level * 2 * n_rows % n_cols
-            halo = lon_in[level * 2 * n_rows // n_cols]
+            halo = lon_of(r)[level * 2 * n_rows // n_cols]
             from_west = jnp.where(
                 lanes == 0,
                 pltpu.roll(halo, (n_cols - spot - r) % n_cols, 1),
@@ -331,6 +333,8 @@
             if substep == 0:
                 rounded[at] = tile_at(level, r).astype(BF16)
             rates[at] = product_of(linear, rounded.pop(at))
+            if early is not None:
+                next(early, None)
             if passage is not None and at > len(units) // 2 + LAG:
                 next(passage, None)
             for _ in itertools.islice(*beside[at]):
@@ -380,7 +384,9 @@
     def finish(level, r, value):
         done[level, order.index(r)] = value
 
-    step_rows(order, sun, field, coefs, linear, encode, lon_in, south_in, north_in, diffused, finish)
+    step_rows(
+        order, sun, field, coefs, linear, encode, lambda r: lon_in, south_in, north_in, diffused, finish
+    )
     for level in range(n_levels):
         south = (done[level, 0] * coefs[SOUTH, level, :1]).astype(BF16)
         north = (done[level, 1] * coefs[NORTH, level, n_rows - 1 :]).astype(BF16)
@@ -398,32 +404,14 @@
     by_parity("lat", north, south, lat_a.at[n_levels], lat_b.at[n_levels])
 
 
-def inner_rows_kernel(sun, field, coefs, linear, encode, done, lon_in, out, diffused):
-    n_levels, n_rows, _, _ = field.shape
-    for level in range(n_levels):
-        out[level, 0] = done[level, 0]
-        out[level, n_rows - 1] = done[level, 1]
-
-    def finish(level, r, value):
-        out[level, r] = value
-
-    order = list(range(1, n_rows - 1))
-    step_rows(order, sun, field, coefs, linear, encode, lon_in, None, None, diffused, finish)
-
-
-def last_step_kernel(
-    sun, field, coefs, linear, encode, lat_b_in, lat_a_in, lon_b_in, lon_a_in, lon_a_own, lon_b_own,
-    out, staged, sems, south_in, north_in, lon_in, diffused,
+def columns_ahead(
+    n_levels, n_rows, n_species, linear, encode, received, own, south_in, north_in, lon_out
 ):
-    n_levels, n_rows, n_species, n_cols = field.shape
-    half_rows = n_rows // 2
+    (west_near, west_far), (east_near, east_far) = near_and_far(*received)
+    (own_east, _), (own_west, _) = sent_columns(*own)
+    n_cols = west_near.shape[1]
     lanes = lane_ids((1, n_cols))
     ends = at_ends()
-    by_parity("lat", lat_a_in[...], lat_b_in[...], north_in, south_in)
-    (west_near, west_far), (east_near, east_far) = near_and_far(lon_b_in, lon_a_in)
-    even = is_even("lon")
-    own_west, _ = split_columns(jnp.where(even, lon_b_own[...], lon_a_own[...]))
-    own_east, _ = split_columns(jnp.where(even, lon_a_own[...], lon_b_own[...]))
 
     def levels_of(west, east):
         return by_level(west, east, n_levels, n_rows)
@@ -432,6 +420,8 @@
         return levels_of(west_near[kind : kind + 1], east_near[kind : kind + 1])
 
     def corner(edge, at, turn):
+        if edge is None:
+            return 0.0
         shift = turn if at == 0 else (turn + (1 if turn > n_rows else n_cols - 1)) % n_cols
         return pltpu.roll(edge[n_levels].astype(F32), shift, 1)
 
@@ -447,26 +437,74 @@
             ends,
         )
 
-    moved = levels_of(
-        column_after(0, west_near, west_far, own_west),
-        column_after(1, east_near, own_east, east_far),
-    )
-    pair = jnp.concatenate(joined(diffused_columns(moved, kind_of(MIXING_ROW)), n_rows), axis=1)
+    west = column_after(0, west_near, west_far, own_west)
+    yield
+    east = column_after(1, east_near, own_east, east_far)
+    yield
+    moved = levels_of(west, east)
+    mixing = kind_of(MIXING_ROW)
+    yield
+    pair = jnp.concatenate(joined(diffused_columns(moved, mixing), n_rows), axis=1)
     rounded = pair.astype(BF16)
     current, summed = rounded.astype(F32), None
+    yield
     for substep in range(SUBSTEPS):
-        change = jnp.dot(encode[...], product_of(linear, rounded), preferred_element_type=F32)
+        rates = product_of(linear, rounded)
+        yield
+        change = jnp.dot(encode[...], rates, preferred_element_type=F32)
         summed = change if summed is None else summed + change
         current = current + change
         rounded = current.astype(BF16)
+        yield
     pair_lit = jnp.concatenate(joined(kind_of(LIT_ROW), n_rows), axis=1)
     pair = pair + jnp.where(pair_lit > 0.0, summed, 0.0)
     for at, speed in enumerate(joined(kind_of(EAST_ROW), n_rows)):
         clipped = jnp.where(
             lanes // n_rows % 2 == 0, jnp.maximum(speed, 0.0), jnp.minimum(speed, 0.0)
         )
-        lon_in[at] = pair[:, at * n_cols : (at + 1) * n_cols] * clipped
-
+        lon_out[at] = pair[:, at * n_cols : (at + 1) * n_cols] * clipped
+
+
+def sent_columns(lon_b_own, lon_a_own):
+    even = is_even("lon")
+    east = split_columns(jnp.where(even, lon_a_own[...], lon_b_own[...]))
+    west = split_columns(jnp.where(even, lon_b_own[...], lon_a_own[...]))
+    return east, west
+
+
+def inner_rows_kernel(
+    sun, field, coefs, linear, encode, lon_b_in, lon_a_in, lon_b_own, lon_a_own, done, lon_in,
+    out, lon_out, diffused,
+):
+    n_levels, n_rows, n_species, _ = field.shape
+    for level in range(n_levels):
+        out[level, 0] = done[level, 0]
+        out[level, n_rows - 1] = done[level, 1]
+
+    def finish(level, r, value):
+        out[level, r] = value
+
+    early = columns_ahead(
+        n_levels, n_rows, n_species, linear, encode,
+        (lon_b_in, lon_a_in), (lon_b_own, lon_a_own), None, None, lon_out,
+    )
+    order = list(range(1, n_rows - 1))
+    step_rows(
+        order, sun, field, coefs, linear, encode, lambda r: lon_in, None, None, diffused, finish, early
+    )
+
+
+def last_step_kernel(
+    sun, field, coefs, linear, encode, lon_b_in, lon_a_in, lon_b_own, lon_a_own, lon_in, lat_b_in, lat_a_in,
+    out, staged, sems, south_in, north_in, lon_ends, diffused,
+):
+    n_levels, n_rows, n_species, _ = field.shape
+    half_rows = n_rows // 2
+    by_parity("lat", lat_a_in[...], lat_b_in[...], north_in, south_in)
+    early = columns_ahead(
+        n_levels, n_rows, n_species, linear, encode,
+        (lon_b_in, lon_a_in), (lon_b_own, lon_a_own), south_in, north_in, lon_ends,
+    )
     copies = []
 
     def send(half):
@@ -483,9 +521,11 @@
     def finish(level, r, value):
         diffused[level, r] = value
 
+    order = list(range(1, half_rows)) + [0] + list(range(half_rows, n_rows))
     step_rows(
-        list(range(n_rows)), sun, field, coefs, linear, encode, lon_in, south_in, north_in, diffused,
-        finish, send(0),
+        order, sun, field, coefs, linear, encode,
+        lambda r: lon_ends if r in (0, n_rows - 1) else lon_in,
+        south_in, north_in, diffused, finish, early, send(0),
     )
     for _ in send(1):
         pass
@@ -594,13 +634,19 @@
         layered,
     )
     lat_halos = swapped(lat_b, "lat", 1), swapped(lat_a, "lat", 0)
-    (field,) = call(
-        inner_rows_kernel, "inner_rows", (*shared, done, lon_in), (layered,), tuple(vmem(1)), layered
+    columns = *lon_halos, lon_b, lon_a
+    field, lon_in = call(
+        inner_rows_kernel,
+        "inner_rows",
+        (*shared, *columns, done, lon_in),
+        (layered, halo),
+        tuple(vmem(2)),
+        layered,
     )
     (advanced,) = call(
         last_step_kernel,
         "last_step",
-        (sunlit, field, coefs, linear, encode, *lat_halos, *lon_halos, lon_a, lon_b),
+        (sunlit, field, coefs, linear, encode, *columns, lon_in, *lat_halos),
         (jax.ShapeDtypeStruct(latent_field.shape, F32),),
         (hbm,),
         pltpu.VMEM((2, n_levels, n_species, n_rows // 2, n_cols), F32),

time: 38.8 us -> 39 us (level)
  transfers between devices with their start and end apart: 6 -> 6, of which waited for: 2 -> 2; matrix products, arithmetic and copies ran while one was open for 0% -> 0% of each run, Pallas kernels for 28% -> 29%
where the time goes in v7:
time: 39 us; the launch traced here: 38.9 us
  Pallas kernels  28.2 us (72%)
  starting transfers between devices  9.16 us (23%)
  waiting for transfers between devices  1.12 us (3%)
    pallas_call x3, Pallas kernels, call(): pl.pallas_call(kernel, out_shape=out_shape, in_specs=vmem(len(operands)),...  23.3 us
    ppermute x6, starting transfers between devices, swapped(): return lax.ppermute(array, axis, pairs + [(j, i) for i, j in pairs])  9.16 us
    pallas_call x1, Pallas kernels, on_device(): pl.pallas_call(first_kernel, out_shape=(column, column, edge, edge), in_s...  3.2 us
    pallas_call x1, Pallas kernels, on_device(): pl.pallas_call(prepare_kernel, out_shape=(layered, jax.ShapeDtypeStruct((...  1.75 us
    ppermute x6, waiting for transfers between devices, swapped(): return lax.ppermute(array, axis, pairs + [(j, i) for i, j in pairs])  1.12 us
  transfers between devices with their start and end apart: 6, of which 2 were waited for; matrix products, arithmetic and copies ran while one was open for 0% of the time, Pallas kernels for 29%

profile of v7, /device:TPU:0, one launch (start us, length us, event | category | flops | bytes accessed | tf_op | source)
XLA Modules:
  0.0 38.9 jit_solution(13545016448536566310)
XLA Ops:
  0.0 0.0 copy-start.5
  0.0 0.0 copy-start.4
  0.0 0.0 copy-start.3
  0.0 0.0 copy-start.10
  0.0 0.0 copy-start.9
  0.0 0.0 copy-start.2
  0.0 0.0 copy-start.1
  0.0 0.0 copy-start
  0.0 0.0 copy-start.8
  0.1 3.2 %first_sends.1 = (f32[80,128]{1,0:T(8,128)}, f32[80,128]{1,0:T(8,128)}, bf16[8,32,128]{2,1,0:T(8,128)(2,1)}, bf16[8,32,128]{2,1,0:T(8,128)(2,1)}) custom-call(s32[1,8]{1,0:T(1,128)} %sun.7, f32[32,8,16,128]{3,2,1,0:T(8,128)} %latent.3, f32[8,16,128]{2,1,0:T(8,128)} %east_c.3, f32[8,16,128]{2,1,0:T(8,128)} %north_c.3, f32[7,16,128]{2,1,0:T(8,128)} %mixing.3), custom_call_target="tpu_custom_call" | custom-call | flops 4000000000 | bytes 2000000 | tf_op jit(solution)/shard_map/first_sends/pallas_call | solution.py:567
  3.3 6.1 %collective-permute-start = (f32[80,128]{1,0:T(8,128)}, f32[80,128]{1,0:T(8,128)S(1)}, u32[]{:S(2)}, u32[]{:S(2)}) collective-permute-start(f32[80,128]{1,0:T(8,128)} %get-tuple-element.23.lon_b_own), channel_id=1, source_target_pairs={{1,2},{3,4},{5,6},{7,0},{2,1},{4,3},{6,5},{0,7},{9,10},{11,12},{13... | collective-permute-start | bytes 122888 | tf_op jit(solution)/shard_map/ppermute | solution.py:543
  9.4 0.0 collective-permute-start.1
  9.4 0.7 %collective-permute-start.2 = (bf16[8,32,128]{2,1,0:T(8,128)(2,1)}, bf16[8,32,128]{2,1,0:T(8,128)(2,1)S(1)}, u32[]{:S(2)}, u32[]{:S(2)}) collective-permute-start(bf16[8,32,128]{2,1,0:T(8,128)(2,1)} %get-tuple-element.25), channel_id=1, source_target_pairs={{8,16},{24,0},{16,8},{0,24},{9,17},{25,1},{17,9},{1,25},{10,18},{2... | collective-permute-start | bytes 196616 | tf_op jit(solution)/shard_map/ppermute | solution.py:543
  10.0 1.0 %collective-permute-start.3 = (bf16[8,32,128]{2,1,0:T(8,128)(2,1)}, bf16[8,32,128]{2,1,0:T(8,128)(2,1)S(1)}, u32[]{:S(2)}, u32[]{:S(2)}) collective-permute-start(bf16[8,32,128]{2,1,0:T(8,128)(2,1)} %get-tuple-element.26), channel_id=1, source_target_pairs={{0,8},{16,24},{8,0},{24,16},{1,9},{17,25},{9,1},{25,17},{2,10},{18... | collective-permute-start | bytes 196616 | tf_op jit(solution)/shard_map/ppermute | solution.py:543
  11.0 0.0 copy-done.5
  11.0 0.0 copy-done.4
  11.0 0.0 copy-done.3
  11.0 0.0 copy-done.10
  11.0 0.0 copy-done.9
  11.0 0.0 copy-done.2
  11.0 0.0 copy-done.1
  11.0 0.0 copy-done
  11.0 0.0 copy-done.8
  11.0 0.0 copy-start.11
  11.1 1.7 %prepare.1 = (f32[8,16,32,128]{3,2,1,0:T(8,128)S(1)}, f32[8,8,16,128]{3,2,1,0:T(8,128)S(1)}, bf16[512,32]{1,0:T(8,128)(2,1)S(1)}, bf16[32,256]{1,0:T(8,128)(2,1)S(1)}) custom-call(f32[32,8,16,128]{3,2,1,0:T(8,128)} %latent.3, f32[8,16,128]{2,1,0:T(8,128)S(1)} %copy-done.3, f32[8,16,128]{2,1,0:T(8,128)S(1)} %copy-done.4, f32[7,16,128]{2,1,0:T(8,128)S(1)} %copy-done.5, ...), custom_call_target="tpu_custom_call" | custom-call | flops 4000000000 | bytes 1 | tf_op jit(solution)/shard_map/prepare/pallas_call | solution.py:587
  12.8 0.0 collective-permute-done.lon_b_in
  12.8 0.8 %collective-permute-done.1.lon_a_in = f32[80,128]{1,0:T(8,128)S(1)} collective-permute-done((f32[80,128]{1,0:T(8,128)}, f32[80,128]{1,0:T(8,128)S(1)}, u32[]{:S(2)}, u32[]{:S(2)}) %collective-permute-start.1) | collective-permute-done | bytes 40992 | tf_op jit(solution)/shard_map/ppermute | solution.py:543
  13.6 0.3 collective-permute-done.2.lat_b_in
  13.9 0.0 collective-permute-done.3.lat_a_in
  13.9 0.0 copy-done.11
  13.9 0.0 copy-start.6
  13.9 0.0 copy-start.7
  13.9 1.8 %edge_rows.1 = (f32[8,2,32,128]{3,2,1,0:T(8,128)S(1)}, bf16[9,32,128]{2,1,0:T(8,128)(2,1)S(1)}, bf16[9,32,128]{2,1,0:T(8,128)(2,1)S(1)}, f32[2,32,128]{2,1,0:T(8,128)S(1)}) custom-call(s32[1,8]{1,0:T(1,128)S(1)} %copy-done.11, f32[8,16,32,128]{3,2,1,0:T(8,128)S(1)} %get-tuple-element.19.field, f32[8,8,16,128]{3,2,1,0:T(8,128)S(1)} %get-tuple-element.20.coefs, ...), custom_call_target="tpu_custom_call" | custom-call | flops 20000000000 | bytes 1 | tf_op jit(solution)/shard_map/edge_rows/pallas_call | solution.py:610
  15.8 0.8 %collective-permute-start.4 = (bf16[9,32,128]{2,1,0:T(8,128)(2,1)S(1)}, bf16[9,32,128]{2,1,0:T(8,128)(2,1)S(1)}, u32[]{:S(2)}, u32[]{:S(2)}) collective-permute-start(bf16[9,32,128]{2,1,0:T(8,128)(2,1)S(1)} %get-tuple-element.31), channel_id=1, source_target_pairs={{8,16},{24,0},{16,8},{0,24},{9,17},{25,1},{17,9},{1,25},{10,18},{2... | collective-permute-start | bytes 221192 | tf_op jit(solution)/shard_map/ppermute | solution.py:543
  16.5 0.7 %collective-permute-start.5 = (bf16[9,32,128]{2,1,0:T(8,128)(2,1)S(1)}, bf16[9,32,128]{2,1,0:T(8,128)(2,1)S(1)}, u32[]{:S(2)}, u32[]{:S(2)}) collective-permute-start(bf16[9,32,128]{2,1,0:T(8,128)(2,1)S(1)} %get-tuple-element.32), channel_id=1, source_target_pairs={{0,8},{16,24},{8,0},{24,16},{1,9},{17,25},{9,1},{25,17},{2,10},{18... | collective-permute-start | bytes 221192 | tf_op jit(solution)/shard_map/ppermute | solution.py:543
  17.2 0.0 copy-done.6
  17.2 0.0 copy-done.7
  17.2 9.6 %inner_rows.1 = (f32[8,16,32,128]{3,2,1,0:T(8,128)S(1)}, f32[2,32,128]{2,1,0:T(8,128)S(1)}) custom-call(s32[1,8]{1,0:T(1,128)S(1)} %copy-done.11, f32[8,16,32,128]{3,2,1,0:T(8,128)S(1)} %get-tuple-element.19.field, f32[8,8,16,128]{3,2,1,0:T(8,128)S(1)} %get-tuple-element.20.coefs, bf16[512,32]{1,0:T(8,128)(2,1)S(1)} %get-tuple-element.21.linear, ...), custom_call_target="tpu_custom_call" | custom-call | flops 20000000000 | bytes 1 | tf_op jit(solution)/shard_map/inner_rows/pallas_call | solution.py:610
  26.8 0.0 collective-permute-done.4.lat_b_in
  26.8 0.0 collective-permute-done.5.lat_a_in
  26.8 11.9 %last_step.1 = f32[32,8,16,128]{3,2,1,0:T(8,128)} custom-call(s32[1,8]{1,0:T(1,128)S(1)} %copy-done.11, f32[8,16,32,128]{3,2,1,0:T(8,128)S(1)} %get-tuple-element.29.field, f32[8,8,16,128]{3,2,1,0:T(8,128)S(1)} %get-tuple-element.20.coefs, bf16[512,32]{1,0:T(8,128)(2,1)S(1)} %get-tuple-element.21.linear, bf16[32,256]{1,0:T(8,128)(2,1)S(1)} %get-tuple-element.22.encode, ...), custom_call_target="tpu_custom_call" | custom-call | flops 20000000000 | bytes 1 | tf_op jit(solution)/shard_map/last_step/pallas_call | solution.py:610
Async XLA Ops:
  0.0 11.0 %copy-start.5 = (f32[7,16,128]{2,1,0:T(8,128)S(1)}, f32[7,16,128]{2,1,0:T(8,128)}, u32[]{:S(2)}) copy-start(f32[7,16,128]{2,1,0:T(8,128)} %mixing.3) | copy-start | bytes 172036
  0.0 11.0 %copy-start.4 = (f32[8,16,128]{2,1,0:T(8,128)S(1)}, f32[8,16,128]{2,1,0:T(8,128)}, u32[]{:S(2)}) copy-start(f32[8,16,128]{2,1,0:T(8,128)} %north_c.3) | copy-start | bytes 196612
  0.0 11.0 %copy-start.3 = (f32[8,16,128]{2,1,0:T(8,128)S(1)}, f32[8,16,128]{2,1,0:T(8,128)}, u32[]{:S(2)}) copy-start(f32[8,16,128]{2,1,0:T(8,128)} %east_c.3) | copy-start | bytes 196612
  0.0 11.0 %copy-start.10 = (f32[256]{0:T(256)S(1)}, f32[256]{0:T(256)}, u32[]{:S(2)}) copy-start(f32[256]{0:T(256)} %param.21) | copy-start | bytes 3076
  0.0 11.0 %copy-start.9 = (bf16[32,224]{1,0:T(8,128)(2,1)S(1)}, bf16[32,224]{1,0:T(8,128)(2,1)}, u32[]{:S(2)}) copy-start(bf16[32,224]{1,0:T(8,128)(2,1)} %refs_4_.1) | copy-start | bytes 43012
  0.0 11.0 %copy-start.2 = (bf16[224,256]{1,0:T(8,128)(2,1)S(1)}, bf16[224,256]{1,0:T(8,128)(2,1)}, u32[]{:S(2)}) copy-start(bf16[224,256]{1,0:T(8,128)(2,1)} %refs_3_.1) | copy-start | bytes 344068
  0.0 11.0 %copy-start.1 = (bf16[256,224]{0,1:T(8,128)(2,1)S(1)}, bf16[256,224]{0,1:T(8,128)(2,1)}, u32[]{:S(2)}) copy-start(bf16[256,224]{0,1:T(8,128)(2,1)} %param.18) | copy-start | bytes 344068
  0.0 11.0 %copy-start = (bf16[256,224]{0,1:T(8,128)(2,1)S(1)}, bf16[256,224]{0,1:T(8,128)(2,1)}, u32[]{:S(2)}) copy-start(bf16[256,224]{0,1:T(8,128)(2,1)} %param.17) | copy-start | bytes 344068
  0.0 11.0 %copy-start.8 = (bf16[224,32]{0,1:T(8,128)(2,1)S(1)}, bf16[224,32]{0,1:T(8,128)(2,1)}, u32[]{:S(2)}) copy-start(bf16[224,32]{0,1:T(8,128)(2,1)} %param.16) | copy-start | bytes 43012
  3.3 9.6 %collective-permute-start = (f32[80,128]{1,0:T(8,128)}, f32[80,128]{1,0:T(8,128)S(1)}, u32[]{:S(2)}, u32[]{:S(2)}) collective-permute-start(f32[80,128]{1,0:T(8,128)} %get-tuple-element.23.lon_b_own), channel_id=1, source_target_pairs={{1,2},{3,4},{5,6},{7,0},{2,1},{4,3},{6,5},{0,7},{9,10},{11,12},{13... | collective-permute-start | bytes 122888 | tf_op jit(solution)/shard_map/ppermute | solution.py:543
  9.4 4.2 %collective-permute-start.1 = (f32[80,128]{1,0:T(8,128)}, f32[80,128]{1,0:T(8,128)S(1)}, u32[]{:S(2)}, u32[]{:S(2)}) collective-permute-start(f32[80,128]{1,0:T(8,128)} %get-tuple-element.24.lon_a_own), channel_id=1, source_target_pairs={{0,1},{2,3},{4,5},{6,7},{1,0},{3,2},{5,4},{7,6},{8,9},{10,11},{12,... | collective-permute-start | bytes 122888 | tf_op jit(solution)/shard_map/ppermute | solution.py:543
  9.4 4.6 %collective-permute-start.2 = (bf16[8,32,128]{2,1,0:T(8,128)(2,1)}, bf16[8,32,128]{2,1,0:T(8,128)(2,1)S(1)}, u32[]{:S(2)}, u32[]{:S(2)}) collective-permute-start(bf16[8,32,128]{2,1,0:T(8,128)(2,1)} %get-tuple-element.25), channel_id=1, source_target_pairs={{8,16},{24,0},{16,8},{0,24},{9,17},{25,1},{17,9},{1,25},{10,18},{2... | collective-permute-start | bytes 196616 | tf_op jit(solution)/shard_map/ppermute | solution.py:543
  10.0 3.9 %collective-permute-start.3 = (bf16[8,32,128]{2,1,0:T(8,128)(2,1)}, bf16[8,32,128]{2,1,0:T(8,128)(2,1)S(1)}, u32[]{:S(2)}, u32[]{:S(2)}) collective-permute-start(bf16[8,32,128]{2,1,0:T(8,128)(2,1)} %get-tuple-element.26), channel_id=1, source_target_pairs={{0,8},{16,24},{8,0},{24,16},{1,9},{17,25},{9,1},{25,17},{2,10},{18... | collective-permute-start | bytes 196616 | tf_op jit(solution)/shard_map/ppermute | solution.py:543
  11.0 2.9 %copy-start.11 = (s32[1,8]{1,0:T(1,128)S(1)}, s32[1,8]{1,0:T(1,128)}, u32[]{:S(2)}) copy-start(s32[1,8]{1,0:T(1,128)} %sun.7) | copy-start | bytes 100
  13.9 3.3 %copy-start.6 = (f32[80,128]{1,0:T(8,128)S(1)}, f32[80,128]{1,0:T(8,128)}, u32[]{:S(2)}) copy-start(f32[80,128]{1,0:T(8,128)} %get-tuple-element.24.lon_a_own) | copy-start | bytes 122884
  13.9 3.3 %copy-start.7 = (f32[80,128]{1,0:T(8,128)S(1)}, f32[80,128]{1,0:T(8,128)}, u32[]{:S(2)}) copy-start(f32[80,128]{1,0:T(8,128)} %get-tuple-element.23.lon_b_own) | copy-start | bytes 122884
  15.8 11.1 %collective-permute-start.4 = (bf16[9,32,128]{2,1,0:T(8,128)(2,1)S(1)}, bf16[9,32,128]{2,1,0:T(8,128)(2,1)S(1)}, u32[]{:S(2)}, u32[]{:S(2)}) collective-permute-start(bf16[9,32,128]{2,1,0:T(8,128)(2,1)S(1)} %get-tuple-element.31), channel_id=1, source_target_pairs={{8,16},{24,0},{16,8},{0,24},{9,17},{25,1},{17,9},{1,25},{10,18},{2... | collective-permute-start | bytes 221192 | tf_op jit(solution)/shard_map/ppermute | solution.py:543
  16.5 10.3 %collective-permute-start.5 = (bf16[9,32,128]{2,1,0:T(8,128)(2,1)S(1)}, bf16[9,32,128]{2,1,0:T(8,128)(2,1)S(1)}, u32[]{:S(2)}, u32[]{:S(2)}) collective-permute-start(bf16[9,32,128]{2,1,0:T(8,128)(2,1)S(1)} %get-tuple-element.32), channel_id=1, source_target_pairs={{0,8},{16,24},{8,0},{24,16},{1,9},{17,25},{9,1},{25,17},{2,10},{18... | collective-permute-start | bytes 221192 | tf_op jit(solution)/shard_map/ppermute | solution.py:543

commit v8 on v7

--- a/solution.py
+++ b/solution.py
@@ -14,6 +14,7 @@
 ROWS_IN_FLIGHT = 2
 LEVELS_AT_ONCE = 4
 LAG = 1
+EARLY_UNITS = (0, 1, 2, 3, 8, 10, 12, 14, 15)
 
 F32 = jnp.float32
 BF16 = jnp.bfloat16
@@ -64,8 +65,14 @@
 EAST_ROW, NORTH_ROW, MIXING_ROW, LIT_ROW = 32, 33, 34, 35
 
 
-def first_kernel(sun, latent, east_c, north_c, mixing, lon_a, lon_b, lat_a, lat_b, *scratch):
+def first_kernel(sun, latent, east_c, north_c, mixing, *refs):
+    outs, scratch, results = refs[:4], refs[4:-5], refs[-5:-1]
+    lon_a, lon_b, lat_a, lat_b = results
     tiles, sun_v, east_v, north_v, mixing_v, faces, turned_faces, sems = scratch
+    sends = [
+        pltpu.make_async_copy(result, out, refs[-1].at[at])
+        for at, (result, out) in enumerate(zip(results, outs))
+    ]
     n_levels, n_species, n_rows, n_cols = tiles.shape
     lanes = lane_ids((1, n_cols))
     is_first, is_last = at_ends()
@@ -106,6 +113,8 @@
             value = rows[pl.ds(r, n_species, stride=n_rows), :]
             ends.append((value * jnp.where(closed, 0.0, speed)).astype(BF16))
         by_parity("lat", ends[1], ends[0], lat_a.at[level], lat_b.at[level])
+    for copy in sends[2:]:
+        copy.start()
     turned_faces[0] = faces[0].T
     turned_faces[1] = faces[1].T
     columns = [
@@ -124,6 +133,10 @@
     west = [jnp.where(kinds == LIT_ROW, lit_west, columns[at]) for at in (2, 3)]
     east = [jnp.where(kinds == LIT_ROW, lit_east, columns[at]) for at in (1, 0)]
     by_parity("lon", jnp.concatenate(east, axis=0), jnp.concatenate(west, axis=0), lon_a, lon_b)
+    for copy in sends[:2]:
+        copy.start()
+    for copy in sends:
+        copy.wait()
 
 
 def split_columns(message):
@@ -263,7 +276,7 @@
 
 
 def step_rows(
-    order, sun, field, coefs, linear, encode, lon_of, south_in, north_in, diffused, finish, early=None, passage=None
+    order, sun, field, coefs, linear, encode, lon_of, south_in, north_in, diffused, finish, early=None, passage=None, tail=None
 ):
     n_levels, n_rows, _, n_cols = field.shape
     lanes = lane_ids((1, n_cols))
@@ -317,7 +330,7 @@
     units, beside = [], []
     for first in range(0, len(order), ROWS_IN_FLIGHT):
         in_flight = order[first : first + ROWS_IN_FLIGHT]
-        places = [(level, r) for r in in_flight for level in range(0, n_levels, LEVELS_AT_ONCE)]
+        places = [(level, r) for level in range(0, n_levels, LEVELS_AT_ONCE) for r in in_flight]
         ahead = order[first + ROWS_IN_FLIGHT : first + 2 * ROWS_IN_FLIGHT]
         steps = itertools.chain(*[transport(r) for r in ahead])
         share = -(-(2 * n_levels - 1) * ROWS_IN_FLIGHT // (SUBSTEPS * len(places)))
@@ -333,11 +346,14 @@
             if substep == 0:
                 rounded[at] = tile_at(level, r).astype(BF16)
             rates[at] = product_of(linear, rounded.pop(at))
-            if early is not None:
+            if early is not None and at in EARLY_UNITS:
                 next(early, None)
             if passage is not None and at > len(units) // 2 + LAG:
                 next(passage, None)
             for _ in itertools.islice(*beside[at]):
+                pass
+        if tail is not None and at >= len(units) - 1:
+            for _ in itertools.islice(tail, LEVELS_AT_ONCE // 2):
                 pass
         if at >= LAG:
             done = at - LAG
@@ -522,12 +538,13 @@
         diffused[level, r] = value
 
     order = list(range(1, half_rows)) + [0] + list(range(half_rows, n_rows))
+    tail = send(1)
     step_rows(
         order, sun, field, coefs, linear, encode,
         lambda r: lon_ends if r in (0, n_rows - 1) else lon_in,
-        south_in, north_in, diffused, finish, early, send(0),
-    )
-    for _ in send(1):
+        south_in, north_in, diffused, finish, early, send(0), tail,
+    )
+    for _ in tail:
         pass
     for copy in copies:
         copy.wait()
@@ -568,7 +585,7 @@
         first_kernel,
         out_shape=(column, column, edge, edge),
         in_specs=[hbm] * 5,
-        out_specs=tuple(vmem(4)),
+        out_specs=(hbm,) * 4,
         scratch_shapes=[
             pltpu.VMEM((n_levels, n_species, n_rows, n_cols), F32),
             pltpu.VMEM(sunlit.shape, sunlit.dtype),
@@ -578,7 +595,9 @@
             pltpu.VMEM((2, n_levels * n_rows, n_cols), F32),
             pltpu.VMEM((2, n_cols, n_levels * n_rows), F32),
             pltpu.SemaphoreType.DMA((n_levels + 4,)),
-        ],
+        ]
+        + [pltpu.VMEM(result.shape, result.dtype) for result in (column, column, edge, edge)]
+        + [pltpu.SemaphoreType.DMA((4,))],
         compiler_params=pltpu.CompilerParams(vmem_limit_bytes=FIRST_VMEM_BYTES),
         name="first_sends",
         cost_estimate=pl.CostEstimate(flops=4_000_000_000, bytes_accessed=2_000_000, transcendentals=0),

time: 39 us -> 38.8 us (level)
  no operation moved by 1% of the time
where the time goes in v8:
time: 38.8 us; the launch traced here: 38.6 us
  Pallas kernels  28 us (72%)
  starting transfers between devices  9.16 us (24%)
  waiting for transfers between devices  1.12 us (3%)
    pallas_call x3, Pallas kernels, call(): pl.pallas_call(kernel, out_shape=out_shape, in_specs=vmem(len(operands)),...  23 us
    ppermute x6, starting transfers between devices, swapped(): return lax.ppermute(array, axis, pairs + [(j, i) for i, j in pairs])  9.16 us
    pallas_call x1, Pallas kernels, on_device(): pl.pallas_call(first_kernel, out_shape=(column, column, edge, edge), in_s...  3.2 us
    pallas_call x1, Pallas kernels, on_device(): pl.pallas_call(prepare_kernel, out_shape=(layered, jax.ShapeDtypeStruct((...  1.75 us
    ppermute x6, waiting for transfers between devices, swapped(): return lax.ppermute(array, axis, pairs + [(j, i) for i, j in pairs])  1.12 us
  transfers between devices with their start and end apart: 6, of which 2 were waited for; matrix products, arithmetic and copies ran while one was open for 0% of the time, Pallas kernels for 29%

profile of v8, /device:TPU:0, one launch (start us, length us, event | category | flops | bytes accessed | tf_op | source)
XLA Modules:
  0.0 38.6 jit_solution(4762993324643856739)
XLA Ops:
  0.0 0.0 copy-start.5
  0.0 0.0 copy-start.4
  0.0 0.0 copy-start.3
  0.0 0.0 copy-start.10
  0.0 0.0 copy-start.9
  0.0 0.0 copy-start.2
  0.0 0.0 copy-start.1
  0.0 0.0 copy-start
  0.0 0.0 copy-start.8
  0.1 3.2 %first_sends.1 = (f32[80,128]{1,0:T(8,128)}, f32[80,128]{1,0:T(8,128)}, bf16[8,32,128]{2,1,0:T(8,128)(2,1)}, bf16[8,32,128]{2,1,0:T(8,128)(2,1)}) custom-call(s32[1,8]{1,0:T(1,128)} %sun.7, f32[32,8,16,128]{3,2,1,0:T(8,128)} %latent.3, f32[8,16,128]{2,1,0:T(8,128)} %east_c.3, f32[8,16,128]{2,1,0:T(8,128)} %north_c.3, f32[7,16,128]{2,1,0:T(8,128)} %mixing.3), custom_call_target="tpu_custom_call" | custom-call | flops 4000000000 | bytes 2000000 | tf_op jit(solution)/shard_map/first_sends/pallas_call | solution.py:584
  3.3 6.1 %collective-permute-start = (f32[80,128]{1,0:T(8,128)}, f32[80,128]{1,0:T(8,128)S(1)}, u32[]{:S(2)}, u32[]{:S(2)}) collective-permute-start(f32[80,128]{1,0:T(8,128)} %get-tuple-element.23.lon_b_own), channel_id=1, source_target_pairs={{1,2},{3,4},{5,6},{7,0},{2,1},{4,3},{6,5},{0,7},{9,10},{11,12},{13... | collective-permute-start | bytes 122888 | tf_op jit(solution)/shard_map/ppermute | solution.py:560
  9.4 0.0 collective-permute-start.1
  9.4 0.7 %collective-permute-start.2 = (bf16[8,32,128]{2,1,0:T(8,128)(2,1)}, bf16[8,32,128]{2,1,0:T(8,128)(2,1)S(1)}, u32[]{:S(2)}, u32[]{:S(2)}) collective-permute-start(bf16[8,32,128]{2,1,0:T(8,128)(2,1)} %get-tuple-element.25), channel_id=1, source_target_pairs={{8,16},{24,0},{16,8},{0,24},{9,17},{25,1},{17,9},{1,25},{10,18},{2... | collective-permute-start | bytes 196616 | tf_op jit(solution)/shard_map/ppermute | solution.py:560
  10.0 1.0 %collective-permute-start.3 = (bf16[8,32,128]{2,1,0:T(8,128)(2,1)}, bf16[8,32,128]{2,1,0:T(8,128)(2,1)S(1)}, u32[]{:S(2)}, u32[]{:S(2)}) collective-permute-start(bf16[8,32,128]{2,1,0:T(8,128)(2,1)} %get-tuple-element.26), channel_id=1, source_target_pairs={{0,8},{16,24},{8,0},{24,16},{1,9},{17,25},{9,1},{25,17},{2,10},{18... | collective-permute-start | bytes 196616 | tf_op jit(solution)/shard_map/ppermute | solution.py:560
  11.0 0.0 copy-done.5
  11.0 0.0 copy-done.4
  11.0 0.0 copy-done.3
  11.0 0.0 copy-done.10
  11.0 0.0 copy-done.9
  11.0 0.0 copy-done.2
  11.0 0.0 copy-done.1
  11.0 0.0 copy-done
  11.0 0.0 copy-done.8
  11.0 0.0 copy-start.11
  11.0 1.7 %prepare.1 = (f32[8,16,32,128]{3,2,1,0:T(8,128)S(1)}, f32[8,8,16,128]{3,2,1,0:T(8,128)S(1)}, bf16[512,32]{1,0:T(8,128)(2,1)S(1)}, bf16[32,256]{1,0:T(8,128)(2,1)S(1)}) custom-call(f32[32,8,16,128]{3,2,1,0:T(8,128)} %latent.3, f32[8,16,128]{2,1,0:T(8,128)S(1)} %copy-done.3, f32[8,16,128]{2,1,0:T(8,128)S(1)} %copy-done.4, f32[7,16,128]{2,1,0:T(8,128)S(1)} %copy-done.5, ...), custom_call_target="tpu_custom_call" | custom-call | flops 4000000000 | bytes 1 | tf_op jit(solution)/shard_map/prepare/pallas_call | solution.py:606
  12.8 0.0 collective-permute-done.lon_b_in
  12.8 0.8 %collective-permute-done.1.lon_a_in = f32[80,128]{1,0:T(8,128)S(1)} collective-permute-done((f32[80,128]{1,0:T(8,128)}, f32[80,128]{1,0:T(8,128)S(1)}, u32[]{:S(2)}, u32[]{:S(2)}) %collective-permute-start.1) | collective-permute-done | bytes 40992 | tf_op jit(solution)/shard_map/ppermute | solution.py:560
  13.6 0.3 collective-permute-done.2.lat_b_in
  13.9 0.0 collective-permute-done.3.lat_a_in
  13.9 0.0 copy-done.11
  13.9 0.0 copy-start.6
  13.9 0.0 copy-start.7
  13.9 1.8 %edge_rows.1 = (f32[8,2,32,128]{3,2,1,0:T(8,128)S(1)}, bf16[9,32,128]{2,1,0:T(8,128)(2,1)S(1)}, bf16[9,32,128]{2,1,0:T(8,128)(2,1)S(1)}, f32[2,32,128]{2,1,0:T(8,128)S(1)}) custom-call(s32[1,8]{1,0:T(1,128)S(1)} %copy-done.11, f32[8,16,32,128]{3,2,1,0:T(8,128)S(1)} %get-tuple-element.19.field, f32[8,8,16,128]{3,2,1,0:T(8,128)S(1)} %get-tuple-element.20.coefs, ...), custom_call_target="tpu_custom_call" | custom-call | flops 20000000000 | bytes 1 | tf_op jit(solution)/shard_map/edge_rows/pallas_call | solution.py:629
  15.8 0.8 %collective-permute-start.4 = (bf16[9,32,128]{2,1,0:T(8,128)(2,1)S(1)}, bf16[9,32,128]{2,1,0:T(8,128)(2,1)S(1)}, u32[]{:S(2)}, u32[]{:S(2)}) collective-permute-start(bf16[9,32,128]{2,1,0:T(8,128)(2,1)S(1)} %get-tuple-element.31), channel_id=1, source_target_pairs={{8,16},{24,0},{16,8},{0,24},{9,17},{25,1},{17,9},{1,25},{10,18},{2... | collective-permute-start | bytes 221192 | tf_op jit(solution)/shard_map/ppermute | solution.py:560
  16.5 0.7 %collective-permute-start.5 = (bf16[9,32,128]{2,1,0:T(8,128)(2,1)S(1)}, bf16[9,32,128]{2,1,0:T(8,128)(2,1)S(1)}, u32[]{:S(2)}, u32[]{:S(2)}) collective-permute-start(bf16[9,32,128]{2,1,0:T(8,128)(2,1)S(1)} %get-tuple-element.32), channel_id=1, source_target_pairs={{0,8},{16,24},{8,0},{24,16},{1,9},{17,25},{9,1},{25,17},{2,10},{18... | collective-permute-start | bytes 221192 | tf_op jit(solution)/shard_map/ppermute | solution.py:560
  17.2 0.0 copy-done.6
  17.2 0.0 copy-done.7
  17.2 9.4 %inner_rows.1 = (f32[8,16,32,128]{3,2,1,0:T(8,128)S(1)}, f32[2,32,128]{2,1,0:T(8,128)S(1)}) custom-call(s32[1,8]{1,0:T(1,128)S(1)} %copy-done.11, f32[8,16,32,128]{3,2,1,0:T(8,128)S(1)} %get-tuple-element.19.field, f32[8,8,16,128]{3,2,1,0:T(8,128)S(1)} %get-tuple-element.20.coefs, bf16[512,32]{1,0:T(8,128)(2,1)S(1)} %get-tuple-element.21.linear, ...), custom_call_target="tpu_custom_call" | custom-call | flops 20000000000 | bytes 1 | tf_op jit(solution)/shard_map/inner_rows/pallas_call | solution.py:629
  26.7 0.0 collective-permute-done.4.lat_b_in
  26.7 0.0 collective-permute-done.5.lat_a_in
  26.7 11.8 %last_step.1 = f32[32,8,16,128]{3,2,1,0:T(8,128)} custom-call(s32[1,8]{1,0:T(1,128)S(1)} %copy-done.11, f32[8,16,32,128]{3,2,1,0:T(8,128)S(1)} %get-tuple-element.29.field, f32[8,8,16,128]{3,2,1,0:T(8,128)S(1)} %get-tuple-element.20.coefs, bf16[512,32]{1,0:T(8,128)(2,1)S(1)} %get-tuple-element.21.linear, bf16[32,256]{1,0:T(8,128)(2,1)S(1)} %get-tuple-element.22.encode, ...), custom_call_target="tpu_custom_call" | custom-call | flops 20000000000 | bytes 1 | tf_op jit(solution)/shard_map/last_step/pallas_call | solution.py:629
Async XLA Ops:
  0.0 11.0 %copy-start.5 = (f32[7,16,128]{2,1,0:T(8,128)S(1)}, f32[7,16,128]{2,1,0:T(8,128)}, u32[]{:S(2)}) copy-start(f32[7,16,128]{2,1,0:T(8,128)} %mixing.3) | copy-start | bytes 172036
  0.0 11.0 %copy-start.4 = (f32[8,16,128]{2,1,0:T(8,128)S(1)}, f32[8,16,128]{2,1,0:T(8,128)}, u32[]{:S(2)}) copy-start(f32[8,16,128]{2,1,0:T(8,128)} %north_c.3) | copy-start | bytes 196612
  0.0 11.0 %copy-start.3 = (f32[8,16,128]{2,1,0:T(8,128)S(1)}, f32[8,16,128]{2,1,0:T(8,128)}, u32[]{:S(2)}) copy-start(f32[8,16,128]{2,1,0:T(8,128)} %east_c.3) | copy-start | bytes 196612
  0.0 11.0 %copy-start.10 = (f32[256]{0:T(256)S(1)}, f32[256]{0:T(256)}, u32[]{:S(2)}) copy-start(f32[256]{0:T(256)} %param.21) | copy-start | bytes 3076
  0.0 11.0 %copy-start.9 = (bf16[32,224]{1,0:T(8,128)(2,1)S(1)}, bf16[32,224]{1,0:T(8,128)(2,1)}, u32[]{:S(2)}) copy-start(bf16[32,224]{1,0:T(8,128)(2,1)} %refs_4_.1) | copy-start | bytes 43012
  0.0 11.0 %copy-start.2 = (bf16[224,256]{1,0:T(8,128)(2,1)S(1)}, bf16[224,256]{1,0:T(8,128)(2,1)}, u32[]{:S(2)}) copy-start(bf16[224,256]{1,0:T(8,128)(2,1)} %refs_3_.1) | copy-start | bytes 344068
  0.0 11.0 %copy-start.1 = (bf16[256,224]{0,1:T(8,128)(2,1)S(1)}, bf16[256,224]{0,1:T(8,128)(2,1)}, u32[]{:S(2)}) copy-start(bf16[256,224]{0,1:T(8,128)(2,1)} %param.18) | copy-start | bytes 344068
  0.0 11.0 %copy-start = (bf16[256,224]{0,1:T(8,128)(2,1)S(1)}, bf16[256,224]{0,1:T(8,128)(2,1)}, u32[]{:S(2)}) copy-start(bf16[256,224]{0,1:T(8,128)(2,1)} %param.17) | copy-start | bytes 344068
  0.0 11.0 %copy-start.8 = (bf16[224,32]{0,1:T(8,128)(2,1)S(1)}, bf16[224,32]{0,1:T(8,128)(2,1)}, u32[]{:S(2)}) copy-start(bf16[224,32]{0,1:T(8,128)(2,1)} %param.16) | copy-start | bytes 43012
  3.3 9.6 %collective-permute-start = (f32[80,128]{1,0:T(8,128)}, f32[80,128]{1,0:T(8,128)S(1)}, u32[]{:S(2)}, u32[]{:S(2)}) collective-permute-start(f32[80,128]{1,0:T(8,128)} %get-tuple-element.23.lon_b_own), channel_id=1, source_target_pairs={{1,2},{3,4},{5,6},{7,0},{2,1},{4,3},{6,5},{0,7},{9,10},{11,12},{13... | collective-permute-start | bytes 122888 | tf_op jit(solution)/shard_map/ppermute | solution.py:560
  9.4 4.2 %collective-permute-start.1 = (f32[80,128]{1,0:T(8,128)}, f32[80,128]{1,0:T(8,128)S(1)}, u32[]{:S(2)}, u32[]{:S(2)}) collective-permute-start(f32[80,128]{1,0:T(8,128)} %get-tuple-element.24.lon_a_own), channel_id=1, source_target_pairs={{0,1},{2,3},{4,5},{6,7},{1,0},{3,2},{5,4},{7,6},{8,9},{10,11},{12,... | collective-permute-start | bytes 122888 | tf_op jit(solution)/shard_map/ppermute | solution.py:560
  9.4 4.6 %collective-permute-start.2 = (bf16[8,32,128]{2,1,0:T(8,128)(2,1)}, bf16[8,32,128]{2,1,0:T(8,128)(2,1)S(1)}, u32[]{:S(2)}, u32[]{:S(2)}) collective-permute-start(bf16[8,32,128]{2,1,0:T(8,128)(2,1)} %get-tuple-element.25), channel_id=1, source_target_pairs={{8,16},{24,0},{16,8},{0,24},{9,17},{25,1},{17,9},{1,25},{10,18},{2... | collective-permute-start | bytes 196616 | tf_op jit(solution)/shard_map/ppermute | solution.py:560
  10.0 3.9 %collective-permute-start.3 = (bf16[8,32,128]{2,1,0:T(8,128)(2,1)}, bf16[8,32,128]{2,1,0:T(8,128)(2,1)S(1)}, u32[]{:S(2)}, u32[]{:S(2)}) collective-permute-start(bf16[8,32,128]{2,1,0:T(8,128)(2,1)} %get-tuple-element.26), channel_id=1, source_target_pairs={{0,8},{16,24},{8,0},{24,16},{1,9},{17,25},{9,1},{25,17},{2,10},{18... | collective-permute-start | bytes 196616 | tf_op jit(solution)/shard_map/ppermute | solution.py:560
  11.0 2.9 %copy-start.11 = (s32[1,8]{1,0:T(1,128)S(1)}, s32[1,8]{1,0:T(1,128)}, u32[]{:S(2)}) copy-start(s32[1,8]{1,0:T(1,128)} %sun.7) | copy-start | bytes 100
  13.9 3.3 %copy-start.6 = (f32[80,128]{1,0:T(8,128)S(1)}, f32[80,128]{1,0:T(8,128)}, u32[]{:S(2)}) copy-start(f32[80,128]{1,0:T(8,128)} %get-tuple-element.24.lon_a_own) | copy-start | bytes 122884
  13.9 3.3 %copy-start.7 = (f32[80,128]{1,0:T(8,128)S(1)}, f32[80,128]{1,0:T(8,128)}, u32[]{:S(2)}) copy-start(f32[80,128]{1,0:T(8,128)} %get-tuple-element.23.lon_b_own) | copy-start | bytes 122884
  15.8 10.9 %collective-permute-start.4 = (bf16[9,32,128]{2,1,0:T(8,128)(2,1)S(1)}, bf16[9,32,128]{2,1,0:T(8,128)(2,1)S(1)}, u32[]{:S(2)}, u32[]{:S(2)}) collective-permute-start(bf16[9,32,128]{2,1,0:T(8,128)(2,1)S(1)} %get-tuple-element.31), channel_id=1, source_target_pairs={{8,16},{24,0},{16,8},{0,24},{9,17},{25,1},{17,9},{1,25},{10,18},{2... | collective-permute-start | bytes 221192 | tf_op jit(solution)/shard_map/ppermute | solution.py:560
  16.5 10.1 %collective-permute-start.5 = (bf16[9,32,128]{2,1,0:T(8,128)(2,1)S(1)}, bf16[9,32,128]{2,1,0:T(8,128)(2,1)S(1)}, u32[]{:S(2)}, u32[]{:S(2)}) collective-permute-start(bf16[9,32,128]{2,1,0:T(8,128)(2,1)S(1)} %get-tuple-element.32), channel_id=1, source_target_pairs={{0,8},{16,24},{8,0},{24,16},{1,9},{17,25},{9,1},{25,17},{2,10},{18... | collective-permute-start | bytes 221192 | tf_op jit(solution)/shard_map/ppermute | solution.py:560

commit v9 on v8

--- a/solution.py
+++ b/solution.py
@@ -14,7 +14,6 @@
 ROWS_IN_FLIGHT = 2
 LEVELS_AT_ONCE = 4
 LAG = 1
-EARLY_UNITS = (0, 1, 2, 3, 8, 10, 12, 14, 15)
 
 F32 = jnp.float32
 BF16 = jnp.bfloat16
@@ -68,7 +67,7 @@
 def first_kernel(sun, latent, east_c, north_c, mixing, *refs):
     outs, scratch, results = refs[:4], refs[4:-5], refs[-5:-1]
     lon_a, lon_b, lat_a, lat_b = results
-    tiles, sun_v, east_v, north_v, mixing_v, faces, turned_faces, sems = scratch
+    tiles, sun_v, east_v, north_v, mixing_v, faces, spread, turned_faces, sems = scratch
     sends = [
         pltpu.make_async_copy(result, out, refs[-1].at[at])
         for at, (result, out) in enumerate(zip(results, outs))
@@ -115,23 +114,30 @@
         by_parity("lat", ends[1], ends[0], lat_a.at[level], lat_b.at[level])
     for copy in sends[2:]:
         copy.start()
-    turned_faces[0] = faces[0].T
-    turned_faces[1] = faces[1].T
-    columns = [
-        jnp.concatenate(
-            [
-                turned_faces[0, pl.ds(slot, n_species, stride=4), :],
-                turned_faces[1, pl.ds(slot, COLUMN_ROWS - n_species, stride=4), :],
-            ],
-            axis=0,
-        )
-        for slot in range(4)
-    ]
+    half_cells = n_levels * n_rows // 2
+    odd = lanes % 2 == 1
     kinds = lax.broadcasted_iota(jnp.int32, (COLUMN_ROWS, n_cols), 0)
     lit_west = sun_v[:, :1].astype(F32)
     lit_east = sun_v[:, n_cols // BLOCK - 1 :].astype(F32)
-    west = [jnp.where(kinds == LIT_ROW, lit_west, columns[at]) for at in (2, 3)]
-    east = [jnp.where(kinds == LIT_ROW, lit_east, columns[at]) for at in (1, 0)]
+    west, east = [], []
+    for half in range(2):
+        for kind in range(2):
+            part = faces[kind, half * half_cells : (half + 1) * half_cells]
+            for lane in range(2):
+                spread[kind, pl.ds(lane, half_cells, stride=2), :] = part
+            turned_faces[kind] = spread[kind].T
+        columns = [
+            jnp.concatenate(
+                [
+                    turned_faces[0, pl.ds(slot, n_species, stride=4), :],
+                    turned_faces[1, pl.ds(slot, COLUMN_ROWS - n_species, stride=4), :],
+                ],
+                axis=0,
+            )
+            for slot in range(4)
+        ]
+        east.append(jnp.where(kinds == LIT_ROW, lit_east, jnp.where(odd, columns[1], columns[0])))
+        west.append(jnp.where(kinds == LIT_ROW, lit_west, jnp.where(odd, columns[3], columns[2])))
     by_parity("lon", jnp.concatenate(east, axis=0), jnp.concatenate(west, axis=0), lon_a, lon_b)
     for copy in sends[:2]:
         copy.start()
@@ -139,8 +145,32 @@
         copy.wait()
 
 
-def split_columns(message):
+def split_halves(message):
     return message[:COLUMN_ROWS], message[COLUMN_ROWS:]
+
+
+def is_odd(n_cols):
+    return lane_ids((1, n_cols)) % 2 == 1
+
+
+def clipped(speed):
+    return jnp.where(is_odd(speed.shape[-1]), jnp.maximum(speed, 0.0), jnp.minimum(speed, 0.0))
+
+
+def halo_columns(lon_b_in, lon_a_in):
+    even = is_even("lon")
+    from_west = split_halves(jnp.where(even, lon_b_in[...], lon_a_in[...]))
+    from_east = split_halves(jnp.where(even, lon_a_in[...], lon_b_in[...]))
+    odd = is_odd(lon_a_in.shape[1])
+    near = [jnp.where(odd, w, e) for w, e in zip(from_west, from_east)]
+    return near, from_west, from_east
+
+
+def beside(odd_lanes, even_lanes):
+    n_cols = odd_lanes.shape[1]
+    return jnp.where(
+        is_odd(n_cols), pltpu.roll(odd_lanes, 1, 1), pltpu.roll(even_lanes, n_cols - 1, 1)
+    )
 
 
 def inflow(column, n_species, clip):
@@ -153,30 +183,27 @@
 
 def moved_column(column, west, east, south, north, n_species, n_rows, ends):
     n_cols = column.shape[1]
-    rows = lane_ids((1, n_cols)) % n_rows
+    rows = lane_ids((1, n_cols)) // 2 % n_rows
     is_first, is_last = ends
     speed = column[EAST_ROW : EAST_ROW + 1]
     lat_speed = column[NORTH_ROW : NORTH_ROW + 1]
     up = jnp.where((rows == n_rows - 1) & is_last, 0.0, jnp.maximum(lat_speed, 0.0))
     down = jnp.where((rows == 0) & is_first, 0.0, jnp.minimum(lat_speed, 0.0))
     value = column[:n_species]
-    from_south = jnp.where(rows == 0, south, pltpu.roll(value * up, 1, 1))
-    from_north = jnp.where(rows == n_rows - 1, north, pltpu.roll(value * down, n_cols - 1, 1))
+    from_south = jnp.where(rows == 0, south, pltpu.roll(value * up, 2, 1))
+    from_north = jnp.where(rows == n_rows - 1, north, pltpu.roll(value * down, n_cols - 2, 1))
     centre = 1.0 - jnp.abs(speed) - up + down
     return value * centre + (west - east) + (from_south - from_north)
 
 
-def by_level(west, east, n_levels, n_rows):
-    n_cols = west.shape[1]
-    of_west = lane_ids((1, n_cols)) < n_rows
-    return [
-        jnp.where(
-            of_west,
-            pltpu.roll(west, (n_cols - level * n_rows) % n_cols, 1),
-            pltpu.roll(east, (n_cols - (level - 1) * n_rows) % n_cols, 1),
-        )
-        for level in range(n_levels)
-    ]
+def by_level(halves, n_levels, n_rows):
+    n_cols = halves[0].shape[1]
+    levels = []
+    for level in range(n_levels):
+        at = level * 2 * n_rows
+        half = halves[at // n_cols]
+        levels.append(half if at % n_cols == 0 else pltpu.roll(half, n_cols - at % n_cols, 1))
+    return levels
 
 
 def joined(levels, n_rows):
@@ -276,7 +303,7 @@
 
 
 def step_rows(
-    order, sun, field, coefs, linear, encode, lon_of, south_in, north_in, diffused, finish, early=None, passage=None, tail=None
+    order, sun, field, coefs, linear, encode, lon_in, south_in, north_in, diffused, finish, passage=None, tail=None
 ):
     n_levels, n_rows, _, n_cols = field.shape
     lanes = lane_ids((1, n_cols))
@@ -288,17 +315,11 @@
         right = None
         for level in range(n_levels):
             value = field[level, r]
-            spot = level * 2 * n_rows % n_cols
-            halo = lon_of(r)[level * 2 * n_rows // n_cols]
-            from_west = jnp.where(
-                lanes == 0,
-                pltpu.roll(halo, (n_cols - spot - r) % n_cols, 1),
-                pltpu.roll(value * coef(EAST, level, r), 1, 1),
-            )
+            spot = level * 2 * n_rows + 2 * r + 1
+            halo = pltpu.roll(lon_in[spot // n_cols], n_cols - spot % n_cols, 1)
+            from_west = jnp.where(lanes == 0, halo, pltpu.roll(value * coef(EAST, level, r), 1, 1))
             from_east = jnp.where(
-                lanes == n_cols - 1,
-                pltpu.roll(halo, n_cols - 1 - spot - n_rows - r, 1),
-                pltpu.roll(value * coef(WEST, level, r), n_cols - 1, 1),
+                lanes == n_cols - 1, halo, pltpu.roll(value * coef(WEST, level, r), n_cols - 1, 1)
             )
             if r == 0:
                 from_south = south_in[level].astype(F32)
@@ -327,7 +348,7 @@
     for r in order[:ROWS_IN_FLIGHT]:
         for _ in transport(r):
             pass
-    units, beside = [], []
+    units, background = [], []
     for first in range(0, len(order), ROWS_IN_FLIGHT):
         in_flight = order[first : first + ROWS_IN_FLIGHT]
         places = [(level, r) for level in range(0, n_levels, LEVELS_AT_ONCE) for r in in_flight]
@@ -336,7 +357,7 @@
         share = -(-(2 * n_levels - 1) * ROWS_IN_FLIGHT // (SUBSTEPS * len(places)))
         for substep in range(SUBSTEPS):
             for place in places:
-                beside.append((steps, share))
+                background.append((steps, share))
                 units.append((substep, place))
     later_by = ROWS_IN_FLIGHT * (n_levels // LEVELS_AT_ONCE)
     rounded, rates = {}, {}
@@ -346,11 +367,9 @@
             if substep == 0:
                 rounded[at] = tile_at(level, r).astype(BF16)
             rates[at] = product_of(linear, rounded.pop(at))
-            if early is not None and at in EARLY_UNITS:
-                next(early, None)
             if passage is not None and at > len(units) // 2 + LAG:
                 next(passage, None)
-            for _ in itertools.islice(*beside[at]):
+            for _ in itertools.islice(*background[at]):
                 pass
         if tail is not None and at >= len(units) - 1:
             for _ in itertools.islice(tail, LEVELS_AT_ONCE // 2):
@@ -371,13 +390,6 @@
                     finish(level + extra, r, part)
 
 
-def near_and_far(lon_b_in, lon_a_in):
-    even = is_even("lon")
-    west = split_columns(jnp.where(even, lon_b_in[...], lon_a_in[...]))
-    east = split_columns(jnp.where(even, lon_a_in[...], lon_b_in[...]))
-    return west, east
-
-
 def edge_rows_kernel(
     sun, field, coefs, linear, encode, lat_b_in, lat_a_in, lon_b_in, lon_a_in,
     done, lat_a, lat_b, lon_in, south_in, north_in, diffused,
@@ -386,36 +398,30 @@
     lanes = lane_ids((1, n_cols))
     is_first, is_last = at_ends()
     by_parity("lat", lat_a_in[...], lat_b_in[...], north_in, south_in)
-    (west_near, _), (east_near, _) = near_and_far(lon_b_in, lon_a_in)
-    halos = by_level(
-        inflow(west_near, n_species, jnp.maximum),
-        inflow(east_near, n_species, jnp.minimum),
-        n_levels,
-        n_rows,
-    )
-    for at, halo in enumerate(joined(halos, n_rows)):
-        lon_in[at] = halo
+    near, _, _ = halo_columns(lon_b_in, lon_a_in)
+    for half, column in enumerate(near):
+        lon_in[half] = column[:n_species] * clipped(column[EAST_ROW : EAST_ROW + 1])
     order = [0, n_rows - 1]
 
     def finish(level, r, value):
         done[level, order.index(r)] = value
 
     step_rows(
-        order, sun, field, coefs, linear, encode, lambda r: lon_in, south_in, north_in, diffused, finish
+        order, sun, field, coefs, linear, encode, lon_in, south_in, north_in, diffused, finish
     )
     for level in range(n_levels):
         south = (done[level, 0] * coefs[SOUTH, level, :1]).astype(BF16)
         north = (done[level, 1] * coefs[NORTH, level, n_rows - 1 :]).astype(BF16)
         by_parity("lat", north, south, lat_a.at[level], lat_b.at[level])
-    rows_of = lanes % n_rows
+    rows_of = lanes // 2 % n_rows
     corners = []
     for closed, clip, turn, row in (
-        (is_first, jnp.minimum, 1, 0),
-        (is_last, jnp.maximum, n_cols - 1, n_rows - 1),
+        (is_first, jnp.minimum, 2, 0),
+        (is_last, jnp.maximum, n_cols - 2, n_rows - 1),
     ):
-        of_west = lat_inflow(west_near, n_species, clip)
-        of_east = pltpu.roll(lat_inflow(east_near, n_species, clip), turn, 1)
-        corners.append(jnp.where(closed, 0.0, jnp.where(rows_of == row, of_west, of_east)))
+        lower, upper = (lat_inflow(column, n_species, clip) for column in near)
+        both = jnp.where(rows_of == row, lower, pltpu.roll(upper, turn, 1))
+        corners.append(jnp.where(closed, 0.0, both))
     south, north = (value.astype(BF16) for value in corners)
     by_parity("lat", north, south, lat_a.at[n_levels], lat_b.at[n_levels])
 
@@ -423,76 +429,50 @@
 def columns_ahead(
     n_levels, n_rows, n_species, linear, encode, received, own, south_in, north_in, lon_out
 ):
-    (west_near, west_far), (east_near, east_far) = near_and_far(*received)
-    (own_east, _), (own_west, _) = sent_columns(*own)
-    n_cols = west_near.shape[1]
-    lanes = lane_ids((1, n_cols))
-    ends = at_ends()
-
-    def levels_of(west, east):
-        return by_level(west, east, n_levels, n_rows)
-
-    def kind_of(kind):
-        return levels_of(west_near[kind : kind + 1], east_near[kind : kind + 1])
-
-    def corner(edge, at, turn):
-        if edge is None:
-            return 0.0
-        shift = turn if at == 0 else (turn + (1 if turn > n_rows else n_cols - 1)) % n_cols
-        return pltpu.roll(edge[n_levels].astype(F32), shift, 1)
-
-    def column_after(at, near, west, east):
-        return moved_column(
-            near,
-            inflow(west, n_species, jnp.maximum),
-            inflow(east, n_species, jnp.minimum),
-            corner(south_in, at, n_cols - (n_rows - 1)),
-            corner(north_in, at, n_rows - 1),
-            n_species,
-            n_rows,
-            ends,
+    near, from_west, from_east = halo_columns(*received)
+    lon_b_own, lon_a_own = own
+    even = is_even("lon")
+    own_east = split_halves(jnp.where(even, lon_a_own[...], lon_b_own[...]))
+    own_west = split_halves(jnp.where(even, lon_b_own[...], lon_a_own[...]))
+    n_cols = near[0].shape[1]
+    odd = is_odd(n_cols)
+    moved = []
+    for half in range(2):
+        far = beside(from_west[half], from_east[half])
+        inner = beside(own_west[half], own_east[half])
+        shift = 2 * (n_rows - 1 - half)
+        moved.append(
+            moved_column(
+                near[half],
+                inflow(jnp.where(odd, far, inner), n_species, jnp.maximum),
+                inflow(jnp.where(odd, inner, far), n_species, jnp.minimum),
+                pltpu.roll(south_in[n_levels].astype(F32), n_cols - shift, 1),
+                pltpu.roll(north_in[n_levels].astype(F32), shift, 1),
+                n_species,
+                n_rows,
+                at_ends(),
+            )
         )
-
-    west = column_after(0, west_near, west_far, own_west)
-    yield
-    east = column_after(1, east_near, own_east, east_far)
-    yield
-    moved = levels_of(west, east)
-    mixing = kind_of(MIXING_ROW)
-    yield
-    pair = jnp.concatenate(joined(diffused_columns(moved, mixing), n_rows), axis=1)
+    mixing = by_level([column[MIXING_ROW : MIXING_ROW + 1] for column in near], n_levels, n_rows)
+    solved = diffused_columns(by_level(moved, n_levels, n_rows), mixing)
+    pair = jnp.concatenate(joined(solved, n_rows), axis=1)
     rounded = pair.astype(BF16)
     current, summed = rounded.astype(F32), None
-    yield
     for substep in range(SUBSTEPS):
         rates = product_of(linear, rounded)
-        yield
         change = jnp.dot(encode[...], rates, preferred_element_type=F32)
         summed = change if summed is None else summed + change
         current = current + change
         rounded = current.astype(BF16)
-        yield
-    pair_lit = jnp.concatenate(joined(kind_of(LIT_ROW), n_rows), axis=1)
-    pair = pair + jnp.where(pair_lit > 0.0, summed, 0.0)
-    for at, speed in enumerate(joined(kind_of(EAST_ROW), n_rows)):
-        clipped = jnp.where(
-            lanes // n_rows % 2 == 0, jnp.maximum(speed, 0.0), jnp.minimum(speed, 0.0)
-        )
-        lon_out[at] = pair[:, at * n_cols : (at + 1) * n_cols] * clipped
-
-
-def sent_columns(lon_b_own, lon_a_own):
-    even = is_even("lon")
-    east = split_columns(jnp.where(even, lon_a_own[...], lon_b_own[...]))
-    west = split_columns(jnp.where(even, lon_b_own[...], lon_a_own[...]))
-    return east, west
-
-
-def inner_rows_kernel(
-    sun, field, coefs, linear, encode, lon_b_in, lon_a_in, lon_b_own, lon_a_own, done, lon_in,
-    out, lon_out, diffused,
-):
-    n_levels, n_rows, n_species, _ = field.shape
+    for half, column in enumerate(near):
+        within = slice(half * n_cols, (half + 1) * n_cols)
+        lit = column[LIT_ROW : LIT_ROW + 1] > 0.0
+        value = pair[:, within] + jnp.where(lit, summed[:, within], 0.0)
+        lon_out[half] = value * clipped(column[EAST_ROW : EAST_ROW + 1])
+
+
+def inner_rows_kernel(sun, field, coefs, linear, encode, done, lon_in, out, diffused):
+    n_levels, n_rows, _, _ = field.shape
     for level in range(n_levels):
         out[level, 0] = done[level, 0]
         out[level, n_rows - 1] = done[level, 1]
@@ -500,26 +480,20 @@
     def finish(level, r, value):
         out[level, r] = value
 
-    early = columns_ahead(
-        n_levels, n_rows, n_species, linear, encode,
-        (lon_b_in, lon_a_in), (lon_b_own, lon_a_own), None, None, lon_out,
-    )
     order = list(range(1, n_rows - 1))
-    step_rows(
-        order, sun, field, coefs, linear, encode, lambda r: lon_in, None, None, diffused, finish, early
-    )
+    step_rows(order, sun, field, coefs, linear, encode, lon_in, None, None, diffused, finish)
 
 
 def last_step_kernel(
-    sun, field, coefs, linear, encode, lon_b_in, lon_a_in, lon_b_own, lon_a_own, lon_in, lat_b_in, lat_a_in,
-    out, staged, sems, south_in, north_in, lon_ends, diffused,
+    sun, field, coefs, linear, encode, lon_b_in, lon_a_in, lon_b_own, lon_a_own, lat_b_in, lat_a_in,
+    out, staged, sems, south_in, north_in, lon_in, diffused,
 ):
     n_levels, n_rows, n_species, _ = field.shape
     half_rows = n_rows // 2
     by_parity("lat", lat_a_in[...], lat_b_in[...], north_in, south_in)
-    early = columns_ahead(
+    columns_ahead(
         n_levels, n_rows, n_species, linear, encode,
-        (lon_b_in, lon_a_in), (lon_b_own, lon_a_own), south_in, north_in, lon_ends,
+        (lon_b_in, lon_a_in), (lon_b_own, lon_a_own), south_in, north_in, lon_in,
     )
     copies = []
 
@@ -537,12 +511,11 @@
     def finish(level, r, value):
         diffused[level, r] = value
 
-    order = list(range(1, half_rows)) + [0] + list(range(half_rows, n_rows))
+    order = list(range(n_rows))
     tail = send(1)
     step_rows(
         order, sun, field, coefs, linear, encode,
-        lambda r: lon_ends if r in (0, n_rows - 1) else lon_in,
-        south_in, north_in, diffused, finish, early, send(0), tail,
+        lon_in, south_in, north_in, diffused, finish, send(0), tail,
     )
     for _ in tail:
         pass
@@ -593,6 +566,7 @@
             pltpu.VMEM(north_courant.shape, F32),
             pltpu.VMEM(mixing.shape, F32),
             pltpu.VMEM((2, n_levels * n_rows, n_cols), F32),
+            pltpu.VMEM((2, n_levels * n_rows, n_cols), F32),
             pltpu.VMEM((2, n_cols, n_levels * n_rows), F32),
             pltpu.SemaphoreType.DMA((n_levels + 4,)),
         ]
@@ -654,18 +628,13 @@
     )
     lat_halos = swapped(lat_b, "lat", 1), swapped(lat_a, "lat", 0)
     columns = *lon_halos, lon_b, lon_a
-    field, lon_in = call(
-        inner_rows_kernel,
-        "inner_rows",
-        (*shared, *columns, done, lon_in),
-        (layered, halo),
-        tuple(vmem(2)),
-        layered,
+    (field,) = call(
+        inner_rows_kernel, "inner_rows", (*shared, done, lon_in), (layered,), tuple(vmem(1)), layered
     )
     (advanced,) = call(
         last_step_kernel,
         "last_step",
-        (sunlit, field, coefs, linear, encode, *columns, lon_in, *lat_halos),
+        (sunlit, field, coefs, linear, encode, *columns, *lat_halos),
         (jax.ShapeDtypeStruct(latent_field.shape, F32),),
         (hbm,),
         pltpu.VMEM((2, n_levels, n_species, n_rows // 2, n_cols), F32),

time: 38.8 us -> 38.7 us (level)
  transfers between devices with their start and end apart: 6 -> 6, of which waited for: 2 -> 2; matrix products, arithmetic and copies ran while one was open for 0% -> 0% of each run, Pallas kernels for 29% -> 28%
where the time goes in v9:
time: 38.7 us; the launch traced here: 38.6 us
  Pallas kernels  27.9 us (72%)
  starting transfers between devices  9.16 us (24%)
  waiting for transfers between devices  1.12 us (3%)
    pallas_call x3, Pallas kernels, call(): pl.pallas_call(kernel, out_shape=out_shape, in_specs=vmem(len(operands)),...  22.9 us
    ppermute x6, starting transfers between devices, swapped(): return lax.ppermute(array, axis, pairs + [(j, i) for i, j in pairs])  9.16 us
    pallas_call x1, Pallas kernels, on_device(): pl.pallas_call(first_kernel, out_shape=(column, column, edge, edge), in_s...  3.24 us
    pallas_call x1, Pallas kernels, on_device(): pl.pallas_call(prepare_kernel, out_shape=(layered, jax.ShapeDtypeStruct((...  1.75 us
    ppermute x6, waiting for transfers between devices, swapped(): return lax.ppermute(array, axis, pairs + [(j, i) for i, j in pairs])  1.12 us
  transfers between devices with their start and end apart: 6, of which 2 were waited for; matrix products, arithmetic and copies ran while one was open for 0% of the time, Pallas kernels for 28%

profile of v9, /device:TPU:0, one launch (start us, length us, event | category | flops | bytes accessed | tf_op | source)
XLA Modules:
  0.0 38.6 jit_solution(3561301981369717765)
XLA Ops:
  0.0 0.0 copy-start.5
  0.0 0.0 copy-start.4
  0.0 0.0 copy-start.3
  0.0 0.0 copy-start.10
  0.0 0.0 copy-start.9
  0.0 0.0 copy-start.2
  0.0 0.0 copy-start.1
  0.0 0.0 copy-start
  0.0 0.0 copy-start.8
  0.1 3.2 %first_sends.1 = (f32[80,128]{1,0:T(8,128)}, f32[80,128]{1,0:T(8,128)}, bf16[8,32,128]{2,1,0:T(8,128)(2,1)}, bf16[8,32,128]{2,1,0:T(8,128)(2,1)}) custom-call(s32[1,8]{1,0:T(1,128)} %sun.7, f32[32,8,16,128]{3,2,1,0:T(8,128)} %latent.3, f32[8,16,128]{2,1,0:T(8,128)} %east_c.3, f32[8,16,128]{2,1,0:T(8,128)} %north_c.3, f32[7,16,128]{2,1,0:T(8,128)} %mixing.3), custom_call_target="tpu_custom_call" | custom-call | flops 4000000000 | bytes 2000000 | tf_op jit(solution)/shard_map/first_sends/pallas_call | solution.py:557
  3.3 6.1 %collective-permute-start.2 = (f32[80,128]{1,0:T(8,128)}, f32[80,128]{1,0:T(8,128)S(1)}, u32[]{:S(2)}, u32[]{:S(2)}) collective-permute-start(f32[80,128]{1,0:T(8,128)} %get-tuple-element.23.lon_b_own), channel_id=1, source_target_pairs={{1,2},{3,4},{5,6},{7,0},{2,1},{4,3},{6,5},{0,7},{9,10},{11,12},{13... | collective-permute-start | bytes 122888 | tf_op jit(solution)/shard_map/ppermute | solution.py:533
  9.4 0.0 collective-permute-start.3
  9.4 0.7 %collective-permute-start = (bf16[8,32,128]{2,1,0:T(8,128)(2,1)}, bf16[8,32,128]{2,1,0:T(8,128)(2,1)S(1)}, u32[]{:S(2)}, u32[]{:S(2)}) collective-permute-start(bf16[8,32,128]{2,1,0:T(8,128)(2,1)} %get-tuple-element.21), channel_id=1, source_target_pairs={{8,16},{24,0},{16,8},{0,24},{9,17},{25,1},{17,9},{1,25},{10,18},{2... | collective-permute-start | bytes 196616 | tf_op jit(solution)/shard_map/ppermute | solution.py:533
  10.1 1.0 %collective-permute-start.1 = (bf16[8,32,128]{2,1,0:T(8,128)(2,1)}, bf16[8,32,128]{2,1,0:T(8,128)(2,1)S(1)}, u32[]{:S(2)}, u32[]{:S(2)}) collective-permute-start(bf16[8,32,128]{2,1,0:T(8,128)(2,1)} %get-tuple-element.22), channel_id=1, source_target_pairs={{0,8},{16,24},{8,0},{24,16},{1,9},{17,25},{9,1},{25,17},{2,10},{18... | collective-permute-start | bytes 196616 | tf_op jit(solution)/shard_map/ppermute | solution.py:533
  11.0 0.0 copy-done.5
  11.0 0.0 copy-done.4
  11.0 0.0 copy-done.3
  11.0 0.0 copy-done.10
  11.0 0.0 copy-done.9
  11.0 0.0 copy-done.2
  11.0 0.0 copy-done.1
  11.1 0.0 copy-done
  11.1 0.0 copy-done.8
  11.1 0.0 copy-start.11
  11.1 1.7 %prepare.1 = (f32[8,16,32,128]{3,2,1,0:T(8,128)S(1)}, f32[8,8,16,128]{3,2,1,0:T(8,128)S(1)}, bf16[512,32]{1,0:T(8,128)(2,1)S(1)}, bf16[32,256]{1,0:T(8,128)(2,1)S(1)}) custom-call(f32[32,8,16,128]{3,2,1,0:T(8,128)} %latent.3, f32[8,16,128]{2,1,0:T(8,128)S(1)} %copy-done.3, f32[8,16,128]{2,1,0:T(8,128)S(1)} %copy-done.4, f32[7,16,128]{2,1,0:T(8,128)S(1)} %copy-done.5, ...), custom_call_target="tpu_custom_call" | custom-call | flops 4000000000 | bytes 1 | tf_op jit(solution)/shard_map/prepare/pallas_call | solution.py:580
  12.8 0.0 collective-permute-done.2.lon_b_in
  12.9 0.8 %collective-permute-done.3.lon_a_in = f32[80,128]{1,0:T(8,128)S(1)} collective-permute-done((f32[80,128]{1,0:T(8,128)}, f32[80,128]{1,0:T(8,128)S(1)}, u32[]{:S(2)}, u32[]{:S(2)}) %collective-permute-start.3) | collective-permute-done | bytes 40992 | tf_op jit(solution)/shard_map/ppermute | solution.py:533
  13.6 0.3 collective-permute-done.lat_b_in
  14.0 0.0 collective-permute-done.1.lat_a_in
  14.0 0.0 copy-done.11
  14.0 1.6 %edge_rows.1 = (f32[8,2,32,128]{3,2,1,0:T(8,128)S(1)}, bf16[9,32,128]{2,1,0:T(8,128)(2,1)S(1)}, bf16[9,32,128]{2,1,0:T(8,128)(2,1)S(1)}, f32[2,32,128]{2,1,0:T(8,128)S(1)}) custom-call(s32[1,8]{1,0:T(1,128)S(1)} %copy-done.11, f32[8,16,32,128]{3,2,1,0:T(8,128)S(1)} %get-tuple-element.17.field, f32[8,8,16,128]{3,2,1,0:T(8,128)S(1)} %get-tuple-element.18.coefs, ...), custom_call_target="tpu_custom_call" | custom-call | flops 20000000000 | bytes 1 | tf_op jit(solution)/shard_map/edge_rows/pallas_call | solution.py:603
  15.6 0.8 %collective-permute-start.4 = (bf16[9,32,128]{2,1,0:T(8,128)(2,1)S(1)}, bf16[9,32,128]{2,1,0:T(8,128)(2,1)S(1)}, u32[]{:S(2)}, u32[]{:S(2)}) collective-permute-start(bf16[9,32,128]{2,1,0:T(8,128)(2,1)S(1)} %get-tuple-element.27), channel_id=1, source_target_pairs={{8,16},{24,0},{16,8},{0,24},{9,17},{25,1},{17,9},{1,25},{10,18},{2... | collective-permute-start | bytes 221192 | tf_op jit(solution)/shard_map/ppermute | solution.py:533
  16.4 0.7 %collective-permute-start.5 = (bf16[9,32,128]{2,1,0:T(8,128)(2,1)S(1)}, bf16[9,32,128]{2,1,0:T(8,128)(2,1)S(1)}, u32[]{:S(2)}, u32[]{:S(2)}) collective-permute-start(bf16[9,32,128]{2,1,0:T(8,128)(2,1)S(1)} %get-tuple-element.28), channel_id=1, source_target_pairs={{0,8},{16,24},{8,0},{24,16},{1,9},{17,25},{9,1},{25,17},{2,10},{18... | collective-permute-start | bytes 221192 | tf_op jit(solution)/shard_map/ppermute | solution.py:533
  17.1 0.0 copy-start.6
  17.1 0.0 copy-start.7
  17.1 9.1 %inner_rows.1.field = f32[8,16,32,128]{3,2,1,0:T(8,128)S(1)} custom-call(s32[1,8]{1,0:T(1,128)S(1)} %copy-done.11, f32[8,16,32,128]{3,2,1,0:T(8,128)S(1)} %get-tuple-element.17.field, f32[8,8,16,128]{3,2,1,0:T(8,128)S(1)} %get-tuple-element.18.coefs, bf16[512,32]{1,0:T(8,128)(2,1)S(1)} %get-tuple-element.19.linear, ...), custom_call_target="tpu_custom_call" | custom-call | flops 20000000000 | bytes 1 | tf_op jit(solution)/shard_map/inner_rows/pallas_call | solution.py:603
  26.2 0.0 collective-permute-done.4.lat_b_in
  26.2 0.0 collective-permute-done.5.lat_a_in
  26.2 0.0 copy-done.6
  26.2 0.0 copy-done.7
  26.2 12.2 %last_step.1 = f32[32,8,16,128]{3,2,1,0:T(8,128)} custom-call(s32[1,8]{1,0:T(1,128)S(1)} %copy-done.11, f32[8,16,32,128]{3,2,1,0:T(8,128)S(1)} %inner_rows.1.field, f32[8,8,16,128]{3,2,1,0:T(8,128)S(1)} %get-tuple-element.18.coefs, bf16[512,32]{1,0:T(8,128)(2,1)S(1)} %get-tuple-element.19.linear, bf16[32,256]{1,0:T(8,128)(2,1)S(1)} %get-tuple-element.20.encode, ...), custom_call_target="tpu_custom_call" | custom-call | flops 20000000000 | bytes 1 | tf_op jit(solution)/shard_map/last_step/pallas_call | solution.py:603
Async XLA Ops:
  0.0 11.0 %copy-start.5 = (f32[7,16,128]{2,1,0:T(8,128)S(1)}, f32[7,16,128]{2,1,0:T(8,128)}, u32[]{:S(2)}) copy-start(f32[7,16,128]{2,1,0:T(8,128)} %mixing.3) | copy-start | bytes 172036
  0.0 11.0 %copy-start.4 = (f32[8,16,128]{2,1,0:T(8,128)S(1)}, f32[8,16,128]{2,1,0:T(8,128)}, u32[]{:S(2)}) copy-start(f32[8,16,128]{2,1,0:T(8,128)} %north_c.3) | copy-start | bytes 196612
  0.0 11.0 %copy-start.3 = (f32[8,16,128]{2,1,0:T(8,128)S(1)}, f32[8,16,128]{2,1,0:T(8,128)}, u32[]{:S(2)}) copy-start(f32[8,16,128]{2,1,0:T(8,128)} %east_c.3) | copy-start | bytes 196612
  0.0 11.0 %copy-start.10 = (f32[256]{0:T(256)S(1)}, f32[256]{0:T(256)}, u32[]{:S(2)}) copy-start(f32[256]{0:T(256)} %param.21) | copy-start | bytes 3076
  0.0 11.0 %copy-start.9 = (bf16[32,224]{1,0:T(8,128)(2,1)S(1)}, bf16[32,224]{1,0:T(8,128)(2,1)}, u32[]{:S(2)}) copy-start(bf16[32,224]{1,0:T(8,128)(2,1)} %refs_4_.1) | copy-start | bytes 43012
  0.0 11.0 %copy-start.2 = (bf16[224,256]{1,0:T(8,128)(2,1)S(1)}, bf16[224,256]{1,0:T(8,128)(2,1)}, u32[]{:S(2)}) copy-start(bf16[224,256]{1,0:T(8,128)(2,1)} %refs_3_.1) | copy-start | bytes 344068
  0.0 11.0 %copy-start.1 = (bf16[256,224]{0,1:T(8,128)(2,1)S(1)}, bf16[256,224]{0,1:T(8,128)(2,1)}, u32[]{:S(2)}) copy-start(bf16[256,224]{0,1:T(8,128)(2,1)} %param.18) | copy-start | bytes 344068
  0.0 11.0 %copy-start = (bf16[256,224]{0,1:T(8,128)(2,1)S(1)}, bf16[256,224]{0,1:T(8,128)(2,1)}, u32[]{:S(2)}) copy-start(bf16[256,224]{0,1:T(8,128)(2,1)} %param.17) | copy-start | bytes 344068
  0.0 11.0 %copy-start.8 = (bf16[224,32]{0,1:T(8,128)(2,1)S(1)}, bf16[224,32]{0,1:T(8,128)(2,1)}, u32[]{:S(2)}) copy-start(bf16[224,32]{0,1:T(8,128)(2,1)} %param.16) | copy-start | bytes 43012
  3.3 9.6 %collective-permute-start.2 = (f32[80,128]{1,0:T(8,128)}, f32[80,128]{1,0:T(8,128)S(1)}, u32[]{:S(2)}, u32[]{:S(2)}) collective-permute-start(f32[80,128]{1,0:T(8,128)} %get-tuple-element.23.lon_b_own), channel_id=1, source_target_pairs={{1,2},{3,4},{5,6},{7,0},{2,1},{4,3},{6,5},{0,7},{9,10},{11,12},{13... | collective-permute-start | bytes 122888 | tf_op jit(solution)/shard_map/ppermute | solution.py:533
  9.4 4.2 %collective-permute-start.3 = (f32[80,128]{1,0:T(8,128)}, f32[80,128]{1,0:T(8,128)S(1)}, u32[]{:S(2)}, u32[]{:S(2)}) collective-permute-start(f32[80,128]{1,0:T(8,128)} %get-tuple-element.24.lon_a_own), channel_id=1, source_target_pairs={{0,1},{2,3},{4,5},{6,7},{1,0},{3,2},{5,4},{7,6},{8,9},{10,11},{12,... | collective-permute-start | bytes 122888 | tf_op jit(solution)/shard_map/ppermute | solution.py:533
  9.4 4.6 %collective-permute-start = (bf16[8,32,128]{2,1,0:T(8,128)(2,1)}, bf16[8,32,128]{2,1,0:T(8,128)(2,1)S(1)}, u32[]{:S(2)}, u32[]{:S(2)}) collective-permute-start(bf16[8,32,128]{2,1,0:T(8,128)(2,1)} %get-tuple-element.21), channel_id=1, source_target_pairs={{8,16},{24,0},{16,8},{0,24},{9,17},{25,1},{17,9},{1,25},{10,18},{2... | collective-permute-start | bytes 196616 | tf_op jit(solution)/shard_map/ppermute | solution.py:533
  10.1 3.9 %collective-permute-start.1 = (bf16[8,32,128]{2,1,0:T(8,128)(2,1)}, bf16[8,32,128]{2,1,0:T(8,128)(2,1)S(1)}, u32[]{:S(2)}, u32[]{:S(2)}) collective-permute-start(bf16[8,32,128]{2,1,0:T(8,128)(2,1)} %get-tuple-element.22), channel_id=1, source_target_pairs={{0,8},{16,24},{8,0},{24,16},{1,9},{17,25},{9,1},{25,17},{2,10},{18... | collective-permute-start | bytes 196616 | tf_op jit(solution)/shard_map/ppermute | solution.py:533
  11.1 2.9 %copy-start.11 = (s32[1,8]{1,0:T(1,128)S(1)}, s32[1,8]{1,0:T(1,128)}, u32[]{:S(2)}) copy-start(s32[1,8]{1,0:T(1,128)} %sun.7) | copy-start | bytes 100
  15.6 10.5 %collective-permute-start.4 = (bf16[9,32,128]{2,1,0:T(8,128)(2,1)S(1)}, bf16[9,32,128]{2,1,0:T(8,128)(2,1)S(1)}, u32[]{:S(2)}, u32[]{:S(2)}) collective-permute-start(bf16[9,32,128]{2,1,0:T(8,128)(2,1)S(1)} %get-tuple-element.27), channel_id=1, source_target_pairs={{8,16},{24,0},{16,8},{0,24},{9,17},{25,1},{17,9},{1,25},{10,18},{2... | collective-permute-start | bytes 221192 | tf_op jit(solution)/shard_map/ppermute | solution.py:533
  16.4 9.8 %collective-permute-start.5 = (bf16[9,32,128]{2,1,0:T(8,128)(2,1)S(1)}, bf16[9,32,128]{2,1,0:T(8,128)(2,1)S(1)}, u32[]{:S(2)}, u32[]{:S(2)}) collective-permute-start(bf16[9,32,128]{2,1,0:T(8,128)(2,1)S(1)} %get-tuple-element.28), channel_id=1, source_target_pairs={{0,8},{16,24},{8,0},{24,16},{1,9},{17,25},{9,1},{25,17},{2,10},{18... | collective-permute-start | bytes 221192 | tf_op jit(solution)/shard_map/ppermute | solution.py:533
  17.1 9.1 %copy-start.6 = (f32[80,128]{1,0:T(8,128)S(1)}, f32[80,128]{1,0:T(8,128)}, u32[]{:S(2)}) copy-start(f32[80,128]{1,0:T(8,128)} %get-tuple-element.24.lon_a_own) | copy-start | bytes 122884
  17.1 9.1 %copy-start.7 = (f32[80,128]{1,0:T(8,128)S(1)}, f32[80,128]{1,0:T(8,128)}, u32[]{:S(2)}) copy-start(f32[80,128]{1,0:T(8,128)} %get-tuple-element.23.lon_b_own) | copy-start | bytes 122884

commit v10 on v9

--- a/solution.py
+++ b/solution.py
@@ -13,7 +13,8 @@
 GROUP = 8
 ROWS_IN_FLIGHT = 2
 LEVELS_AT_ONCE = 4
-LAG = 1
+LAG = 2
+SPECIES_AT_ONCE = 8
 
 F32 = jnp.float32
 BF16 = jnp.bfloat16
@@ -72,7 +73,7 @@
         pltpu.make_async_copy(result, out, refs[-1].at[at])
         for at, (result, out) in enumerate(zip(results, outs))
     ]
-    n_levels, n_species, n_rows, n_cols = tiles.shape
+    n_species, n_levels, n_rows, n_cols = tiles.shape
     lanes = lane_ids((1, n_cols))
     is_first, is_last = at_ends()
     copies = [
@@ -81,35 +82,45 @@
             ((sun, sun_v), (east_c, east_v), (north_c, north_v), (mixing, mixing_v))
         )
     ]
-    levels = [
-        pltpu.make_async_copy(latent.at[:, level], tiles.at[level], sems.at[level])
-        for level in range(n_levels)
+    groups = [
+        pltpu.make_async_copy(
+            latent.at[at : at + SPECIES_AT_ONCE],
+            tiles.at[at : at + SPECIES_AT_ONCE],
+            sems.at[at // SPECIES_AT_ONCE],
+        )
+        for at in range(0, n_species, SPECIES_AT_ONCE)
     ]
-    for copy in copies + levels:
+    for copy in copies + groups:
         copy.start()
     for copy in copies:
         copy.wait()
-    def face_lanes(planes):
-        packed = None
-        for at, plane in enumerate(planes):
-            turned = pltpu.roll(plane, (4 * at + 2) % n_cols, 1)
-            packed = turned if packed is None else jnp.where(lanes // 4 == at, turned, packed)
-        return packed
+    def with_plane(packed, plane, at):
+        turned = pltpu.roll(plane, (4 * at + 2) % n_cols, 1)
+        return turned if packed is None else jnp.where(lanes // 4 == at, turned, packed)
 
     for level in range(n_levels):
-        levels[level].wait()
-        within = slice(level * n_rows, (level + 1) * n_rows)
-        faces[0, within] = face_lanes([tiles[level, at] for at in range(n_species)])
         planes = [east_v[level], north_v[level]]
         if level < n_levels - 1:
             planes.append(mixing_v[level])
         zero = jnp.zeros((n_rows, n_cols), F32)
-        faces[1, within] = face_lanes(planes + [zero] * (COLUMN_ROWS - n_species - len(planes)))
-        rows = tiles.at[level].reshape(n_species * n_rows, n_cols)
+        packed = None
+        for at, plane in enumerate(planes + [zero] * (COLUMN_ROWS - n_species - len(planes))):
+            packed = with_plane(packed, plane, at)
+        faces[1, level * n_rows : (level + 1) * n_rows] = packed
+    packed = [None] * n_levels
+    for group, copy in enumerate(groups):
+        copy.wait()
+        for at in range(group * SPECIES_AT_ONCE, (group + 1) * SPECIES_AT_ONCE):
+            packed = [
+                with_plane(value, tiles[at, level], at) for level, value in enumerate(packed)
+            ]
+    rows = tiles.reshape(n_species * n_levels * n_rows, n_cols)
+    for level in range(n_levels):
+        faces[0, level * n_rows : (level + 1) * n_rows] = packed[level]
         ends = []
         for r, closed, clip in ((0, is_first, jnp.minimum), (n_rows - 1, is_last, jnp.maximum)):
             speed = clip(north_v[level, r : r + 1, :], 0.0)
-            value = rows[pl.ds(r, n_species, stride=n_rows), :]
+            value = rows[pl.ds(level * n_rows + r, n_species, stride=n_levels * n_rows), :]
             ends.append((value * jnp.where(closed, 0.0, speed)).astype(BF16))
         by_parity("lat", ends[1], ends[0], lat_a.at[level], lat_b.at[level])
     for copy in sends[2:]:
@@ -371,7 +382,7 @@
                 next(passage, None)
             for _ in itertools.islice(*background[at]):
                 pass
-        if tail is not None and at >= len(units) - 1:
+        if tail is not None and at >= len(units) + LAG - 2:
             for _ in itertools.islice(tail, LEVELS_AT_ONCE // 2):
                 pass
         if at >= LAG:
@@ -560,7 +571,7 @@
         in_specs=[hbm] * 5,
         out_specs=(hbm,) * 4,
         scratch_shapes=[
-            pltpu.VMEM((n_levels, n_species, n_rows, n_cols), F32),
+            pltpu.VMEM(latent_field.shape, F32),
             pltpu.VMEM(sunlit.shape, sunlit.dtype),
             pltpu.VMEM(east_courant.shape, F32),
             pltpu.VMEM(north_courant.shape, F32),

time: 38.7 us -> 39.2 us (1.013)
  Pallas kernels: 27.9 us -> 28.3 us
    pallas_call x3, Pallas kernels: 22.9 us -> 23.5 us  [call(): pl.pallas_call(kernel, out_shape=out_shape, in_specs=vmem(len(operands)),...]
where the time goes in v10:
time: 39.2 us; the launch traced here: 39 us
  Pallas kernels  28.3 us (72%)
  starting transfers between devices  9.16 us (23%)
  waiting for transfers between devices  1.12 us (3%)
    pallas_call x3, Pallas kernels, call(): pl.pallas_call(kernel, out_shape=out_shape, in_specs=vmem(len(operands)),...  23.5 us
    ppermute x6, starting transfers between devices, swapped(): return lax.ppermute(array, axis, pairs + [(j, i) for i, j in pairs])  9.16 us
    pallas_call x1, Pallas kernels, on_device(): pl.pallas_call(first_kernel, out_shape=(column, column, edge, edge), in_s...  3.12 us
    pallas_call x1, Pallas kernels, on_device(): pl.pallas_call(prepare_kernel, out_shape=(layered, jax.ShapeDtypeStruct((...  1.75 us
    ppermute x6, waiting for transfers between devices, swapped(): return lax.ppermute(array, axis, pairs + [(j, i) for i, j in pairs])  1.12 us
  transfers between devices with their start and end apart: 6, of which 2 were waited for; matrix products, arithmetic and copies ran while one was open for 0% of the time, Pallas kernels for 28%

profile of v10, /device:TPU:0, one launch (start us, length us, event | category | flops | bytes accessed | tf_op | source)
XLA Modules:
  0.0 39.0 jit_solution(17320683562755999529)
XLA Ops:
  0.0 0.0 copy-start.5
  0.0 0.0 copy-start.4
  0.0 0.0 copy-start.3
  0.0 0.0 copy-start.10
  0.0 0.0 copy-start.9
  0.0 0.0 copy-start.2
  0.0 0.0 copy-start.1
  0.0 0.0 copy-start
  0.0 0.0 copy-start.8
  0.1 3.1 %first_sends.1 = (f32[80,128]{1,0:T(8,128)}, f32[80,128]{1,0:T(8,128)}, bf16[8,32,128]{2,1,0:T(8,128)(2,1)}, bf16[8,32,128]{2,1,0:T(8,128)(2,1)}) custom-call(s32[1,8]{1,0:T(1,128)} %sun.7, f32[32,8,16,128]{3,2,1,0:T(8,128)} %latent.3, f32[8,16,128]{2,1,0:T(8,128)} %east_c.3, f32[8,16,128]{2,1,0:T(8,128)} %north_c.3, f32[7,16,128]{2,1,0:T(8,128)} %mixing.3), custom_call_target="tpu_custom_call" | custom-call | flops 4000000000 | bytes 2000000 | tf_op jit(solution)/shard_map/first_sends/pallas_call | solution.py:568
  3.2 6.1 %collective-permute-start.2 = (f32[80,128]{1,0:T(8,128)}, f32[80,128]{1,0:T(8,128)S(1)}, u32[]{:S(2)}, u32[]{:S(2)}) collective-permute-start(f32[80,128]{1,0:T(8,128)} %get-tuple-element.23.lon_b_own), channel_id=1, source_target_pairs={{1,2},{3,4},{5,6},{7,0},{2,1},{4,3},{6,5},{0,7},{9,10},{11,12},{13... | collective-permute-start | bytes 122888 | tf_op jit(solution)/shard_map/ppermute | solution.py:544
  9.3 0.0 collective-permute-start.3
  9.3 0.7 %collective-permute-start = (bf16[8,32,128]{2,1,0:T(8,128)(2,1)}, bf16[8,32,128]{2,1,0:T(8,128)(2,1)S(1)}, u32[]{:S(2)}, u32[]{:S(2)}) collective-permute-start(bf16[8,32,128]{2,1,0:T(8,128)(2,1)} %get-tuple-element.21), channel_id=1, source_target_pairs={{8,16},{24,0},{16,8},{0,24},{9,17},{25,1},{17,9},{1,25},{10,18},{2... | collective-permute-start | bytes 196616 | tf_op jit(solution)/shard_map/ppermute | solution.py:544
  9.9 1.0 %collective-permute-start.1 = (bf16[8,32,128]{2,1,0:T(8,128)(2,1)}, bf16[8,32,128]{2,1,0:T(8,128)(2,1)S(1)}, u32[]{:S(2)}, u32[]{:S(2)}) collective-permute-start(bf16[8,32,128]{2,1,0:T(8,128)(2,1)} %get-tuple-element.22), channel_id=1, source_target_pairs={{0,8},{16,24},{8,0},{24,16},{1,9},{17,25},{9,1},{25,17},{2,10},{18... | collective-permute-start | bytes 196616 | tf_op jit(solution)/shard_map/ppermute | solution.py:544
  10.9 0.0 copy-done.5
  10.9 0.0 copy-done.4
  10.9 0.0 copy-done.3
  10.9 0.0 copy-done.10
  10.9 0.0 copy-done.9
  10.9 0.0 copy-done.2
  10.9 0.0 copy-done.1
  10.9 0.0 copy-done
  10.9 0.0 copy-done.8
  11.0 0.0 copy-start.11
  11.0 1.7 %prepare.1 = (f32[8,16,32,128]{3,2,1,0:T(8,128)S(1)}, f32[8,8,16,128]{3,2,1,0:T(8,128)S(1)}, bf16[512,32]{1,0:T(8,128)(2,1)S(1)}, bf16[32,256]{1,0:T(8,128)(2,1)S(1)}) custom-call(f32[32,8,16,128]{3,2,1,0:T(8,128)} %latent.3, f32[8,16,128]{2,1,0:T(8,128)S(1)} %copy-done.3, f32[8,16,128]{2,1,0:T(8,128)S(1)} %copy-done.4, f32[7,16,128]{2,1,0:T(8,128)S(1)} %copy-done.5, ...), custom_call_target="tpu_custom_call" | custom-call | flops 4000000000 | bytes 1 | tf_op jit(solution)/shard_map/prepare/pallas_call | solution.py:591
  12.7 0.0 collective-permute-done.2.lon_b_in
  12.7 0.8 %collective-permute-done.3.lon_a_in = f32[80,128]{1,0:T(8,128)S(1)} collective-permute-done((f32[80,128]{1,0:T(8,128)}, f32[80,128]{1,0:T(8,128)S(1)}, u32[]{:S(2)}, u32[]{:S(2)}) %collective-permute-start.3) | collective-permute-done | bytes 40992 | tf_op jit(solution)/shard_map/ppermute | solution.py:544
  13.5 0.3 collective-permute-done.lat_b_in
  13.8 0.0 collective-permute-done.1.lat_a_in
  13.9 0.0 copy-done.11
  13.9 1.6 %edge_rows.1 = (f32[8,2,32,128]{3,2,1,0:T(8,128)S(1)}, bf16[9,32,128]{2,1,0:T(8,128)(2,1)S(1)}, bf16[9,32,128]{2,1,0:T(8,128)(2,1)S(1)}, f32[2,32,128]{2,1,0:T(8,128)S(1)}) custom-call(s32[1,8]{1,0:T(1,128)S(1)} %copy-done.11, f32[8,16,32,128]{3,2,1,0:T(8,128)S(1)} %get-tuple-element.17.field, f32[8,8,16,128]{3,2,1,0:T(8,128)S(1)} %get-tuple-element.18.coefs, ...), custom_call_target="tpu_custom_call" | custom-call | flops 20000000000 | bytes 1 | tf_op jit(solution)/shard_map/edge_rows/pallas_call | solution.py:614
  15.5 0.8 %collective-permute-start.4 = (bf16[9,32,128]{2,1,0:T(8,128)(2,1)S(1)}, bf16[9,32,128]{2,1,0:T(8,128)(2,1)S(1)}, u32[]{:S(2)}, u32[]{:S(2)}) collective-permute-start(bf16[9,32,128]{2,1,0:T(8,128)(2,1)S(1)} %get-tuple-element.27), channel_id=1, source_target_pairs={{8,16},{24,0},{16,8},{0,24},{9,17},{25,1},{17,9},{1,25},{10,18},{2... | collective-permute-start | bytes 221192 | tf_op jit(solution)/shard_map/ppermute | solution.py:544
  16.3 0.7 %collective-permute-start.5 = (bf16[9,32,128]{2,1,0:T(8,128)(2,1)S(1)}, bf16[9,32,128]{2,1,0:T(8,128)(2,1)S(1)}, u32[]{:S(2)}, u32[]{:S(2)}) collective-permute-start(bf16[9,32,128]{2,1,0:T(8,128)(2,1)S(1)} %get-tuple-element.28), channel_id=1, source_target_pairs={{0,8},{16,24},{8,0},{24,16},{1,9},{17,25},{9,1},{25,17},{2,10},{18... | collective-permute-start | bytes 221192 | tf_op jit(solution)/shard_map/ppermute | solution.py:544
  17.0 0.0 copy-start.6
  17.0 0.0 copy-start.7
  17.0 9.2 %inner_rows.1.field = f32[8,16,32,128]{3,2,1,0:T(8,128)S(1)} custom-call(s32[1,8]{1,0:T(1,128)S(1)} %copy-done.11, f32[8,16,32,128]{3,2,1,0:T(8,128)S(1)} %get-tuple-element.17.field, f32[8,8,16,128]{3,2,1,0:T(8,128)S(1)} %get-tuple-element.18.coefs, bf16[512,32]{1,0:T(8,128)(2,1)S(1)} %get-tuple-element.19.linear, ...), custom_call_target="tpu_custom_call" | custom-call | flops 20000000000 | bytes 1 | tf_op jit(solution)/shard_map/inner_rows/pallas_call | solution.py:614
  26.2 0.0 collective-permute-done.4.lat_b_in
  26.2 0.0 collective-permute-done.5.lat_a_in
  26.2 0.0 copy-done.6
  26.2 0.0 copy-done.7
  26.2 12.6 %last_step.1 = f32[32,8,16,128]{3,2,1,0:T(8,128)} custom-call(s32[1,8]{1,0:T(1,128)S(1)} %copy-done.11, f32[8,16,32,128]{3,2,1,0:T(8,128)S(1)} %inner_rows.1.field, f32[8,8,16,128]{3,2,1,0:T(8,128)S(1)} %get-tuple-element.18.coefs, bf16[512,32]{1,0:T(8,128)(2,1)S(1)} %get-tuple-element.19.linear, bf16[32,256]{1,0:T(8,128)(2,1)S(1)} %get-tuple-element.20.encode, ...), custom_call_target="tpu_custom_call" | custom-call | flops 20000000000 | bytes 1 | tf_op jit(solution)/shard_map/last_step/pallas_call | solution.py:614
Async XLA Ops:
  0.0 10.9 %copy-start.5 = (f32[7,16,128]{2,1,0:T(8,128)S(1)}, f32[7,16,128]{2,1,0:T(8,128)}, u32[]{:S(2)}) copy-start(f32[7,16,128]{2,1,0:T(8,128)} %mixing.3) | copy-start | bytes 172036
  0.0 10.9 %copy-start.4 = (f32[8,16,128]{2,1,0:T(8,128)S(1)}, f32[8,16,128]{2,1,0:T(8,128)}, u32[]{:S(2)}) copy-start(f32[8,16,128]{2,1,0:T(8,128)} %north_c.3) | copy-start | bytes 196612
  0.0 10.9 %copy-start.3 = (f32[8,16,128]{2,1,0:T(8,128)S(1)}, f32[8,16,128]{2,1,0:T(8,128)}, u32[]{:S(2)}) copy-start(f32[8,16,128]{2,1,0:T(8,128)} %east_c.3) | copy-start | bytes 196612
  0.0 10.9 %copy-start.10 = (f32[256]{0:T(256)S(1)}, f32[256]{0:T(256)}, u32[]{:S(2)}) copy-start(f32[256]{0:T(256)} %param.21) | copy-start | bytes 3076
  0.0 10.9 %copy-start.9 = (bf16[32,224]{1,0:T(8,128)(2,1)S(1)}, bf16[32,224]{1,0:T(8,128)(2,1)}, u32[]{:S(2)}) copy-start(bf16[32,224]{1,0:T(8,128)(2,1)} %refs_4_.1) | copy-start | bytes 43012
  0.0 10.9 %copy-start.2 = (bf16[224,256]{1,0:T(8,128)(2,1)S(1)}, bf16[224,256]{1,0:T(8,128)(2,1)}, u32[]{:S(2)}) copy-start(bf16[224,256]{1,0:T(8,128)(2,1)} %refs_3_.1) | copy-start | bytes 344068
  0.0 10.9 %copy-start.1 = (bf16[256,224]{0,1:T(8,128)(2,1)S(1)}, bf16[256,224]{0,1:T(8,128)(2,1)}, u32[]{:S(2)}) copy-start(bf16[256,224]{0,1:T(8,128)(2,1)} %param.18) | copy-start | bytes 344068
  0.0 10.9 %copy-start = (bf16[256,224]{0,1:T(8,128)(2,1)S(1)}, bf16[256,224]{0,1:T(8,128)(2,1)}, u32[]{:S(2)}) copy-start(bf16[256,224]{0,1:T(8,128)(2,1)} %param.17) | copy-start | bytes 344068
  0.0 10.9 %copy-start.8 = (bf16[224,32]{0,1:T(8,128)(2,1)S(1)}, bf16[224,32]{0,1:T(8,128)(2,1)}, u32[]{:S(2)}) copy-start(bf16[224,32]{0,1:T(8,128)(2,1)} %param.16) | copy-start | bytes 43012
  3.2 9.6 %collective-permute-start.2 = (f32[80,128]{1,0:T(8,128)}, f32[80,128]{1,0:T(8,128)S(1)}, u32[]{:S(2)}, u32[]{:S(2)}) collective-permute-start(f32[80,128]{1,0:T(8,128)} %get-tuple-element.23.lon_b_own), channel_id=1, source_target_pairs={{1,2},{3,4},{5,6},{7,0},{2,1},{4,3},{6,5},{0,7},{9,10},{11,12},{13... | collective-permute-start | bytes 122888 | tf_op jit(solution)/shard_map/ppermute | solution.py:544
  9.3 4.2 %collective-permute-start.3 = (f32[80,128]{1,0:T(8,128)}, f32[80,128]{1,0:T(8,128)S(1)}, u32[]{:S(2)}, u32[]{:S(2)}) collective-permute-start(f32[80,128]{1,0:T(8,128)} %get-tuple-element.24.lon_a_own), channel_id=1, source_target_pairs={{0,1},{2,3},{4,5},{6,7},{1,0},{3,2},{5,4},{7,6},{8,9},{10,11},{12,... | collective-permute-start | bytes 122888 | tf_op jit(solution)/shard_map/ppermute | solution.py:544
  9.3 4.6 %collective-permute-start = (bf16[8,32,128]{2,1,0:T(8,128)(2,1)}, bf16[8,32,128]{2,1,0:T(8,128)(2,1)S(1)}, u32[]{:S(2)}, u32[]{:S(2)}) collective-permute-start(bf16[8,32,128]{2,1,0:T(8,128)(2,1)} %get-tuple-element.21), channel_id=1, source_target_pairs={{8,16},{24,0},{16,8},{0,24},{9,17},{25,1},{17,9},{1,25},{10,18},{2... | collective-permute-start | bytes 196616 | tf_op jit(solution)/shard_map/ppermute | solution.py:544
  9.9 3.9 %collective-permute-start.1 = (bf16[8,32,128]{2,1,0:T(8,128)(2,1)}, bf16[8,32,128]{2,1,0:T(8,128)(2,1)S(1)}, u32[]{:S(2)}, u32[]{:S(2)}) collective-permute-start(bf16[8,32,128]{2,1,0:T(8,128)(2,1)} %get-tuple-element.22), channel_id=1, source_target_pairs={{0,8},{16,24},{8,0},{24,16},{1,9},{17,25},{9,1},{25,17},{2,10},{18... | collective-permute-start | bytes 196616 | tf_op jit(solution)/shard_map/ppermute | solution.py:544
  11.0 2.9 %copy-start.11 = (s32[1,8]{1,0:T(1,128)S(1)}, s32[1,8]{1,0:T(1,128)}, u32[]{:S(2)}) copy-start(s32[1,8]{1,0:T(1,128)} %sun.7) | copy-start | bytes 100
  15.5 10.7 %collective-permute-start.4 = (bf16[9,32,128]{2,1,0:T(8,128)(2,1)S(1)}, bf16[9,32,128]{2,1,0:T(8,128)(2,1)S(1)}, u32[]{:S(2)}, u32[]{:S(2)}) collective-permute-start(bf16[9,32,128]{2,1,0:T(8,128)(2,1)S(1)} %get-tuple-element.27), channel_id=1, source_target_pairs={{8,16},{24,0},{16,8},{0,24},{9,17},{25,1},{17,9},{1,25},{10,18},{2... | collective-permute-start | bytes 221192 | tf_op jit(solution)/shard_map/ppermute | solution.py:544
  16.3 9.9 %collective-permute-start.5 = (bf16[9,32,128]{2,1,0:T(8,128)(2,1)S(1)}, bf16[9,32,128]{2,1,0:T(8,128)(2,1)S(1)}, u32[]{:S(2)}, u32[]{:S(2)}) collective-permute-start(bf16[9,32,128]{2,1,0:T(8,128)(2,1)S(1)} %get-tuple-element.28), channel_id=1, source_target_pairs={{0,8},{16,24},{8,0},{24,16},{1,9},{17,25},{9,1},{25,17},{2,10},{18... | collective-permute-start | bytes 221192 | tf_op jit(solution)/shard_map/ppermute | solution.py:544
  17.0 9.2 %copy-start.6 = (f32[80,128]{1,0:T(8,128)S(1)}, f32[80,128]{1,0:T(8,128)}, u32[]{:S(2)}) copy-start(f32[80,128]{1,0:T(8,128)} %get-tuple-element.24.lon_a_own) | copy-start | bytes 122884
  17.0 9.2 %copy-start.7 = (f32[80,128]{1,0:T(8,128)S(1)}, f32[80,128]{1,0:T(8,128)}, u32[]{:S(2)}) copy-start(f32[80,128]{1,0:T(8,128)} %get-tuple-element.23.lon_b_own) | copy-start | bytes 122884

commit v11 on v9

--- a/solution.py
+++ b/solution.py
@@ -138,7 +138,8 @@
         ]
         east.append(jnp.where(kinds == LIT_ROW, lit_east, jnp.where(odd, columns[1], columns[0])))
         west.append(jnp.where(kinds == LIT_ROW, lit_west, jnp.where(odd, columns[3], columns[2])))
-    by_parity("lon", jnp.concatenate(east, axis=0), jnp.concatenate(west, axis=0), lon_a, lon_b)
+    east, west = (jnp.concatenate(parts, axis=0).astype(BF16) for parts in (east, west))
+    by_parity("lon", east, west, lon_a, lon_b)
     for copy in sends[:2]:
         copy.start()
     for copy in sends:
@@ -146,6 +147,7 @@
 
 
 def split_halves(message):
+    message = message.astype(F32)
     return message[:COLUMN_ROWS], message[COLUMN_ROWS:]
 
 
@@ -548,7 +550,7 @@
 ):
     n_species, n_levels, n_rows, n_cols = latent_field.shape
     layered = jax.ShapeDtypeStruct((n_levels, n_rows, n_species, n_cols), F32)
-    column = jax.ShapeDtypeStruct((2 * COLUMN_ROWS, n_cols), F32)
+    column = jax.ShapeDtypeStruct((2 * COLUMN_ROWS, n_cols), BF16)
     edge = jax.ShapeDtypeStruct((n_levels, n_species, n_cols), BF16)
     cornered = jax.ShapeDtypeStruct((n_levels + 1, n_species, n_cols), BF16)
     params = pltpu.CompilerParams(vmem_limit_bytes=VMEM_BYTES)

time: 38.7 us -> 38.3 us (0.990)
  Pallas kernels: 27.9 us -> 27.5 us
where the time goes in v11:
time: 38.3 us; the launch traced here: 38.2 us
  Pallas kernels  27.5 us (72%)
  starting transfers between devices  9.16 us (24%)
  waiting for transfers between devices  1.12 us (3%)
    pallas_call x3, Pallas kernels, call(): pl.pallas_call(kernel, out_shape=out_shape, in_specs=vmem(len(operands)),...  22.6 us
    ppermute x6, starting transfers between devices, swapped(): return lax.ppermute(array, axis, pairs + [(j, i) for i, j in pairs])  9.16 us
    pallas_call x1, Pallas kernels, on_device(): pl.pallas_call(first_kernel, out_shape=(column, column, edge, edge), in_s...  3.22 us
    pallas_call x1, Pallas kernels, on_device(): pl.pallas_call(prepare_kernel, out_shape=(layered, jax.ShapeDtypeStruct((...  1.75 us
    ppermute x6, waiting for transfers between devices, swapped(): return lax.ppermute(array, axis, pairs + [(j, i) for i, j in pairs])  1.12 us
  transfers between devices with their start and end apart: 6, of which 2 were waited for; matrix products, arithmetic and copies ran while one was open for 0% of the time, Pallas kernels for 28%

profile of v11, /device:TPU:0, one launch (start us, length us, event | category | flops | bytes accessed | tf_op | source)
XLA Modules:
  0.0 38.2 jit_solution(13231317283387910458)
XLA Ops:
  0.0 0.0 copy-start.5
  0.0 0.0 copy-start.4
  0.0 0.0 copy-start.3
  0.0 0.0 copy-start.10
  0.0 0.0 copy-start.9
  0.0 0.0 copy-start.2
  0.0 0.0 copy-start.1
  0.0 0.0 copy-start
  0.0 0.0 copy-start.8
  0.1 3.2 %first_sends.1 = (bf16[80,128]{1,0:T(8,128)(2,1)}, bf16[80,128]{1,0:T(8,128)(2,1)}, bf16[8,32,128]{2,1,0:T(8,128)(2,1)}, bf16[8,32,128]{2,1,0:T(8,128)(2,1)}) custom-call(s32[1,8]{1,0:T(1,128)} %sun.7, f32[32,8,16,128]{3,2,1,0:T(8,128)} %latent.3, f32[8,16,128]{2,1,0:T(8,128)} %east_c.3, f32[8,16,128]{2,1,0:T(8,128)} %north_c.3, f32[7,16,128]{2,1,0:T(8,128)} %mixing.3), custom_call_target="tpu_custom_call" | custom-call | flops 4000000000 | bytes 2000000 | tf_op jit(solution)/shard_map/first_sends/pallas_call | solution.py:559
  3.3 6.1 %collective-permute-start.2 = (bf16[80,128]{1,0:T(8,128)(2,1)}, bf16[80,128]{1,0:T(8,128)(2,1)S(1)}, u32[]{:S(2)}, u32[]{:S(2)}) collective-permute-start(bf16[80,128]{1,0:T(8,128)(2,1)} %get-tuple-element.23.lon_b_own), channel_id=1, source_target_pairs={{1,2},{3,4},{5,6},{7,0},{2,1},{4,3},{6,5},{0,7},{9,10},{11,12},{13... | collective-permute-start | bytes 61448 | tf_op jit(solution)/shard_map/ppermute | solution.py:535
  9.4 0.0 collective-permute-start.3
  9.4 0.7 %collective-permute-start = (bf16[8,32,128]{2,1,0:T(8,128)(2,1)}, bf16[8,32,128]{2,1,0:T(8,128)(2,1)S(1)}, u32[]{:S(2)}, u32[]{:S(2)}) collective-permute-start(bf16[8,32,128]{2,1,0:T(8,128)(2,1)} %get-tuple-element.21), channel_id=1, source_target_pairs={{8,16},{24,0},{16,8},{0,24},{9,17},{25,1},{17,9},{1,25},{10,18},{2... | collective-permute-start | bytes 196616 | tf_op jit(solution)/shard_map/ppermute | solution.py:535
  10.0 1.0 %collective-permute-start.1 = (bf16[8,32,128]{2,1,0:T(8,128)(2,1)}, bf16[8,32,128]{2,1,0:T(8,128)(2,1)S(1)}, u32[]{:S(2)}, u32[]{:S(2)}) collective-permute-start(bf16[8,32,128]{2,1,0:T(8,128)(2,1)} %get-tuple-element.22), channel_id=1, source_target_pairs={{0,8},{16,24},{8,0},{24,16},{1,9},{17,25},{9,1},{25,17},{2,10},{18... | collective-permute-start | bytes 196616 | tf_op jit(solution)/shard_map/ppermute | solution.py:535
  11.0 0.0 copy-done.5
  11.0 0.0 copy-done.4
  11.0 0.0 copy-done.3
  11.0 0.0 copy-done.10
  11.0 0.0 copy-done.9
  11.0 0.0 copy-done.2
  11.0 0.0 copy-done.1
  11.0 0.0 copy-done
  11.1 0.0 copy-done.8
  11.1 0.0 copy-start.11
  11.1 1.7 %prepare.1 = (f32[8,16,32,128]{3,2,1,0:T(8,128)S(1)}, f32[8,8,16,128]{3,2,1,0:T(8,128)S(1)}, bf16[512,32]{1,0:T(8,128)(2,1)S(1)}, bf16[32,256]{1,0:T(8,128)(2,1)S(1)}) custom-call(f32[32,8,16,128]{3,2,1,0:T(8,128)} %latent.3, f32[8,16,128]{2,1,0:T(8,128)S(1)} %copy-done.3, f32[8,16,128]{2,1,0:T(8,128)S(1)} %copy-done.4, f32[7,16,128]{2,1,0:T(8,128)S(1)} %copy-done.5, ...), custom_call_target="tpu_custom_call" | custom-call | flops 4000000000 | bytes 1 | tf_op jit(solution)/shard_map/prepare/pallas_call | solution.py:582
  12.8 0.0 collective-permute-done.2.lon_b_in
  12.8 0.5 %collective-permute-done.3.lon_a_in = bf16[80,128]{1,0:T(8,128)(2,1)S(1)} collective-permute-done((bf16[80,128]{1,0:T(8,128)(2,1)}, bf16[80,128]{1,0:T(8,128)(2,1)S(1)}, u32[]{:S(2)}, u32[]{:S(2)}) %collective-permute-start.3) | collective-permute-done | bytes 20512 | tf_op jit(solution)/shard_map/ppermute | solution.py:535
  13.4 0.6 %collective-permute-done.lat_b_in = bf16[8,32,128]{2,1,0:T(8,128)(2,1)S(1)} collective-permute-done((bf16[8,32,128]{2,1,0:T(8,128)(2,1)}, bf16[8,32,128]{2,1,0:T(8,128)(2,1)S(1)}, u32[]{:S(2)}, u32[]{:S(2)}) %collective-permute-start) | collective-permute-done | bytes 65568 | tf_op jit(solution)/shard_map/ppermute | solution.py:535
  14.0 0.0 collective-permute-done.1.lat_a_in
  14.0 0.0 copy-done.11
  14.0 1.6 %edge_rows.1 = (f32[8,2,32,128]{3,2,1,0:T(8,128)S(1)}, bf16[9,32,128]{2,1,0:T(8,128)(2,1)S(1)}, bf16[9,32,128]{2,1,0:T(8,128)(2,1)S(1)}, f32[2,32,128]{2,1,0:T(8,128)S(1)}) custom-call(s32[1,8]{1,0:T(1,128)S(1)} %copy-done.11, f32[8,16,32,128]{3,2,1,0:T(8,128)S(1)} %get-tuple-element.17.field, f32[8,8,16,128]{3,2,1,0:T(8,128)S(1)} %get-tuple-element.18.coefs, ...), custom_call_target="tpu_custom_call" | custom-call | flops 20000000000 | bytes 1 | tf_op jit(solution)/shard_map/edge_rows/pallas_call | solution.py:605
  15.6 0.8 %collective-permute-start.4 = (bf16[9,32,128]{2,1,0:T(8,128)(2,1)S(1)}, bf16[9,32,128]{2,1,0:T(8,128)(2,1)S(1)}, u32[]{:S(2)}, u32[]{:S(2)}) collective-permute-start(bf16[9,32,128]{2,1,0:T(8,128)(2,1)S(1)} %get-tuple-element.27), channel_id=1, source_target_pairs={{8,16},{24,0},{16,8},{0,24},{9,17},{25,1},{17,9},{1,25},{10,18},{2... | collective-permute-start | bytes 221192 | tf_op jit(solution)/shard_map/ppermute | solution.py:535
  16.4 0.7 %collective-permute-start.5 = (bf16[9,32,128]{2,1,0:T(8,128)(2,1)S(1)}, bf16[9,32,128]{2,1,0:T(8,128)(2,1)S(1)}, u32[]{:S(2)}, u32[]{:S(2)}) collective-permute-start(bf16[9,32,128]{2,1,0:T(8,128)(2,1)S(1)} %get-tuple-element.28), channel_id=1, source_target_pairs={{0,8},{16,24},{8,0},{24,16},{1,9},{17,25},{9,1},{25,17},{2,10},{18... | collective-permute-start | bytes 221192 | tf_op jit(solution)/shard_map/ppermute | solution.py:535
  17.0 0.0 copy-start.6
  17.0 0.0 copy-start.7
  17.0 8.9 %inner_rows.1.field = f32[8,16,32,128]{3,2,1,0:T(8,128)S(1)} custom-call(s32[1,8]{1,0:T(1,128)S(1)} %copy-done.11, f32[8,16,32,128]{3,2,1,0:T(8,128)S(1)} %get-tuple-element.17.field, f32[8,8,16,128]{3,2,1,0:T(8,128)S(1)} %get-tuple-element.18.coefs, bf16[512,32]{1,0:T(8,128)(2,1)S(1)} %get-tuple-element.19.linear, ...), custom_call_target="tpu_custom_call" | custom-call | flops 20000000000 | bytes 1 | tf_op jit(solution)/shard_map/inner_rows/pallas_call | solution.py:605
  25.9 0.0 collective-permute-done.4.lat_b_in
  25.9 0.0 collective-permute-done.5.lat_a_in
  25.9 0.0 copy-done.6
  26.0 0.0 copy-done.7
  26.0 12.1 %last_step.1 = f32[32,8,16,128]{3,2,1,0:T(8,128)} custom-call(s32[1,8]{1,0:T(1,128)S(1)} %copy-done.11, f32[8,16,32,128]{3,2,1,0:T(8,128)S(1)} %inner_rows.1.field, f32[8,8,16,128]{3,2,1,0:T(8,128)S(1)} %get-tuple-element.18.coefs, bf16[512,32]{1,0:T(8,128)(2,1)S(1)} %get-tuple-element.19.linear, bf16[32,256]{1,0:T(8,128)(2,1)S(1)} %get-tuple-element.20.encode, ...), custom_call_target="tpu_custom_call" | custom-call | flops 20000000000 | bytes 1 | tf_op jit(solution)/shard_map/last_step/pallas_call | solution.py:605
Async XLA Ops:
  0.0 11.0 %copy-start.5 = (f32[7,16,128]{2,1,0:T(8,128)S(1)}, f32[7,16,128]{2,1,0:T(8,128)}, u32[]{:S(2)}) copy-start(f32[7,16,128]{2,1,0:T(8,128)} %mixing.3) | copy-start | bytes 172036
  0.0 11.0 %copy-start.4 = (f32[8,16,128]{2,1,0:T(8,128)S(1)}, f32[8,16,128]{2,1,0:T(8,128)}, u32[]{:S(2)}) copy-start(f32[8,16,128]{2,1,0:T(8,128)} %north_c.3) | copy-start | bytes 196612
  0.0 11.0 %copy-start.3 = (f32[8,16,128]{2,1,0:T(8,128)S(1)}, f32[8,16,128]{2,1,0:T(8,128)}, u32[]{:S(2)}) copy-start(f32[8,16,128]{2,1,0:T(8,128)} %east_c.3) | copy-start | bytes 196612
  0.0 11.0 %copy-start.10 = (f32[256]{0:T(256)S(1)}, f32[256]{0:T(256)}, u32[]{:S(2)}) copy-start(f32[256]{0:T(256)} %param.21) | copy-start | bytes 3076
  0.0 11.0 %copy-start.9 = (bf16[32,224]{1,0:T(8,128)(2,1)S(1)}, bf16[32,224]{1,0:T(8,128)(2,1)}, u32[]{:S(2)}) copy-start(bf16[32,224]{1,0:T(8,128)(2,1)} %refs_4_.1) | copy-start | bytes 43012
  0.0 11.0 %copy-start.2 = (bf16[224,256]{1,0:T(8,128)(2,1)S(1)}, bf16[224,256]{1,0:T(8,128)(2,1)}, u32[]{:S(2)}) copy-start(bf16[224,256]{1,0:T(8,128)(2,1)} %refs_3_.1) | copy-start | bytes 344068
  0.0 11.0 %copy-start.1 = (bf16[256,224]{0,1:T(8,128)(2,1)S(1)}, bf16[256,224]{0,1:T(8,128)(2,1)}, u32[]{:S(2)}) copy-start(bf16[256,224]{0,1:T(8,128)(2,1)} %param.18) | copy-start | bytes 344068
  0.0 11.0 %copy-start = (bf16[256,224]{0,1:T(8,128)(2,1)S(1)}, bf16[256,224]{0,1:T(8,128)(2,1)}, u32[]{:S(2)}) copy-start(bf16[256,224]{0,1:T(8,128)(2,1)} %param.17) | copy-start | bytes 344068
  0.0 11.0 %copy-start.8 = (bf16[224,32]{0,1:T(8,128)(2,1)S(1)}, bf16[224,32]{0,1:T(8,128)(2,1)}, u32[]{:S(2)}) copy-start(bf16[224,32]{0,1:T(8,128)(2,1)} %param.16) | copy-start | bytes 43012
  3.3 9.6 %collective-permute-start.2 = (bf16[80,128]{1,0:T(8,128)(2,1)}, bf16[80,128]{1,0:T(8,128)(2,1)S(1)}, u32[]{:S(2)}, u32[]{:S(2)}) collective-permute-start(bf16[80,128]{1,0:T(8,128)(2,1)} %get-tuple-element.23.lon_b_own), channel_id=1, source_target_pairs={{1,2},{3,4},{5,6},{7,0},{2,1},{4,3},{6,5},{0,7},{9,10},{11,12},{13... | collective-permute-start | bytes 61448 | tf_op jit(solution)/shard_map/ppermute | solution.py:535
  9.4 4.0 %collective-permute-start.3 = (bf16[80,128]{1,0:T(8,128)(2,1)}, bf16[80,128]{1,0:T(8,128)(2,1)S(1)}, u32[]{:S(2)}, u32[]{:S(2)}) collective-permute-start(bf16[80,128]{1,0:T(8,128)(2,1)} %get-tuple-element.24.lon_a_own), channel_id=1, source_target_pairs={{0,1},{2,3},{4,5},{6,7},{1,0},{3,2},{5,4},{7,6},{8,9},{10,11},{12,... | collective-permute-start | bytes 61448 | tf_op jit(solution)/shard_map/ppermute | solution.py:535
  9.4 4.6 %collective-permute-start = (bf16[8,32,128]{2,1,0:T(8,128)(2,1)}, bf16[8,32,128]{2,1,0:T(8,128)(2,1)S(1)}, u32[]{:S(2)}, u32[]{:S(2)}) collective-permute-start(bf16[8,32,128]{2,1,0:T(8,128)(2,1)} %get-tuple-element.21), channel_id=1, source_target_pairs={{8,16},{24,0},{16,8},{0,24},{9,17},{25,1},{17,9},{1,25},{10,18},{2... | collective-permute-start | bytes 196616 | tf_op jit(solution)/shard_map/ppermute | solution.py:535
  10.0 3.9 %collective-permute-start.1 = (bf16[8,32,128]{2,1,0:T(8,128)(2,1)}, bf16[8,32,128]{2,1,0:T(8,128)(2,1)S(1)}, u32[]{:S(2)}, u32[]{:S(2)}) collective-permute-start(bf16[8,32,128]{2,1,0:T(8,128)(2,1)} %get-tuple-element.22), channel_id=1, source_target_pairs={{0,8},{16,24},{8,0},{24,16},{1,9},{17,25},{9,1},{25,17},{2,10},{18... | collective-permute-start | bytes 196616 | tf_op jit(solution)/shard_map/ppermute | solution.py:535
  11.1 2.9 %copy-start.11 = (s32[1,8]{1,0:T(1,128)S(1)}, s32[1,8]{1,0:T(1,128)}, u32[]{:S(2)}) copy-start(s32[1,8]{1,0:T(1,128)} %sun.7) | copy-start | bytes 100
  15.6 10.3 %collective-permute-start.4 = (bf16[9,32,128]{2,1,0:T(8,128)(2,1)S(1)}, bf16[9,32,128]{2,1,0:T(8,128)(2,1)S(1)}, u32[]{:S(2)}, u32[]{:S(2)}) collective-permute-start(bf16[9,32,128]{2,1,0:T(8,128)(2,1)S(1)} %get-tuple-element.27), channel_id=1, source_target_pairs={{8,16},{24,0},{16,8},{0,24},{9,17},{25,1},{17,9},{1,25},{10,18},{2... | collective-permute-start | bytes 221192 | tf_op jit(solution)/shard_map/ppermute | solution.py:535
  16.4 9.6 %collective-permute-start.5 = (bf16[9,32,128]{2,1,0:T(8,128)(2,1)S(1)}, bf16[9,32,128]{2,1,0:T(8,128)(2,1)S(1)}, u32[]{:S(2)}, u32[]{:S(2)}) collective-permute-start(bf16[9,32,128]{2,1,0:T(8,128)(2,1)S(1)} %get-tuple-element.28), channel_id=1, source_target_pairs={{0,8},{16,24},{8,0},{24,16},{1,9},{17,25},{9,1},{25,17},{2,10},{18... | collective-permute-start | bytes 221192 | tf_op jit(solution)/shard_map/ppermute | solution.py:535
  17.0 8.9 %copy-start.6 = (bf16[80,128]{1,0:T(8,128)(2,1)S(1)}, bf16[80,128]{1,0:T(8,128)(2,1)}, u32[]{:S(2)}) copy-start(bf16[80,128]{1,0:T(8,128)(2,1)} %get-tuple-element.24.lon_a_own) | copy-start | bytes 61444
  17.0 8.9 %copy-start.7 = (bf16[80,128]{1,0:T(8,128)(2,1)S(1)}, bf16[80,128]{1,0:T(8,128)(2,1)}, u32[]{:S(2)}) copy-start(bf16[80,128]{1,0:T(8,128)(2,1)} %get-tuple-element.23.lon_b_own) | copy-start | bytes 61444
